TPU v7x, 256 devices: a whole 4x4x8 slice. The times are simulated.
256 devices in a mesh: leaf: 256 (over x, y, z, core).
Axes of the slice: x: 4, y: 4, z: 8, core: 2. Of those that a mesh axis runs over, the one named last changes fastest.
Arguments:
- right_sides: bfloat16 [16, 524288], P(None, 'leaf'), may hold values from -6 to 6
- point_order: int32 [256, 2048], P('leaf'), may hold values from 0 to 2047, each once within a row
- leaf_inverse: bfloat16 [524288, 2048], P('leaf')
- test_bases: bfloat16 [8, 64, 524288], P(None, None, 'leaf')
- trial_bases: bfloat16 [8, 64, 524288], P(None, None, 'leaf'), may hold values from -0.75 to 0.75
- coupling_cores: bfloat16 [8, 16384, 128], P(None, 'leaf'), as said below
Outputs:
- solution: float32 [16, 524288], P(None, 'leaf')
Inputs may be any that keep to these rules, and one draw needn't show every extreme that they name: `point_order`: each row is a permutation of 0 to 2047. `coupling_cores`: at each level k, the blocks held by the leaves of one half of a node (equal d >> k) are equal.
All inputs are finite; a program needn't handle non-finite values.
Results may differ from a plain program's by a relative error of at most 0.01.
Values sent between devices are 32-bit elements; how exact they have to be, the bound alone decides.
No kernel may reach another device: no remote copies, remote signals or barrier semaphores. Data moves between devices by JAX's collectives and lax.ppermute only.
A program may use at most 64 MiB of HBM per device.

v0:
```python
import jax
import jax.numpy as jnp
from jax import lax
from jax.sharding import PartitionSpec as P


def half_sums(projection, level, position, devices):
    gathered = lax.all_gather(projection[None], "leaf", axis=0, tiled=True)
    totals = gathered.reshape((devices >> level, 2**level) + projection.shape).sum(axis=1)
    own_sum = lax.dynamic_index_in_dim(totals, position >> level, 0, keepdims=False)
    far_sum = lax.dynamic_index_in_dim(totals, position >> level ^ 1, 0, keepdims=False)
    return (own_sum, far_sum)


def local(right_sides, point_order, leaf_inverse, test_bases, trial_bases, coupling_cores):
    highest = lax.Precision.HIGHEST
    devices = lax.axis_size("leaf")
    position = lax.axis_index("leaf")
    levels = test_bases.shape[0]
    positions = point_order[0]
    ordered = jnp.take(right_sides, positions, axis=1)
    current = jnp.dot(ordered, leaf_inverse, preferred_element_type=jnp.float32)
    for level in range(levels):
        rounded = current.astype(jnp.bfloat16)
        projection = lax.dot_general(
            rounded, test_bases[level], (((1,), (1,)), ((), ())), preferred_element_type=jnp.float32
        )
        own_sum, far_sum = half_sums(projection, level, position, devices)
        upper = position >> level & 1
        stacked = jnp.where(
            upper == 0,
            jnp.concatenate([own_sum, far_sum], axis=1),
            jnp.concatenate([far_sum, own_sum], axis=1),
        )
        cores = coupling_cores[level].astype(jnp.float32)
        weights = lax.dot_general(
            stacked,
            cores,
            (((1,), (1,)), ((), ())),
            precision=highest,
            preferred_element_type=jnp.float32,
        )
        correction = jnp.dot(
            weights.astype(jnp.bfloat16), trial_bases[level], preferred_element_type=jnp.float32
        )
        current = current - correction
    return jnp.zeros_like(current).at[:, positions].set(current)


def solution(mesh):
    in_specs = (
        P(None, "leaf"),
        P("leaf", None),
        P("leaf", None),
        P(None, None, "leaf"),
        P(None, None, "leaf"),
        P(None, "leaf", None),
    )
    out_specs = P(None, "leaf")
    return jax.shard_map(local, mesh=mesh, in_specs=in_specs, out_specs=out_specs, check_vma=False)
```

profile of v0, /device:TPU:32, one launch (start us, length us, event | category | flops | bytes accessed | tf_op | source)
XLA Modules:
  0.0 894.0 jit_solution(16095753398885705968)
XLA Ops:
  7.3 1.1 copy.10
  9.1 6.2 gather_fusion
  15.3 4.4 fusion.1
  19.7 0.8 fusion.28
  20.5 106.5 %all-gather.17.cloned.1.call-done = f32[4096,64]{1,0:T(8,128)} async-done(((f32[16,64]{1,0:T(8,128)}), f32[4096,64]{1,0:T(8,128)}) %all-gather.17.cloned.1.call-update) | async-done | bytes 1048592 | tf_op jit(solution)/shard_map/all_gather | solution.py:8
  127.9 1.1 convolution_subtract_fusion.7
  129.1 0.8 fusion.25
  129.9 103.9 %all-gather.19.cloned.1.call-done = f32[4096,64]{1,0:T(8,128)} async-done(((f32[16,64]{1,0:T(8,128)}), f32[4096,64]{1,0:T(8,128)}) %all-gather.19.cloned.1.call-update) | async-done | bytes 1048592 | tf_op jit(solution)/shard_map/all_gather | solution.py:8
  233.8 2.0 reduce_sum.67
  236.0 1.1 convolution_subtract_fusion.6
  237.1 0.8 fusion.22
  238.0 103.1 %all-gather.21.cloned.1.call-done = f32[4096,64]{1,0:T(8,128)} async-done(((f32[16,64]{1,0:T(8,128)}), f32[4096,64]{1,0:T(8,128)}) %all-gather.21.cloned.1.call-update) | async-done | bytes 1048592 | tf_op jit(solution)/shard_map/all_gather | solution.py:8
  341.1 1.9 reduce_sum.68
  343.2 1.1 convolution_subtract_fusion.5
  345.3 103.1 %all-gather.23.cloned.1.call-done = f32[4096,64]{1,0:T(8,128)} async-done(((f32[16,64]{1,0:T(8,128)}), f32[4096,64]{1,0:T(8,128)}) %all-gather.23.cloned.1.call-update) | async-done | bytes 1048592 | tf_op jit(solution)/shard_map/all_gather | solution.py:8
  448.4 1.8 reduce_sum.69
  450.4 1.1 convolution_subtract_fusion.4
  451.6 0.8 fusion.16
  452.4 103.1 %all-gather.25.cloned.1.call-done = f32[4096,64]{1,0:T(8,128)} async-done(((f32[16,64]{1,0:T(8,128)}), f32[4096,64]{1,0:T(8,128)}) %all-gather.25.cloned.1.call-update) | async-done | bytes 1048592 | tf_op jit(solution)/shard_map/all_gather | solution.py:8
  555.6 1.7 reduce_sum.70
  557.5 1.1 convolution_subtract_fusion.3
  559.5 103.1 %all-gather.27.cloned.1.call-done = f32[4096,64]{1,0:T(8,128)} async-done(((f32[16,64]{1,0:T(8,128)}), f32[4096,64]{1,0:T(8,128)}) %all-gather.27.cloned.1.call-update) | async-done | bytes 1048592 | tf_op jit(solution)/shard_map/all_gather | solution.py:8
  662.7 1.7 reduce_sum.71
  664.6 1.1 convolution_subtract_fusion.2
  666.6 103.1 %all-gather.29.cloned.1.call-done = f32[4096,64]{1,0:T(8,128)} async-done(((f32[16,64]{1,0:T(8,128)}), f32[4096,64]{1,0:T(8,128)}) %all-gather.29.cloned.1.call-update) | async-done | bytes 1048592 | tf_op jit(solution)/shard_map/all_gather | solution.py:8
  769.8 1.7 reduce_sum.72
  771.7 1.1 convolution_subtract_fusion.1
  773.7 103.2 %all-gather.31.cloned.1.call-done = f32[4096,64]{1,0:T(8,128)} async-done(((f32[16,64]{1,0:T(8,128)}), f32[4096,64]{1,0:T(8,128)}) %all-gather.31.cloned.1.call-update) | async-done | bytes 1048592 | tf_op jit(solution)/shard_map/all_gather | solution.py:8
  876.8 1.8 reduce_sum.73
  878.8 1.1 fusion
  880.3 5.8 scatter_custom_fusion
  886.2 1.0 copy.12
  (44 shorter events, 7.6 us)
Async XLA Ops:
  6.5 120.5 %all-gather.17.cloned.1.call-start = ((), (), s32[]{:S(2)}) async-start(), calls=%async_computation | async-start | bytes 2105344 | tf_op jit(solution)/shard_map/all_gather | solution.py:8
  15.3 4.4 copy-start
  15.3 112.5 %copy-start.1 = (bf16[8,64,128]{2,1,0:T(8,128)(2,1)S(1)}, bf16[8,64,128]{2,1,0:T(8,128)(2,1)}, u32[]{:S(2)}) copy-start(bf16[8,64,128]{2,1,0:T(8,128)(2,1)} %param.11) | copy-start | bytes 393220
  20.5 213.3 %all-gather.19.cloned.1.call-start = ((), (), s32[]{:S(2)}) async-start(), calls=%async_computation.1 | async-start | bytes 2105344 | tf_op jit(solution)/shard_map/all_gather | solution.py:8
  129.9 211.3 %all-gather.21.cloned.1.call-start = ((), (), s32[]{:S(2)}) async-start(), calls=%async_computation.2 | async-start | bytes 2105344 | tf_op jit(solution)/shard_map/all_gather | solution.py:8
  238.0 210.4 %all-gather.23.cloned.1.call-start = ((), (), s32[]{:S(2)}) async-start(), calls=%async_computation.3 | async-start | bytes 2105344 | tf_op jit(solution)/shard_map/all_gather | solution.py:8
  345.2 210.4 %all-gather.25.cloned.1.call-start = ((), (), s32[]{:S(2)}) async-start(), calls=%async_computation.4 | async-start | bytes 2105344 | tf_op jit(solution)/shard_map/all_gather | solution.py:8
  452.4 210.3 %all-gather.27.cloned.1.call-start = ((), (), s32[]{:S(2)}) async-start(), calls=%async_computation.5 | async-start | bytes 2105344 | tf_op jit(solution)/shard_map/all_gather | solution.py:8
  559.5 210.3 %all-gather.29.cloned.1.call-start = ((), (), s32[]{:S(2)}) async-start(), calls=%async_computation.6 | async-start | bytes 2105344 | tf_op jit(solution)/shard_map/all_gather | solution.py:8
  666.6 210.3 %all-gather.31.cloned.1.call-start = ((), (), s32[]{:S(2)}) async-start(), calls=%async_computation.7 | async-start | bytes 2105344 | tf_op jit(solution)/shard_map/all_gather | solution.py:8
Sparse Core Ops, SparseCore 0:
  20.6 106.3 all-gather.16
  130.7 103.0 all-gather.18
  238.1 103.0 all-gather.20
  345.3 103.0 all-gather.22
  452.5 103.0 all-gather.24
  559.6 103.0 all-gather.26
  666.7 103.0 all-gather.28
  773.8 103.0 all-gather.30
where the time goes:
time: 897 us; the launch traced here: 894 us
  waiting for transfers between devices  829 us (92%)
  matrix products  21.2 us (2%)
  local copies, waits for them, and re-layouts  15.2 us (2%)
  other arithmetic  14.1 us (2%)
  between operations  13.8 us (2%)
    all_gather x8, waiting for transfers between devices, half_sums(): gathered = lax.all_gather(projection[None], 'leaf', axis=0, tiled=True)  829 us
  transfers between devices with their start and end apart: 8, of which 8 were waited for; matrix products, arithmetic and copies ran while one was open for 0% of the time, Pallas kernels for 0%

commit v1 on v0

v1 whole, which is shorter than its diff:
```python
import functools

import jax
import jax.numpy as jnp
from jax import lax
from jax.experimental import pallas as pl
from jax.experimental.pallas import tpu as pltpu
from jax.sharding import PartitionSpec as P


F32 = jnp.float32
BF16 = jnp.bfloat16
STAGES = 4
RHS = 16
RANK = 64
LANES = 128
BLOCK = 256
NT = (((1,), (1,)), ((), ()))


def mm(a, b):
    return lax.dot_general(
        a, b, (((1,), (0,)), ((), ())), precision=lax.Precision.HIGHEST, preferred_element_type=F32
    )


def mm_nt(a, b):
    return lax.dot_general(a, b, NT, precision=lax.Precision.HIGHEST, preferred_element_type=F32)


def round16(x):
    return x.astype(BF16).astype(F32)


def groups(bits, devices):
    size = 2 ** len(bits)
    out = []
    for base in range(devices):
        if any(base >> b & 1 for b in bits):
            continue
        out.append([base + sum((j >> t & 1) << b for t, b in enumerate(bits)) for j in range(size)])
    return out


def one_hot_low(positions, leaf):
    rows = lax.broadcasted_iota(jnp.int32, (LANES, leaf), 0)
    return jnp.where(rows == (positions & (LANES - 1)), 1.0, 0.0).astype(BF16)


def front_kernel(rs_ref, pos_ref, inv_ref, u_ref, v_ref, core_ref, cur_ref, pay_ref, rest_ref, ordered, proj, gram):
    step = pl.program_id(0)
    leaf = rs_ref.shape[1]
    tiles = leaf // LANES

    @pl.when(step == 0)
    def _():
        positions = pos_ref[...]
        hot = one_hot_low(positions, leaf)
        high = positions // LANES
        rows = jnp.concatenate([rs_ref[:, h * LANES : (h + 1) * LANES] for h in range(tiles)], axis=0)
        picked = jnp.dot(rows, hot, preferred_element_type=F32)
        total = jnp.zeros((RHS, leaf), F32)
        for h in range(tiles):
            total = total + jnp.where(high == h, picked[h * RHS : (h + 1) * RHS], 0.0)
        ordered[...] = total.astype(BF16)
        proj[...] = jnp.zeros_like(proj)
        gram[...] = jnp.zeros_like(gram)

    current = jnp.dot(ordered[...], inv_ref[...], preferred_element_type=F32)
    cur_ref[...] = current
    proj[...] += lax.dot_general(current.astype(BF16), u_ref[...], NT, preferred_element_type=F32)
    for a in range(STAGES):
        lo = a * LANES
        gram[lo : lo + LANES, lo:] += lax.dot_general(
            v_ref[lo : lo + LANES, :], u_ref[lo:, :], NT, preferred_element_type=F32
        )

    @pl.when(step == pl.num_programs(0) - 1)
    def _():
        lane = lax.broadcasted_iota(jnp.int32, (RANK, LANES), 1)

        def diagonal(a):
            lo = a * LANES
            return jnp.where(lane < RANK, 0.0, gram[lo : lo + RANK, lo : lo + LANES])

        pay_ref[:RHS] = proj[:, :LANES]
        pay_ref[RHS : RHS + RANK] = core_ref[0].astype(F32)
        pay_ref[RHS + RANK :] = diagonal(0)
        at = 0
        for b in range(1, STAGES):
            rest_ref[at : at + RHS] = proj[:, b * LANES : (b + 1) * LANES]
            at += RHS
        for b in range(1, STAGES):
            rest_ref[at : at + RANK] = diagonal(b)
            at += RANK
        for b in range(STAGES):
            for c in range(b + 1, STAGES):
                rest_ref[at : at + LANES] = gram[b * LANES : (b + 1) * LANES, c * LANES : (c + 1) * LANES]
                at += LANES


def tiles_after(a):
    later = STAGES - 1 - a
    return RHS * later, RANK * later, LANES * (later * (later - 1) // 2)


def solve_kernel(a, copies, got_ref, rest_ref, core_ref, w_ref, *out):
    lane = lax.broadcasted_iota(jnp.int32, (RHS, LANES), 1)
    own = lax.axis_index("leaf") >> (2 * a) & 3
    pair = [got_ref[n, :RHS] for n in range(4)]
    weights = []
    for n in range(4):
        m = n & 2
        stacked = jnp.where(lane < RANK, pair[m], pltpu.roll(pair[m + 1], RANK, 1))
        weights.append(round16(mm_nt(stacked, got_ref[n, RHS : RHS + RANK])))
    after = [pair[n] - mm(weights[n], got_ref[n, RHS + RANK :]) for n in range(4)]
    stacked = jnp.where(lane < RANK, pltpu.roll(after[0] + after[1], RANK, 1), after[2] + after[3])
    second = round16(mm_nt(stacked, core_ref[0].astype(F32)))
    first = jnp.zeros_like(second)
    for n in range(4):
        first = jnp.where(own == n, weights[n], first)
    w_ref[:, :RANK] = first
    w_ref[:, RANK:] = second
    later = STAGES - 1 - a
    if later:
        (out_ref,) = out
        n_proj, n_own, n_cross = tiles_after(a)
        cross = n_proj + n_own
        for i in range(later):
            tile = cross + i * LANES
            value = rest_ref[i * RHS : (i + 1) * RHS]
            value = value - mm(first, rest_ref[tile : tile + RANK]) - mm(second, rest_ref[tile + RANK : tile + LANES])
            for n in range(copies):
                out_ref[n, i * RHS : (i + 1) * RHS] = value
        for n in range(copies):
            out_ref[n, n_proj:cross] = rest_ref[n_proj:cross]
            if n_cross:
                out_ref[n, cross:] = rest_ref[cross + later * LANES :]


def sum_kernel(a, copies, got_ref, core_ref, pay_ref, *out):
    n_proj, n_own, n_cross = tiles_after(a - 1)

    def total(lo, hi):
        return (got_ref[0, lo:hi] + got_ref[1, lo:hi]) + (got_ref[2, lo:hi] + got_ref[3, lo:hi])

    pair = total(0, RHS)
    core = core_ref[0].astype(F32)
    diagonal = total(n_proj, n_proj + RANK)
    for n in range(copies):
        pay_ref[n, :RHS] = pair
        pay_ref[n, RHS : RHS + RANK] = core
        pay_ref[n, RHS + RANK :] = diagonal
    if out:
        (rest_ref,) = out
        m_proj, m_own, _ = tiles_after(a)
        rest_ref[:m_proj] = total(RHS, n_proj)
        rest_ref[m_proj : m_proj + m_own] = total(n_proj + RANK, n_proj + n_own)
        if n_cross:
            rest_ref[m_proj + m_own :] = total(n_proj + n_own, n_proj + n_own + n_cross)


def final_kernel(cur_ref, w0_ref, w1_ref, w2_ref, w3_ref, v_ref, pos_ref, out_ref):
    leaf = cur_ref.shape[1]
    current = cur_ref[...]
    for a, w_ref in enumerate((w0_ref, w1_ref, w2_ref, w3_ref)):
        current = current - jnp.dot(
            w_ref[...].astype(BF16), v_ref[a * LANES : (a + 1) * LANES], preferred_element_type=F32
        )
    positions = pos_ref[...]
    hot = one_hot_low(positions, leaf)
    high = positions // LANES
    first = round16(current)
    left = current - first
    second = round16(left)
    parts = jnp.concatenate([first, second, left - second], axis=0)
    for h in range(leaf // LANES):
        chosen = jnp.where(high == h, parts, 0.0).astype(BF16)
        moved = lax.dot_general(chosen, hot, NT, preferred_element_type=F32)
        out_ref[:, h * LANES : (h + 1) * LANES] = (moved[:RHS] + moved[RHS : 2 * RHS]) + moved[2 * RHS :]


def local(right_sides, point_order, leaf_inverse, test_bases, trial_bases, coupling_cores):
    devices = lax.axis_size("leaf")
    leaf = right_sides.shape[1]
    total = STAGES * LANES
    test = test_bases.reshape(total, leaf)
    trial = trial_bases.reshape(total, leaf)
    vmem = pl.BlockSpec(memory_space=pltpu.VMEM)
    params = pltpu.CompilerParams(vmem_limit_bytes=40 * 2**20)

    def core_spec(level):
        return pl.BlockSpec((1, RANK, LANES), lambda *_: (level, 0, 0))

    def shape(*dims):
        return jax.ShapeDtypeStruct(dims, F32)

    pay_rows = RHS + 2 * RANK
    rest_rows = sum(tiles_after(0)) + LANES * (STAGES - 1)
    current, pay, rest = pl.pallas_call(
        front_kernel,
        grid=(leaf // BLOCK,),
        in_specs=[
            pl.BlockSpec((RHS, leaf), lambda j: (0, 0)),
            pl.BlockSpec((1, leaf), lambda j: (0, 0)),
            pl.BlockSpec((leaf, BLOCK), lambda j: (0, j)),
            pl.BlockSpec((total, BLOCK), lambda j: (0, j)),
            pl.BlockSpec((total, BLOCK), lambda j: (0, j)),
            core_spec(0),
        ],
        out_specs=[
            pl.BlockSpec((RHS, BLOCK), lambda j: (0, j)),
            pl.BlockSpec((pay_rows, LANES), lambda j: (0, 0)),
            pl.BlockSpec((rest_rows, LANES), lambda j: (0, 0)),
        ],
        out_shape=[shape(RHS, leaf), shape(pay_rows, LANES), shape(rest_rows, LANES)],
        scratch_shapes=[
            pltpu.VMEM((RHS, leaf), BF16),
            pltpu.VMEM((RHS, total), F32),
            pltpu.VMEM((total, total), F32),
        ],
        compiler_params=params,
        name="front",
    )(right_sides, point_order, leaf_inverse, test, trial, coupling_cores)

    def exchange(values, a):
        near = groups((2 * a, 2 * a + 1), devices)
        if a == 0:
            return lax.all_gather(values, "leaf", axis=0, axis_index_groups=near, tiled=True)
        return lax.all_to_all(values, "leaf", 0, 0, axis_index_groups=near, tiled=True)

    def copies(a):
        return 1 if a == 0 else 4

    weights = []
    pay = pay[None]
    for a in range(STAGES):
        got = exchange(pay, a)
        later = STAGES - 1 - a
        out_shape = [shape(RHS, LANES)]
        if later:
            out_shape.append(shape(copies(a), sum(tiles_after(a)), LANES))
        else:
            rest = jnp.zeros((8, LANES), F32)
        solved = pl.pallas_call(
            functools.partial(solve_kernel, a, copies(a)),
            grid=(1,),
            in_specs=[vmem, vmem, core_spec(2 * a + 1)],
            out_specs=[vmem] * len(out_shape),
            out_shape=out_shape,
            compiler_params=params,
            name="solve" + str(a),
        )(got, rest, coupling_cores)
        weights.append(solved[0])
        if not later:
            break
        got = exchange(solved[1], a)
        out_shape = [shape(copies(a + 1), pay_rows, LANES)]
        if later > 1:
            out_shape.append(shape(sum(tiles_after(a + 1)) + LANES * (later - 1), LANES))
        summed = pl.pallas_call(
            functools.partial(sum_kernel, a + 1, copies(a + 1)),
            grid=(1,),
            in_specs=[vmem, core_spec(2 * a + 2)],
            out_specs=[vmem] * len(out_shape),
            out_shape=out_shape,
            compiler_params=params,
            name="sum" + str(a),
        )(got, coupling_cores)
        pay = summed[0]
        if later > 1:
            rest = summed[1]

    return pl.pallas_call(
        final_kernel,
        in_specs=[vmem] * 7,
        out_specs=vmem,
        out_shape=shape(RHS, leaf),
        compiler_params=params,
        name="last",
    )(current, *weights, trial, point_order)


def solution(mesh):
    in_specs = (
        P(None, "leaf"),
        P("leaf", None),
        P("leaf", None),
        P(None, None, "leaf"),
        P(None, None, "leaf"),
        P(None, "leaf", None),
    )
    out_specs = P(None, "leaf")
    return jax.shard_map(local, mesh=mesh, in_specs=in_specs, out_specs=out_specs, check_vma=False)
```

time: 897 us -> 144 us (0.16)
  waiting for transfers between devices: 829 us -> 26.2 us
  blocking collectives: 0 us -> 75.7 us
  matrix products: 21.2 us -> 0 us
  Pallas kernels: 0 us -> 17.5 us
  other arithmetic: 14.1 us -> 0 us
    all_gather x8 -> x1, waiting for transfers between devices: 829 us -> 26.2 us  [exchange(): lax.all_gather(values, 'leaf', axis=0, axis_index_groups=near, tiled=True)]
    all_to_all x0 -> x5, blocking collectives: none -> 69.4 us  [exchange(): lax.all_to_all(values, 'leaf', 0, 0, axis_index_groups=near, tiled=True)]
    dot_general x25 -> x0, matrix products: 21.2 us -> none  [the longest x8 9.15 us: local(): jnp.dot(weights.astype(jnp.bfloat16), trial_bases[level], preferred_eleme...]
    pallas_call x0 -> x9, Pallas kernels: none -> 17.5 us  [the longest x1 9.31 us: local(): pl.pallas_call(front_kernel, grid=(leaf // BLOCK,), in_specs=[pl.BlockSpe...]
    reduce_sum x7 -> x0, other arithmetic: 12.6 us -> none  [half_sums(): gathered.reshape((devices >> level, 2 ** level) + projection.shape)]
    unnamed x5 -> x20, local copies, waits for them, and re-layouts: 1.12 us -> 10.3 us
  transfers between devices with their start and end apart: 8 -> 1, of which waited for: 8 -> 1; matrix products, arithmetic and copies ran while one was open for 0% -> 0% of each run, Pallas kernels for 0% -> 0%
where the time goes in v1:
time: 144 us; the launch traced here: 143 us
  blocking collectives  75.7 us (53%)
  waiting for transfers between devices  26.2 us (18%)
  Pallas kernels  17.5 us (12%)
  between operations  13.4 us (9%)
  local copies, waits for them, and re-layouts  10.3 us (7%)
    all_to_all x5, blocking collectives, exchange(): lax.all_to_all(values, 'leaf', 0, 0, axis_index_groups=near, tiled=True)  69.4 us
    all_gather x1, waiting for transfers between devices, exchange(): lax.all_gather(values, 'leaf', axis=0, axis_index_groups=near, tiled=True)  26.2 us
    unnamed x20, local copies, waits for them, and re-layouts  10.3 us
    pallas_call x1, Pallas kernels, local(): pl.pallas_call(front_kernel, grid=(leaf // BLOCK,), in_specs=[pl.BlockSpe...  9.31 us
    all_gather x1, blocking collectives, exchange(): lax.all_gather(values, 'leaf', axis=0, axis_index_groups=near, tiled=True)  6.28 us
    pallas_call x4, Pallas kernels, local(): pl.pallas_call(functools.partial(solve_kernel, a, copies(a)), grid=(1,),...  4.41 us
    pallas_call x1, Pallas kernels, local(): pl.pallas_call(final_kernel, in_specs=[vmem] * 7, out_specs=vmem, out_sha...  3.63 us
  transfers between devices with their start and end apart: 1, of which 1 were waited for; matrix products, arithmetic and copies ran while one was open for 0% of the time, Pallas kernels for 0%

profile of v1, /device:TPU:32, one launch (start us, length us, event | category | flops | bytes accessed | tf_op | source)
XLA Modules:
  0.0 143.1 jit_solution(3244359224283799505)
XLA Ops:
  6.5 0.0 all-gather.3.cloned.1.call-start
  6.5 0.0 copy-start
  6.5 0.9 copy-done
  7.4 0.0 copy-start.2
  7.4 3.4 %copy-done.2 = bf16[2048,2048]{1,0:T(8,128)(2,1)S(1)} copy-done((bf16[2048,2048]{1,0:T(8,128)(2,1)S(1)}, bf16[2048,2048]{1,0:T(8,128)(2,1)}, u32[]{:S(2)}) %copy-start.2) | copy-done | bytes 8388632
  10.8 1.6 %copy-done.3 = bf16[8,64,2048]{2,1,0:T(8,128)(2,1)S(1)} copy-done((bf16[8,64,2048]{2,1,0:T(8,128)(2,1)S(1)}, bf16[8,64,2048]{2,1,0:T(8,128)(2,1)}, u32[]{:S(2)}) %copy-start.3) | copy-done | bytes 2097176
  12.4 0.0 copy-start.5
  12.4 1.6 %copy-done.5 = bf16[8,64,2048]{2,1,0:T(8,128)(2,1)S(1)} copy-done((bf16[8,64,2048]{2,1,0:T(8,128)(2,1)S(1)}, bf16[8,64,2048]{2,1,0:T(8,128)(2,1)}, u32[]{:S(2)}) %copy-start.5) | copy-done | bytes 2097176
  14.0 0.0 copy-start.7
  14.0 0.8 copy-done.7
  14.8 0.0 copy-start.8
  14.8 0.7 copy-done.8
  15.5 0.0 copy-start.1
  15.5 9.3 %front.1 = (f32[16,2048]{1,0:T(8,128)S(1)}, f32[144,128]{1,0:T(8,128)S(1)}, f32[1008,128]{1,0:T(8,128)S(1)}) custom-call(bf16[16,2048]{1,0:T(8,128)(2,1)S(1)} %copy-done.7, s32[1,2048]{1,0:T(1,128)S(1)} %copy-done.8, bf16[2048,2048]{1,0:T(8,128)(2,1)S(1)} %copy-done.2, bf16[512,2048]{1,0:T(8,128)(2,1)S(1)} %bitcast.5, bf16[512,2048]{1,0:T(8,128)(2,1)S(1)} %bitcast.3, ...), custom_call_target="tpu_custom_call" | custom-call | tf_op jit(solution)/shard_map/front/pallas_call | solution.py:200
  24.9 6.3 %all-gather = f32[576,128]{1,0:T(8,128)S(1)} all-gather(f32[144,128]{1,0:T(8,128)S(1)} %get-tuple-element.19), channel_id=2, replica_groups={{0,1,2,3},{4,5,6,7},{8,9,10,11},{12,13,14,15},{16,17,18,19},{20,21,22,2..., dimensions={0}, use_global_device_ids=true | all-gather | bytes 368640 | tf_op jit(solution)/shard_map/all_gather | solution.py:229
  31.1 1.7 %solve0.1 = (f32[16,128]{1,0:T(8,128)S(1)}, f32[1,624,128]{2,1,0:T(8,128)}) custom-call(f32[4,144,128]{2,1,0:T(8,128)S(1)} %bitcast.6, f32[1008,128]{1,0:T(8,128)S(1)} %get-tuple-element.20.rest_ref, bf16[8,64,128]{2,1,0:T(8,128)(2,1)S(1)} %copy-done), custom_call_target="tpu_custom_call" | custom-call | tf_op jit(solution)/shard_map/solve0/pallas_call | solution.py:245
  32.9 0.0 all-gather.3.cloned.1.call-update
  32.9 26.2 %all-gather.3.cloned.1.call-done.got_ref = f32[4,624,128]{2,1,0:T(8,128)} async-done(((f32[1,624,128]{2,1,0:T(8,128)}), f32[4,624,128]{2,1,0:T(8,128)}) %all-gather.3.cloned.1.call-update) | async-done | bytes 1277968 | tf_op jit(solution)/shard_map/all_gather | solution.py:229
  59.1 0.0 copy-done.1
  59.1 1.3 copy-done.6
  60.4 0.1 sum0.1
  60.5 19.1 %all_to_all.25.got_ref = f32[4,144,128]{2,1,0:T(8,128)S(1)} all-to-all(f32[4,144,128]{2,1,0:T(8,128)S(1)} %get-tuple-element.23), channel_id=1, replica_groups={{0,4,8,12},{1,5,9,13},{2,6,10,14},{3,7,11,15},{16,20,24,28},{17,21,25,2..., dimensions={0} | all-to-all | bytes 589824 | tf_op jit(solution)/shard_map/all_to_all | solution.py:230
  79.6 1.0 solve1.1
  80.5 19.8 %all_to_all.26.got_ref = f32[4,288,128]{2,1,0:T(8,128)S(1)} all-to-all(f32[4,288,128]{2,1,0:T(8,128)S(1)} %get-tuple-element.26), channel_id=1, replica_groups={{0,4,8,12},{1,5,9,13},{2,6,10,14},{3,7,11,15},{16,20,24,28},{17,21,25,2..., dimensions={0} | all-to-all | bytes 1179648 | tf_op jit(solution)/shard_map/all_to_all | solution.py:230
  100.4 11.1 %all_to_all.27.got_ref = f32[4,144,128]{2,1,0:T(8,128)S(1)} all-to-all(f32[4,144,128]{2,1,0:T(8,128)S(1)} %get-tuple-element.27), channel_id=1, replica_groups={{0,16,32,48},{1,17,33,49},{2,18,34,50},{3,19,35,51},{4,20,36,52},{5,21,..., dimensions={0} | all-to-all | bytes 589824 | tf_op jit(solution)/shard_map/all_to_all | solution.py:230
  111.5 0.9 solve2.1
  112.4 8.5 %all_to_all.28.got_ref = f32[4,80,128]{2,1,0:T(8,128)S(1)} all-to-all(f32[4,80,128]{2,1,0:T(8,128)S(1)} %get-tuple-element.30), channel_id=1, replica_groups={{0,16,32,48},{1,17,33,49},{2,18,34,50},{3,19,35,51},{4,20,36,52},{5,21,..., dimensions={0} | all-to-all | bytes 327680 | tf_op jit(solution)/shard_map/all_to_all | solution.py:230
  120.9 10.9 %all_to_all.29.got_ref = f32[4,144,128]{2,1,0:T(8,128)S(1)} all-to-all(f32[4,144,128]{2,1,0:T(8,128)S(1)} %sum2.1), channel_id=1, replica_groups={{0,64,128,192},{1,65,129,193},{2,66,130,194},{3,67,131,195},{4,68,132,1..., dimensions={0} | all-to-all | bytes 589824 | tf_op jit(solution)/shard_map/all_to_all | solution.py:230
  131.8 0.8 solve3.1.w3_ref
  132.6 0.0 copy-done.4
  132.6 0.0 copy-done.9
  132.6 3.6 %last.1 = f32[16,2048]{1,0:T(8,128)} custom-call(f32[16,2048]{1,0:T(8,128)S(1)} %get-tuple-element.18.cur_ref, f32[16,128]{1,0:T(8,128)S(1)} %get-tuple-element.21.w0_ref, f32[16,128]{1,0:T(8,128)S(1)} %get-tuple-element.25.w1_ref, f32[16,128]{1,0:T(8,128)S(1)} %get-tuple-element.29.w2_ref, f32[16,128]{1,0:T(8,128)S(1)} %solve3.1.w3_ref, ...), custom_call_target="tpu_custom_call" | custom-call | tf_op jit(solution)/shard_map/last/pallas_call | solution.py:274
  (7 shorter events, 0.1 us)
Async XLA Ops:
  6.5 52.6 %all-gather.3.cloned.1.call-start = ((), (), s32[]{:S(2)}) async-start(), calls=%async_computation.5 | async-start | bytes 1597440 | tf_op jit(solution)/shard_map/all_gather | solution.py:229
  6.5 0.9 copy-start
  7.4 3.4 %copy-start.2 = (bf16[2048,2048]{1,0:T(8,128)(2,1)S(1)}, bf16[2048,2048]{1,0:T(8,128)(2,1)}, u32[]{:S(2)}) copy-start(bf16[2048,2048]{1,0:T(8,128)(2,1)} %inv_ref.1) | copy-start | bytes 25165828
  10.8 1.6 %copy-start.3 = (bf16[8,64,2048]{2,1,0:T(8,128)(2,1)S(1)}, bf16[8,64,2048]{2,1,0:T(8,128)(2,1)}, u32[]{:S(2)}) copy-start(bf16[8,64,2048]{2,1,0:T(8,128)(2,1)} %param.10) | copy-start | bytes 6291460
  12.4 1.6 %copy-start.5 = (bf16[8,64,2048]{2,1,0:T(8,128)(2,1)S(1)}, bf16[8,64,2048]{2,1,0:T(8,128)(2,1)}, u32[]{:S(2)}) copy-start(bf16[8,64,2048]{2,1,0:T(8,128)(2,1)} %param.9) | copy-start | bytes 6291460
  14.0 0.8 copy-start.7
  14.8 0.7 copy-start.8
  15.5 43.5 %copy-start.1 = (bf16[8,64,128]{2,1,0:T(8,128)(2,1)S(1)}, bf16[8,64,128]{2,1,0:T(8,128)(2,1)}, u32[]{:S(2)}) copy-start(bf16[8,64,128]{2,1,0:T(8,128)(2,1)} %core_ref.15) | copy-start | bytes 393220
  59.1 1.3 copy-start.6
  100.4 32.3 %copy-start.4 = (bf16[8,64,2048]{2,1,0:T(8,128)(2,1)S(1)}, bf16[8,64,2048]{2,1,0:T(8,128)(2,1)}, u32[]{:S(2)}) copy-start(bf16[8,64,2048]{2,1,0:T(8,128)(2,1)} %param.10) | copy-start | bytes 6291460
  100.4 32.3 %copy-start.9 = (s32[1,2048]{1,0:T(1,128)S(1)}, s32[1,2048]{1,0:T(1,128)}, u32[]{:S(2)}) copy-start(s32[1,2048]{1,0:T(1,128)} %pos_ref.3) | copy-start | bytes 24580
Sparse Core Ops, SparseCore 0:
  33.0 26.0 all-gather.2

commit v2 on v0

v2 whole, which is shorter than its diff:
```python
import functools

import jax
import jax.numpy as jnp
from jax import lax
from jax.experimental import pallas as pl
from jax.experimental.pallas import tpu as pltpu
from jax.sharding import PartitionSpec as P


F32 = jnp.float32
BF16 = jnp.bfloat16
PAIRS = 4
RHS = 16
RANK = 64
LANES = 128
WIDE = 256
CHUNKS = 4
NT = (((1,), (1,)), ((), ()))
MESSAGE = RHS + 2 * RANK


def split(x, parts):
    out = []
    for _ in range(parts):
        piece = x.astype(BF16)
        out.append(piece)
        x = x - piece.astype(F32)
    return out


def times(weights, product):
    high, low = split(product, 2)
    return jnp.dot(weights, high, preferred_element_type=F32) + jnp.dot(weights, low, preferred_element_type=F32)


def core_times(stacked, cores):
    rows = stacked.shape[0]
    out = lax.dot_general(jnp.concatenate(split(stacked, 3), axis=0), cores, NT, preferred_element_type=F32)
    return (out[:rows] + (out[rows : 2 * rows] + out[2 * rows :])).astype(BF16)


def lanes(rows=RHS):
    return lax.broadcasted_iota(jnp.int32, (rows, LANES), 1)


def swap(x):
    return pltpu.roll(x, RANK, 1)


def bit(k):
    return lax.axis_index("leaf") >> k & 1


def order(k, own, far):
    upper = bit(k) == 1
    return jnp.where(upper, far, own), jnp.where(upper, own, far)


def side_by_side(k, low, high):
    if k % 2:
        return jnp.where(lanes() < RANK, swap(low), high)
    return jnp.where(lanes() < RANK, low, swap(high))


def one_hot_low(positions, leaf):
    rows = lax.broadcasted_iota(jnp.int32, (WIDE, leaf), 0)
    return jnp.where(rows == (positions & (WIDE - 1)), 1.0, 0.0).astype(BF16)


def gather_points(sides, positions):
    leaf = sides.shape[1]
    sides = sides.astype(BF16)
    positions = positions.astype(jnp.int32)
    high = positions // WIDE
    rows = jnp.concatenate([sides[:, h * WIDE : (h + 1) * WIDE] for h in range(leaf // WIDE)], axis=0)
    picked = jnp.dot(rows, one_hot_low(positions, leaf), preferred_element_type=F32)
    total = jnp.zeros((RHS, leaf), F32)
    for h in range(leaf // WIDE):
        total = total + jnp.where(high == h, picked[h * RHS : (h + 1) * RHS], 0.0)
    return total.astype(BF16)


def front_kernel(
    rows_ref, inv_hbm, u_hbm, v_hbm, cur_ref, pay_ref, rest_ref, near_ref, keep_ref, send_ref,
    inv, u, v, ordered, proj, gram, sems,
):
    leaf = rows_ref.shape[1]
    width = leaf // CHUNKS
    copies = []
    for j in range(CHUNKS):
        at = pl.ds(j * width, width)
        copies.append(
            [
                pltpu.make_async_copy(inv_hbm.at[:, at], inv.at[:, at], sems.at[0, j]),
                pltpu.make_async_copy(u_hbm.at[:, at], u.at[:, at], sems.at[1, j]),
                pltpu.make_async_copy(v_hbm.at[:, at], v.at[:, at], sems.at[2, j]),
            ]
        )
        for copy in copies[-1]:
            copy.start()
    ordered[...] = gather_points(rows_ref[:RHS], rows_ref[RHS : RHS + 1])
    half = 2 * LANES
    for j in range(CHUNKS):
        for copy in copies[j]:
            copy.wait()
        lo, hi = j * width, (j + 1) * width
        current = jnp.dot(ordered[...], inv[:, lo:hi], preferred_element_type=F32)
        cur_ref[:, lo:hi] = current
        rounded = current.astype(BF16)
        left = lax.dot_general(
            jnp.concatenate([rounded, v[:half, lo:hi]], axis=0), u[:half, lo:hi], NT, preferred_element_type=F32
        )
        right = lax.dot_general(
            jnp.concatenate([rounded, v[:, lo:hi]], axis=0), u[half:, lo:hi], NT, preferred_element_type=F32
        )
        if j == 0:
            proj[:, :half] = left[:RHS]
            proj[:, half:] = right[:RHS]
            gram[:half, :half] = left[RHS:]
            gram[:, half:] = right[RHS:]
        else:
            proj[:, :half] += left[:RHS]
            proj[:, half:] += right[:RHS]
            gram[:half, :half] += left[RHS:]
            gram[:, half:] += right[RHS:]

    right_half = lanes(RANK) >= RANK

    def tile(a, b):
        return gram[a * LANES : (a + 1) * LANES, b * LANES : (b + 1) * LANES]

    def diag(a):
        return jnp.where(right_half, gram[a * LANES : a * LANES + RANK, a * LANES : (a + 1) * LANES], 0.0)

    pay_ref[:RHS] = proj[:, :LANES]
    pay_ref[RHS:] = diag(0)
    for b in range(1, PAIRS):
        rest_ref[(b - 1) * RHS : b * RHS] = proj[:, b * LANES : (b + 1) * LANES]
        near_ref[(b - 1) * LANES : b * LANES] = tile(0, b)
    rest_ref[(PAIRS - 1) * RHS :] = diag(1)
    own = bit(0)
    tail = jnp.concatenate([tile(2, 3), jnp.where(right_half, diag(3), swap(diag(2)))], axis=0)
    cut = tail.shape[0] // 2
    halves = [jnp.concatenate([tile(1, 2), tail[:cut]], axis=0), jnp.concatenate([tile(1, 3), tail[cut:]], axis=0)]
    keep_ref[...], send_ref[...] = order(0, *halves)


def pack_kernel(pay_ref, core_ref, out_ref):
    out_ref[:RHS] = pay_ref[:RHS]
    out_ref[RHS : RHS + RANK] = core_ref[0].astype(F32)
    out_ref[RHS + RANK :] = pay_ref[RHS:]


def first_kernel(got_ref, rest_ref, near_ref, core_ref, w_ref, out_ref):
    own = lax.axis_index("leaf") & 3
    weights, after = [], []
    for m in (0, 2):
        pair = [got_ref[m, :RHS], got_ref[m + 1, :RHS]]
        stacked = side_by_side(0, *pair)
        for n in (0, 1):
            weights.append(core_times(stacked, got_ref[m + n, RHS : RHS + RANK].astype(BF16)))
            pair[n] = pair[n] - times(weights[-1], got_ref[m + n, RHS + RANK :])
        after.append(pair[0] + pair[1])
    second = core_times(side_by_side(1, *after), core_ref[0])
    first = jnp.zeros((RHS, RANK), F32)
    for n in range(4):
        first = jnp.where(own == n, weights[n].astype(F32), first)
    w_ref[:, :RANK] = first
    w_ref[:, RANK:] = second.astype(F32)
    both = w_ref[...].astype(BF16)
    for i in range(PAIRS - 1):
        rows = slice(i * RHS, (i + 1) * RHS)
        out_ref[rows] = rest_ref[rows] - times(both, near_ref[i * LANES : (i + 1) * LANES])
    out_ref[(PAIRS - 1) * RHS :] = rest_ref[(PAIRS - 1) * RHS :]


def node_kernel(got_ref, core_ref, pay_ref, keep_ref):
    total = (got_ref[0] + got_ref[1]) + (got_ref[2] + got_ref[3])
    pay_ref[:RHS] = total[:RHS]
    pay_ref[RHS : RHS + RANK] = core_ref[0].astype(F32)
    pay_ref[RHS + RANK :] = total[(PAIRS - 1) * RHS :]
    keep_ref[...] = total[RHS : (PAIRS - 1) * RHS]


def level2_kernel(own_ref, far_ref, w_ref, out_ref):
    own, far = own_ref[:RHS], far_ref[:RHS]
    cores = slice(RHS, RHS + RANK)
    both = both_weights(2, own, far, own_ref[cores], far_ref[cores])
    w_ref[...] = both.astype(F32)
    diag = jnp.concatenate([own_ref[RHS + RANK :], far_ref[RHS + RANK :]], axis=0)
    out_ref[...] = (own + far) - times(both, diag)


def level3_kernel(own_ref, far_ref, core_ref, w2_ref, keep_ref, near_ref, far_near_ref, w_ref, out_ref):
    stacked = side_by_side(3, *order(3, own_ref[...], far_ref[...]))
    w_ref[:, :RANK] = w2_ref[:, :RANK]
    w_ref[:, RANK:] = core_times(stacked, core_ref[0]).astype(F32)
    both = w_ref[...].astype(BF16)
    for i, product in enumerate(order(0, near_ref[...], far_near_ref[...])):
        rows = slice(i * RHS, (i + 1) * RHS)
        out_ref[rows] = keep_ref[rows] - times(both, product)


def add_kernel(a_ref, b_ref, out_ref):
    out_ref[...] = a_ref[...] + b_ref[...]


def late_kernel(a_ref, b_ref, after_ref, out_ref):
    out_ref[...] = a_ref[...] + b_ref[...]


def take_kernel(a_ref, b_ref, after_ref, near_ref, out_ref):
    rows = near_ref.shape[0]
    near_ref[...] = a_ref[:rows] + b_ref[:rows]
    out_ref[...] = a_ref[rows:] + b_ref[rows:]


def level4_products(own_ref, far_ref, core_ref, out_ref):
    rows = own_ref.shape[0]
    out_ref[:rows], out_ref[rows : 2 * rows] = order(0, own_ref[...], far_ref[...])
    out_ref[2 * rows :] = core_ref[0].astype(F32)


def level5_products(own_ref, far_ref, after_ref, core_ref, out_ref):
    out_ref[:RANK] = own_ref[RANK:LANES] + far_ref[RANK:LANES]
    total = own_ref[LANES : LANES + RANK] + far_ref[LANES : LANES + RANK]
    out_ref[RANK:LANES] = jnp.where(lanes(RANK) < RANK, 0.0, total)
    out_ref[LANES:] = core_ref[0].astype(F32)


def level6_products(own_ref, far_ref, after_ref, core_ref, out_ref):
    out_ref[:RANK] = own_ref[RANK:LANES] + far_ref[RANK:LANES]
    out_ref[RANK:] = core_ref[0].astype(F32)


def both_weights(k, own, far, core, far_core):
    stacked = side_by_side(k, *order(k, own, far))
    return core_times(stacked, jnp.concatenate([core, far_core], axis=0).astype(BF16))


def level4_kernel(own_ref, far_ref, prod_ref, far_prod_ref, w_ref, out_ref):
    own, far = own_ref[...], far_ref[...]
    both = both_weights(4, own[:RHS], far[:RHS], prod_ref[LANES + RANK :], far_prod_ref[LANES + RANK :])
    w_ref[...] = both.astype(F32)
    cross = jnp.concatenate([prod_ref[:RANK], far_prod_ref[:RANK]], axis=0)
    diag = jnp.concatenate([prod_ref[LANES : LANES + RANK], far_prod_ref[LANES : LANES + RANK]], axis=0)
    diag = jnp.where(lanes(LANES) < RANK, 0.0, swap(diag))
    total = own + far
    out_ref[:RHS] = total[:RHS] - times(both, diag)
    out_ref[RHS:] = total[RHS:] - times(both, cross)


def level5_kernel(own_ref, far_ref, prod_ref, far_prod_ref, w_ref, out_ref):
    both = both_weights(5, own_ref[:RHS], far_ref[:RHS], prod_ref[LANES:], far_prod_ref[LANES:])
    w_ref[...] = both.astype(F32)
    cross = jnp.concatenate([prod_ref[:RANK], far_prod_ref[:RANK]], axis=0)
    out_ref[...] = (own_ref[RHS:] + far_ref[RHS:]) - times(both, cross)


def level6_kernel(own_ref, far_ref, prod_ref, far_prod_ref, w_ref, out_ref):
    both = both_weights(6, own_ref[...], far_ref[...], prod_ref[RANK:], far_prod_ref[RANK:])
    w_ref[...] = both.astype(F32)
    diag = jnp.concatenate([prod_ref[:RANK], far_prod_ref[:RANK]], axis=0)
    out_ref[...] = (own_ref[...] + far_ref[...]) - times(both, diag)


def last_kernel(own_ref, far_ref, core_ref, cur_ref, w01_ref, w23_ref, w4_ref, w5_ref, w6_ref, v_ref, pos_ref, out_ref):
    leaf = cur_ref.shape[1]
    w7 = core_times(side_by_side(7, *order(7, own_ref[...], far_ref[...])), core_ref[0])
    weights = [w01_ref[...].astype(BF16), w23_ref[...].astype(BF16)]
    weights += [w_ref[:, :RANK].astype(BF16) for w_ref in (w4_ref, w5_ref, w6_ref)] + [w7]
    current = cur_ref[...] - jnp.dot(jnp.concatenate(weights, axis=1), v_ref[...], preferred_element_type=F32)
    positions = pos_ref[...]
    high = positions // WIDE
    parts = jnp.concatenate([x.astype(F32) for x in split(current, 2)], axis=0)
    count = leaf // WIDE
    chosen = [jnp.where(high == h, parts, 0.0).astype(BF16) for h in range(count)]
    moved = lax.dot_general(
        jnp.concatenate(chosen, axis=0), one_hot_low(positions, leaf), NT, preferred_element_type=F32
    )
    for h in range(count):
        lo = 2 * RHS * h
        out_ref[:, h * WIDE : (h + 1) * WIDE] = moved[lo : lo + RHS] + moved[lo + RHS : lo + 2 * RHS]


def local(right_sides, point_order, leaf_inverse, test_bases, trial_bases, coupling_cores):
    devices = lax.axis_size("leaf")
    leaf = right_sides.shape[1]
    total = PAIRS * LANES
    test = test_bases.reshape(total, leaf)
    trial = trial_bases.reshape(total, leaf)
    vmem = pl.BlockSpec(memory_space=pltpu.VMEM)
    anywhere = pl.BlockSpec(memory_space=pl.ANY)
    hbm = pl.BlockSpec(memory_space=pltpu.HBM)

    def shape(*dims):
        return jax.ShapeDtypeStruct(dims, F32)

    def core(level):
        return pl.BlockSpec((1, RANK, LANES), lambda *_: (level, 0, 0))

    def call(kernel, name, args, shapes, level=None, at=None, after=None, limit=16):
        specs = [vmem] * len(args)
        grid = {}
        if at is not None:
            specs[at] = core(level)
            grid = {"grid": (1,)}
        if after is not None:
            specs[after] = anywhere
        return pl.pallas_call(
            kernel,
            in_specs=specs,
            out_specs=[vmem] * len(shapes),
            out_shape=shapes,
            compiler_params=pltpu.CompilerParams(vmem_limit_bytes=limit * 2**20),
            name=name,
            **grid,
        )(*args)

    def pair(values, k):
        return lax.ppermute(values, "leaf", [(d, d ^ 1 << k) for d in range(devices)])

    near_four = [[4 * n + i for i in range(4)] for n in range(devices // 4)]

    def four(values):
        return lax.all_gather(values, "leaf", axis=0, axis_index_groups=near_four)

    cores = coupling_cores
    tail = (LANES + RANK) // 2
    late_rows = LANES + tail
    rows = jnp.concatenate([right_sides.astype(F32), point_order.astype(F32), jnp.zeros((7, leaf), F32)], axis=0)
    current, pay, rest, near, late, late_send = pl.pallas_call(
        front_kernel,
        in_specs=[vmem, anywhere, anywhere, anywhere],
        out_specs=[vmem] * 6,
        out_shape=[
            shape(RHS, leaf),
            shape(RHS + RANK, LANES),
            shape((PAIRS - 1) * RHS + RANK, LANES),
            shape((PAIRS - 1) * LANES, LANES),
            shape(late_rows, LANES),
            shape(late_rows, LANES),
        ],
        scratch_shapes=[
            pltpu.VMEM((leaf, leaf), BF16),
            pltpu.VMEM((total, leaf), BF16),
            pltpu.VMEM((total, leaf), BF16),
            pltpu.VMEM((RHS, leaf), BF16),
            pltpu.VMEM((RHS, total), F32),
            pltpu.VMEM((total, total), F32),
            pltpu.SemaphoreType.DMA((3, CHUNKS)),
        ],
        compiler_params=pltpu.CompilerParams(vmem_limit_bytes=52 * 2**20),
        name="front",
    )(rows, leaf_inverse, test, trial)
    (pay,) = call(pack_kernel, "pack", (pay, cores), [shape(MESSAGE, LANES)], level=0, at=1)

    one = shape(RHS, LANES)
    two = shape(2 * RHS, LANES)

    late_far = pair(late_send, 0)
    got = four(pay)
    (late,) = call(late_kernel, "late0", (late, late_far, got), [shape(late_rows, LANES)], after=2)
    late_far = pair(late, 1)
    w01, rest = call(first_kernel, "first", (got, rest, near, cores), [one, shape(*rest.shape)], level=1, at=3)
    pay, keep = call(node_kernel, "node", (four(rest), cores), [shape(MESSAGE, LANES), two], level=2, at=1)
    pay_far = pair(pay, 2)
    near, prod = call(take_kernel, "late1", (late, late_far, pay), [shape(LANES, LANES), shape(tail, LANES)], after=2)
    near_far = pair(near, 0)
    prod_far = pair(prod, 2)
    w2, half = call(level2_kernel, "level2", (pay, pay_far), [one, one])
    half_far = pair(half, 3)
    w23, keep = call(
        level3_kernel, "level3", (half, half_far, cores, w2, keep, near, near_far), [one, two], level=3, at=2
    )
    keep_far = pair(keep, 2)
    (prod,) = call(late_kernel, "late2", (prod, prod_far, half_far), [shape(tail, LANES)], after=2)
    prod_far = pair(prod, 3)
    (keep,) = call(add_kernel, "sum2", (keep, keep_far), [two])
    keep_far = pair(keep, 3)
    (prod,) = call(late_kernel, "late3", (prod, prod_far, keep), [shape(tail, LANES)], after=2)
    (prod4,) = call(level4_products, "both", (prod, pair(prod, 0), cores), [shape(2 * LANES, LANES)], level=4, at=2)
    far4 = pair(prod4, 4)
    (keep,) = call(add_kernel, "sum3", (keep, keep_far), [two])
    keep_far = pair(keep, 4)
    w4, keep = call(level4_kernel, "level4", (keep, keep_far, prod4, far4), [one, two])
    (prod5,) = call(
        level5_products, "late4", (prod4, far4, w4, cores), [shape(3 * RANK, LANES)], level=5, at=3, after=2
    )
    far5 = pair(prod5, 5)
    w5, keep = call(level5_kernel, "level5", (keep, pair(keep, 5), prod5, far5), [one, one])
    (prod6,) = call(
        level6_products, "late5", (prod5, far5, w5, cores), [shape(2 * RANK, LANES)], level=6, at=3, after=2
    )
    far6 = pair(prod6, 6)
    w6, keep = call(level6_kernel, "level6", (keep, pair(keep, 6), prod6, far6), [one, one])
    return call(
        last_kernel,
        "last",
        (keep, pair(keep, 7), cores, current, w01, w23, w4, w5, w6, trial, point_order),
        [shape(RHS, leaf)],
        level=7,
        at=2,
        limit=32,
    )[0]


def solution(mesh):
    in_specs = (
        P(None, "leaf"),
        P("leaf", None),
        P("leaf", None),
        P(None, None, "leaf"),
        P(None, None, "leaf"),
        P(None, "leaf", None),
    )
    out_specs = P(None, "leaf")
    return jax.shard_map(local, mesh=mesh, in_specs=in_specs, out_specs=out_specs, check_vma=False)
```

time: 897 us -> 86.8 us (0.10)
  the two profiles are of different devices: /device:TPU:32 before, /device:TPU:4 now
where the time goes in v2:
time: 86.8 us; the launch traced here: 86.6 us
  waiting for transfers between devices  31.6 us (36%)
  starting transfers between devices  30.9 us (36%)
  blocking collectives  12.1 us (14%)
  Pallas kernels  10.1 us (12%)
  other arithmetic  1.64 us (2%)
    ppermute x17, waiting for transfers between devices, pair(): lax.ppermute(values, 'leaf', [(d, d ^ 1 << k) for d in range(devices)])  31.6 us
    ppermute x17, starting transfers between devices, pair(): lax.ppermute(values, 'leaf', [(d, d ^ 1 << k) for d in range(devices)])  30.9 us
    all_gather x2, blocking collectives, four(): return lax.all_gather(values, 'leaf', axis=0, axis_index_groups=near_four)  12.1 us
    pallas_call x1, Pallas kernels, local(): pl.pallas_call(front_kernel, in_specs=[vmem, anywhere, anywhere, anywhere...  5.65 us
    pallas_call x18, Pallas kernels, call(): pl.pallas_call(kernel, in_specs=specs, out_specs=[vmem] * len(shapes), ou...  4.48 us
  transfers between devices with their start and end apart: 17, of which 9 were waited for; matrix products, arithmetic and copies ran while one was open for 0% of the time, Pallas kernels for 2%

profile of v2, /device:TPU:4, one launch (start us, length us, event | category | flops | bytes accessed | tf_op | source)
XLA Modules:
  0.0 86.6 jit_solution(16028720886759281575)
XLA Ops:
  0.0 0.7 convert_element_type.7
  0.7 0.8 convert_element_type.6
  1.7 5.6 %front.1 = (f32[16,2048]{1,0:T(8,128)S(1)}, f32[80,128]{1,0:T(8,128)S(1)}, f32[112,128]{1,0:T(8,128)S(1)}, f32[384,128]{1,0:T(8,128)S(1)}, f32[224,128]{1,0:T(8,128)S(1)}, /*index=5*/f32[224,128]{1,0:T(8,128)S(1)}) custom-call(f32[24,2048]{1,0:T(8,128)S(1)} %maximum_maximum_fusion.rows_ref, bf16[2048,2048]{1,0:T(8,128)(2,1)} %inv_hbm.1, ...), custom_call_target="tpu_custom_call" | custom-call | tf_op jit(solution)/shard_map/front/pallas_call | solution.py:333
  7.5 6.4 %all-gather = f32[576,128]{1,0:T(8,128)S(1)} all-gather(f32[144,128]{1,0:T(8,128)S(1)} %pack.1), channel_id=2, replica_groups={{0,1,2,3},{4,5,6,7},{8,9,10,11},{12,13,14,15},{16,17,18,19},{20,21,22,2..., dimensions={0}, use_global_device_ids=true | all-gather | bytes 368640 | tf_op jit(solution)/shard_map/all_gather | solution.py:327
  13.9 0.9 %first.1 = (f32[16,128]{1,0:T(8,128)S(1)}, f32[112,128]{1,0:T(8,128)S(1)}) custom-call(f32[4,144,128]{2,1,0:T(8,128)S(1)} %bitcast.6, f32[112,128]{1,0:T(8,128)S(1)} %get-tuple-element.28.rest_ref, f32[384,128]{1,0:T(8,128)S(1)} %get-tuple-element.29.near_ref, bf16[8,64,128]{2,1,0:T(8,128)(2,1)S(1)} %copy-done.1), custom_call_target="tpu_custom_call" | custom-call | tf_op jit(solution)/shard_map/first/pallas_call | solution.py:311
  14.8 1.8 %collective-permute-start.3 = (f32[224,128]{1,0:T(8,128)S(1)}, f32[224,128]{1,0:T(8,128)S(1)}, u32[]{:S(2)}, u32[]{:S(2)}) collective-permute-start(f32[224,128]{1,0:T(8,128)S(1)} %late0.1.a_ref), channel_id=1, source_target_pairs={{0,2},{1,3},{2,0},{3,1},{4,6},{5,7},{6,4},{7,5},{8,10},{9,11},{10,... | collective-permute-start | bytes 344072 | tf_op jit(solution)/shard_map/ppermute | solution.py:322
  16.7 5.7 %all-gather.1 = f32[448,128]{1,0:T(8,128)S(1)} all-gather(f32[112,128]{1,0:T(8,128)S(1)} %get-tuple-element.30), channel_id=3, replica_groups={{0,1,2,3},{4,5,6,7},{8,9,10,11},{12,13,14,15},{16,17,18,19},{20,21,22,2..., dimensions={0}, use_global_device_ids=true | all-gather | bytes 286720 | tf_op jit(solution)/shard_map/all_gather | solution.py:327
  22.4 3.3 %collective-permute-start = (f32[144,128]{1,0:T(8,128)S(1)}, f32[144,128]{1,0:T(8,128)S(1)}, u32[]{:S(2)}, u32[]{:S(2)}) collective-permute-start(f32[144,128]{1,0:T(8,128)S(1)} %get-tuple-element.31.own_ref.after_ref), channel_id=1, source_target_pairs={{0,4},{1,5},{2,6},{3,7},{4,0},{5,1},{6,2},{7,3},{8,12},{9,13},{10,... | collective-permute-start | bytes 221192 | tf_op jit(solution)/shard_map/ppermute | solution.py:322
  26.0 4.3 %collective-permute-done.far_ref = f32[144,128]{1,0:T(8,128)S(1)} collective-permute-done((f32[144,128]{1,0:T(8,128)S(1)}, f32[144,128]{1,0:T(8,128)S(1)}, u32[]{:S(2)}, u32[]{:S(2)}) %collective-permute-start) | collective-permute-done | bytes 73760 | tf_op jit(solution)/shard_map/ppermute | solution.py:322
  30.3 0.3 level2.1
  30.7 7.7 %collective-permute-start.1 = (f32[16,128]{1,0:T(8,128)S(1)}, f32[16,128]{1,0:T(8,128)S(1)}, u32[]{:S(2)}, u32[]{:S(2)}) collective-permute-start(f32[16,128]{1,0:T(8,128)S(1)} %get-tuple-element.32.own_ref), channel_id=1, source_target_pairs={{0,8},{1,9},{2,10},{3,11},{4,12},{5,13},{6,14},{7,15},{8,0},{9,1},... | collective-permute-start | bytes 24584 | tf_op jit(solution)/shard_map/ppermute | solution.py:322
  38.4 1.6 %collective-permute-done.1.far_ref.after_ref = f32[16,128]{1,0:T(8,128)S(1)} collective-permute-done((f32[16,128]{1,0:T(8,128)S(1)}, f32[16,128]{1,0:T(8,128)S(1)}, u32[]{:S(2)}, u32[]{:S(2)}) %collective-permute-start.1) | collective-permute-done | bytes 8224 | tf_op jit(solution)/shard_map/ppermute | solution.py:322
  40.0 6.0 %collective-permute-start.9 = (f32[96,128]{1,0:T(8,128)S(1)}, f32[96,128]{1,0:T(8,128)S(1)}, u32[]{:S(2)}, u32[]{:S(2)}) collective-permute-start(f32[96,128]{1,0:T(8,128)S(1)} %late2.1.a_ref), channel_id=1, source_target_pairs={{0,8},{1,9},{2,10},{3,11},{4,12},{5,13},{6,14},{7,15},{8,0},{9,1},... | collective-permute-start | bytes 147464 | tf_op jit(solution)/shard_map/ppermute | solution.py:322
  46.1 0.4 level3.1
  46.5 4.6 %collective-permute-done.5.b_ref = f32[32,128]{1,0:T(8,128)S(1)} collective-permute-done((f32[32,128]{1,0:T(8,128)S(1)}, f32[32,128]{1,0:T(8,128)S(1)}, u32[]{:S(2)}, u32[]{:S(2)}) %collective-permute-start.5) | collective-permute-done | bytes 16416 | tf_op jit(solution)/shard_map/ppermute | solution.py:322
  51.2 1.2 %collective-permute-done.10.far_ref = f32[96,128]{1,0:T(8,128)S(1)} collective-permute-done((f32[96,128]{1,0:T(8,128)S(1)}, f32[96,128]{1,0:T(8,128)S(1)}, u32[]{:S(2)}, u32[]{:S(2)}) %collective-permute-start.10) | collective-permute-done | bytes 49184 | tf_op jit(solution)/shard_map/ppermute | solution.py:322
  52.5 1.7 %collective-permute-start.11 = (f32[256,128]{1,0:T(8,128)S(1)}, f32[256,128]{1,0:T(8,128)S(1)}, u32[]{:S(2)}, u32[]{:S(2)}) collective-permute-start(f32[256,128]{1,0:T(8,128)S(1)} %both.1.prod_ref.own_ref), channel_id=1, source_target_pairs={{0,16},{1,17},{2,18},{3,19},{4,20},{5,21},{6,22},{7,23},{8,24},{9,... | collective-permute-start | bytes 393224 | tf_op jit(solution)/shard_map/ppermute | solution.py:322
  54.1 2.9 %collective-permute-start.6 = (f32[32,128]{1,0:T(8,128)S(1)}, f32[32,128]{1,0:T(8,128)S(1)}, u32[]{:S(2)}, u32[]{:S(2)}) collective-permute-start(f32[32,128]{1,0:T(8,128)S(1)} %sum2.1.a_ref.after_ref), channel_id=1, source_target_pairs={{0,8},{1,9},{2,10},{3,11},{4,12},{5,13},{6,14},{7,15},{8,0},{9,1},... | collective-permute-start | bytes 49160 | tf_op jit(solution)/shard_map/ppermute | solution.py:322
  57.1 4.7 %collective-permute-done.6.b_ref = f32[32,128]{1,0:T(8,128)S(1)} collective-permute-done((f32[32,128]{1,0:T(8,128)S(1)}, f32[32,128]{1,0:T(8,128)S(1)}, u32[]{:S(2)}, u32[]{:S(2)}) %collective-permute-start.6) | collective-permute-done | bytes 16416 | tf_op jit(solution)/shard_map/ppermute | solution.py:322
  61.8 0.4 collective-permute-start.7
  62.2 3.3 %collective-permute-done.7.far_ref = f32[32,128]{1,0:T(8,128)S(1)} collective-permute-done((f32[32,128]{1,0:T(8,128)S(1)}, f32[32,128]{1,0:T(8,128)S(1)}, u32[]{:S(2)}, u32[]{:S(2)}) %collective-permute-start.7) | collective-permute-done | bytes 16416 | tf_op jit(solution)/shard_map/ppermute | solution.py:322
  65.9 3.0 %collective-permute-start.13 = (f32[192,128]{1,0:T(8,128)S(1)}, f32[192,128]{1,0:T(8,128)S(1)}, u32[]{:S(2)}, u32[]{:S(2)}) collective-permute-start(f32[192,128]{1,0:T(8,128)S(1)} %late4.1.prod_ref.own_ref), channel_id=1, source_target_pairs={{0,32},{1,33},{2,34},{3,35},{4,36},{5,37},{6,38},{7,39},{8,40},{9,... | collective-permute-start | bytes 294920 | tf_op jit(solution)/shard_map/ppermute | solution.py:322
  68.9 0.6 collective-permute-start.12
  69.5 4.6 %collective-permute-done.12.far_ref = f32[32,128]{1,0:T(8,128)S(1)} collective-permute-done((f32[32,128]{1,0:T(8,128)S(1)}, f32[32,128]{1,0:T(8,128)S(1)}, u32[]{:S(2)}, u32[]{:S(2)}) %collective-permute-start.12) | collective-permute-done | bytes 16416 | tf_op jit(solution)/shard_map/ppermute | solution.py:322
  74.1 0.3 level5.1
  74.5 1.3 %collective-permute-start.15 = (f32[128,128]{1,0:T(8,128)S(1)}, f32[128,128]{1,0:T(8,128)S(1)}, u32[]{:S(2)}, u32[]{:S(2)}) collective-permute-start(f32[128,128]{1,0:T(8,128)S(1)} %late5.1.prod_ref), channel_id=1, source_target_pairs={{0,64},{1,65},{2,66},{3,67},{4,68},{5,69},{6,70},{7,71},{8,72},{9,... | collective-permute-start | bytes 196616 | tf_op jit(solution)/shard_map/ppermute | solution.py:322
  75.8 0.8 collective-permute-start.14
  76.6 2.8 %collective-permute-done.14.far_ref = f32[16,128]{1,0:T(8,128)S(1)} collective-permute-done((f32[16,128]{1,0:T(8,128)S(1)}, f32[16,128]{1,0:T(8,128)S(1)}, u32[]{:S(2)}, u32[]{:S(2)}) %collective-permute-start.14) | collective-permute-done | bytes 8224 | tf_op jit(solution)/shard_map/ppermute | solution.py:322
  79.4 0.3 level6.1
  79.8 0.8 collective-permute-start.16
  80.6 4.3 %collective-permute-done.16.far_ref = f32[16,128]{1,0:T(8,128)S(1)} collective-permute-done((f32[16,128]{1,0:T(8,128)S(1)}, f32[16,128]{1,0:T(8,128)S(1)}, u32[]{:S(2)}, u32[]{:S(2)}) %collective-permute-start.16) | collective-permute-done | bytes 8224 | tf_op jit(solution)/shard_map/ppermute | solution.py:322
  84.9 1.7 %last.1 = f32[16,2048]{1,0:T(8,128)} custom-call(f32[16,128]{1,0:T(8,128)S(1)} %get-tuple-element.44.own_ref, f32[16,128]{1,0:T(8,128)S(1)} %collective-permute-done.16.far_ref, bf16[8,64,128]{2,1,0:T(8,128)(2,1)S(1)} %copy-done.1, f32[16,2048]{1,0:T(8,128)S(1)} %get-tuple-element.45.cur_ref, f32[16,128]{1,0:T(8,128)S(1)} %get-tuple-element.46.w01_ref, ...), custom_call_target="tpu_custom_call" | custom-call | tf_op jit(solution)/shard_map/last/pallas_call | solution.py:311
  (34 shorter events, 1.1 us)
Async XLA Ops:
  1.7 5.8 %copy-start.1 = (bf16[8,64,128]{2,1,0:T(8,128)(2,1)S(1)}, bf16[8,64,128]{2,1,0:T(8,128)(2,1)}, u32[]{:S(2)}) copy-start(bf16[8,64,128]{2,1,0:T(8,128)(2,1)} %core_ref.15) | copy-start | bytes 393220
  7.4 7.4 %collective-permute-start.2 = (f32[224,128]{1,0:T(8,128)S(1)}, f32[224,128]{1,0:T(8,128)S(1)}, u32[]{:S(2)}, u32[]{:S(2)}) collective-permute-start(f32[224,128]{1,0:T(8,128)S(1)} %get-tuple-element.36), channel_id=1, source_target_pairs={{0,1},{1,0},{2,3},{3,2},{4,5},{5,4},{6,7},{7,6},{8,9},{9,8},{10,11... | collective-permute-start | bytes 344072 | tf_op jit(solution)/shard_map/ppermute | solution.py:322
  14.8 70.1 %copy-start = (bf16[8,64,2048]{2,1,0:T(8,128)(2,1)S(1)}, bf16[8,64,2048]{2,1,0:T(8,128)(2,1)}, u32[]{:S(2)}) copy-start(bf16[8,64,2048]{2,1,0:T(8,128)(2,1)} %param.10) | copy-start | bytes 6291460
  14.8 70.1 %copy-start.2 = (s32[1,2048]{1,0:T(1,128)S(1)}, s32[1,2048]{1,0:T(1,128)}, u32[]{:S(2)}) copy-start(s32[1,2048]{1,0:T(1,128)} %pos_ref.1) | copy-start | bytes 24580
  14.8 10.9 %collective-permute-start.3 = (f32[224,128]{1,0:T(8,128)S(1)}, f32[224,128]{1,0:T(8,128)S(1)}, u32[]{:S(2)}, u32[]{:S(2)}) collective-permute-start(f32[224,128]{1,0:T(8,128)S(1)} %late0.1.a_ref), channel_id=1, source_target_pairs={{0,2},{1,3},{2,0},{3,1},{4,6},{5,7},{6,4},{7,5},{8,10},{9,11},{10,... | collective-permute-start | bytes 344072 | tf_op jit(solution)/shard_map/ppermute | solution.py:322
  22.4 7.9 %collective-permute-start = (f32[144,128]{1,0:T(8,128)S(1)}, f32[144,128]{1,0:T(8,128)S(1)}, u32[]{:S(2)}, u32[]{:S(2)}) collective-permute-start(f32[144,128]{1,0:T(8,128)S(1)} %get-tuple-element.31.own_ref.after_ref), channel_id=1, source_target_pairs={{0,4},{1,5},{2,6},{3,7},{4,0},{5,1},{6,2},{7,3},{8,12},{9,13},{10,... | collective-permute-start | bytes 221192 | tf_op jit(solution)/shard_map/ppermute | solution.py:322
  25.8 14.3 %collective-permute-start.8 = (f32[96,128]{1,0:T(8,128)S(1)}, f32[96,128]{1,0:T(8,128)S(1)}, u32[]{:S(2)}, u32[]{:S(2)}) collective-permute-start(f32[96,128]{1,0:T(8,128)S(1)} %get-tuple-element.39.a_ref), channel_id=1, source_target_pairs={{0,4},{1,5},{2,6},{3,7},{4,0},{5,1},{6,2},{7,3},{8,12},{9,13},{10,... | collective-permute-start | bytes 147464 | tf_op jit(solution)/shard_map/ppermute | solution.py:322
  25.9 20.2 %collective-permute-start.4 = (f32[128,128]{1,0:T(8,128)S(1)}, f32[128,128]{1,0:T(8,128)S(1)}, u32[]{:S(2)}, u32[]{:S(2)}) collective-permute-start(f32[128,128]{1,0:T(8,128)S(1)} %get-tuple-element.37.near_ref), channel_id=1, source_target_pairs={{0,1},{1,0},{2,3},{3,2},{4,5},{5,4},{6,7},{7,6},{8,9},{9,8},{10,11... | collective-permute-start | bytes 196616 | tf_op jit(solution)/shard_map/ppermute | solution.py:322
  30.7 9.3 %collective-permute-start.1 = (f32[16,128]{1,0:T(8,128)S(1)}, f32[16,128]{1,0:T(8,128)S(1)}, u32[]{:S(2)}, u32[]{:S(2)}) collective-permute-start(f32[16,128]{1,0:T(8,128)S(1)} %get-tuple-element.32.own_ref), channel_id=1, source_target_pairs={{0,8},{1,9},{2,10},{3,11},{4,12},{5,13},{6,14},{7,15},{8,0},{9,1},... | collective-permute-start | bytes 24584 | tf_op jit(solution)/shard_map/ppermute | solution.py:322
  40.0 11.1 %collective-permute-start.9 = (f32[96,128]{1,0:T(8,128)S(1)}, f32[96,128]{1,0:T(8,128)S(1)}, u32[]{:S(2)}, u32[]{:S(2)}) collective-permute-start(f32[96,128]{1,0:T(8,128)S(1)} %late2.1.a_ref), channel_id=1, source_target_pairs={{0,8},{1,9},{2,10},{3,11},{4,12},{5,13},{6,14},{7,15},{8,0},{9,1},... | collective-permute-start | bytes 147464 | tf_op jit(solution)/shard_map/ppermute | solution.py:322
  46.5 4.7 %collective-permute-start.5 = (f32[32,128]{1,0:T(8,128)S(1)}, f32[32,128]{1,0:T(8,128)S(1)}, u32[]{:S(2)}, u32[]{:S(2)}) collective-permute-start(f32[32,128]{1,0:T(8,128)S(1)} %get-tuple-element.38.a_ref), channel_id=1, source_target_pairs={{0,4},{1,5},{2,6},{3,7},{4,0},{5,1},{6,2},{7,3},{8,12},{9,13},{10,... | collective-permute-start | bytes 49160 | tf_op jit(solution)/shard_map/ppermute | solution.py:322
  51.1 1.3 %collective-permute-start.10 = (f32[96,128]{1,0:T(8,128)S(1)}, f32[96,128]{1,0:T(8,128)S(1)}, u32[]{:S(2)}, u32[]{:S(2)}) collective-permute-start(f32[96,128]{1,0:T(8,128)S(1)} %late3.1.own_ref), channel_id=1, source_target_pairs={{0,1},{1,0},{2,3},{3,2},{4,5},{5,4},{6,7},{7,6},{8,9},{9,8},{10,11... | collective-permute-start | bytes 147464 | tf_op jit(solution)/shard_map/ppermute | solution.py:322
  52.5 13.1 %collective-permute-start.11 = (f32[256,128]{1,0:T(8,128)S(1)}, f32[256,128]{1,0:T(8,128)S(1)}, u32[]{:S(2)}, u32[]{:S(2)}) collective-permute-start(f32[256,128]{1,0:T(8,128)S(1)} %both.1.prod_ref.own_ref), channel_id=1, source_target_pairs={{0,16},{1,17},{2,18},{3,19},{4,20},{5,21},{6,22},{7,23},{8,24},{9,... | collective-permute-start | bytes 393224 | tf_op jit(solution)/shard_map/ppermute | solution.py:322
  54.1 7.6 %collective-permute-start.6 = (f32[32,128]{1,0:T(8,128)S(1)}, f32[32,128]{1,0:T(8,128)S(1)}, u32[]{:S(2)}, u32[]{:S(2)}) collective-permute-start(f32[32,128]{1,0:T(8,128)S(1)} %sum2.1.a_ref.after_ref), channel_id=1, source_target_pairs={{0,8},{1,9},{2,10},{3,11},{4,12},{5,13},{6,14},{7,15},{8,0},{9,1},... | collective-permute-start | bytes 49160 | tf_op jit(solution)/shard_map/ppermute | solution.py:322
  61.8 3.7 %collective-permute-start.7 = (f32[32,128]{1,0:T(8,128)S(1)}, f32[32,128]{1,0:T(8,128)S(1)}, u32[]{:S(2)}, u32[]{:S(2)}) collective-permute-start(f32[32,128]{1,0:T(8,128)S(1)} %sum3.1.own_ref), channel_id=1, source_target_pairs={{0,16},{1,17},{2,18},{3,19},{4,20},{5,21},{6,22},{7,23},{8,24},{9,... | collective-permute-start | bytes 49160 | tf_op jit(solution)/shard_map/ppermute | solution.py:322
  65.9 8.2 %collective-permute-start.13 = (f32[192,128]{1,0:T(8,128)S(1)}, f32[192,128]{1,0:T(8,128)S(1)}, u32[]{:S(2)}, u32[]{:S(2)}) collective-permute-start(f32[192,128]{1,0:T(8,128)S(1)} %late4.1.prod_ref.own_ref), channel_id=1, source_target_pairs={{0,32},{1,33},{2,34},{3,35},{4,36},{5,37},{6,38},{7,39},{8,40},{9,... | collective-permute-start | bytes 294920 | tf_op jit(solution)/shard_map/ppermute | solution.py:322
  68.9 5.2 %collective-permute-start.12 = (f32[32,128]{1,0:T(8,128)S(1)}, f32[32,128]{1,0:T(8,128)S(1)}, u32[]{:S(2)}, u32[]{:S(2)}) collective-permute-start(f32[32,128]{1,0:T(8,128)S(1)} %get-tuple-element.40.own_ref), channel_id=1, source_target_pairs={{0,32},{1,33},{2,34},{3,35},{4,36},{5,37},{6,38},{7,39},{8,40},{9,... | collective-permute-start | bytes 49160 | tf_op jit(solution)/shard_map/ppermute | solution.py:322
  74.5 4.9 %collective-permute-start.15 = (f32[128,128]{1,0:T(8,128)S(1)}, f32[128,128]{1,0:T(8,128)S(1)}, u32[]{:S(2)}, u32[]{:S(2)}) collective-permute-start(f32[128,128]{1,0:T(8,128)S(1)} %late5.1.prod_ref), channel_id=1, source_target_pairs={{0,64},{1,65},{2,66},{3,67},{4,68},{5,69},{6,70},{7,71},{8,72},{9,... | collective-permute-start | bytes 196616 | tf_op jit(solution)/shard_map/ppermute | solution.py:322
  75.8 3.7 %collective-permute-start.14 = (f32[16,128]{1,0:T(8,128)S(1)}, f32[16,128]{1,0:T(8,128)S(1)}, u32[]{:S(2)}, u32[]{:S(2)}) collective-permute-start(f32[16,128]{1,0:T(8,128)S(1)} %get-tuple-element.42.own_ref), channel_id=1, source_target_pairs={{0,64},{1,65},{2,66},{3,67},{4,68},{5,69},{6,70},{7,71},{8,72},{9,... | collective-permute-start | bytes 24584 | tf_op jit(solution)/shard_map/ppermute | solution.py:322
  79.8 5.2 %collective-permute-start.16 = (f32[16,128]{1,0:T(8,128)S(1)}, f32[16,128]{1,0:T(8,128)S(1)}, u32[]{:S(2)}, u32[]{:S(2)}) collective-permute-start(f32[16,128]{1,0:T(8,128)S(1)} %get-tuple-element.44.own_ref), channel_id=1, source_target_pairs={{0,128},{1,129},{2,130},{3,131},{4,132},{5,133},{6,134},{7,135},{8... | collective-permute-start | bytes 24584 | tf_op jit(solution)/shard_map/ppermute | solution.py:322

commit v3 on v0

v3 whole, which is shorter than its diff:
```python
import functools

import jax
import jax.numpy as jnp
from jax import lax
from jax.experimental import pallas as pl
from jax.experimental.pallas import tpu as pltpu
from jax.sharding import PartitionSpec as P


F32 = jnp.float32
BF16 = jnp.bfloat16
PAIRS = 4
RHS = 16
RANK = 64
LANES = 128
WIDE = 256
CHUNKS = 4
NT = (((1,), (1,)), ((), ()))
PAY = RHS + RANK // 2


def split(x, parts):
    out = []
    for _ in range(parts):
        piece = x.astype(BF16)
        out.append(piece)
        x = x - piece.astype(F32)
    return out


def times(weights, product):
    high, low = split(product, 2)
    return jnp.dot(weights, high, preferred_element_type=F32) + jnp.dot(weights, low, preferred_element_type=F32)


def core_times(stacked, cores):
    rows = stacked.shape[0]
    out = lax.dot_general(jnp.concatenate(split(stacked, 3), axis=0), cores, NT, preferred_element_type=F32)
    return (out[:rows] + (out[rows : 2 * rows] + out[2 * rows :])).astype(BF16)


def lanes(rows=RHS):
    return lax.broadcasted_iota(jnp.int32, (rows, LANES), 1)


def swap(x):
    return pltpu.roll(x, RANK, 1)


def bit(k):
    return lax.axis_index("leaf") >> k & 1


def order(k, own, far):
    upper = bit(k) == 1
    return jnp.where(upper, far, own), jnp.where(upper, own, far)


def side_by_side(k, low, high):
    if k % 2:
        return jnp.where(lanes() < RANK, swap(low), high)
    return jnp.where(lanes() < RANK, low, swap(high))


def one_hot_low(positions, leaf):
    rows = lax.broadcasted_iota(jnp.int32, (WIDE, leaf), 0)
    return jnp.where(rows == (positions & (WIDE - 1)), 1.0, 0.0).astype(BF16)


def gather_points(sides, positions):
    leaf = sides.shape[1]
    high = positions // WIDE
    rows = jnp.concatenate([sides[:, h * WIDE : (h + 1) * WIDE] for h in range(leaf // WIDE)], axis=0)
    picked = jnp.dot(rows, one_hot_low(positions, leaf), preferred_element_type=F32)
    total = jnp.zeros((RHS, leaf), F32)
    for h in range(leaf // WIDE):
        total = total + jnp.where(high == h, picked[h * RHS : (h + 1) * RHS], 0.0)
    return total.astype(BF16)


def chunked(leaf, pairs, sems):
    width = leaf // CHUNKS
    copies = []
    for j in range(CHUNKS):
        at = pl.ds(j * width, width)
        copies.append(
            [pltpu.make_async_copy(src.at[:, at], dst.at[:, at], sems.at[i, j]) for i, (src, dst) in enumerate(pairs)]
        )
        for copy in copies[-1]:
            copy.start()
    return copies


def pack(right):
    half = RANK // 2
    return jnp.where(lanes(half) < RANK, swap(right[:half]), right[half:])


def unpack(rows):
    both = jnp.concatenate([swap(rows), rows], axis=0)
    return jnp.where(lanes(RANK) < RANK, 0.0, both)


def leaf_kernel(
    rs_ref, pos_ref, inv_hbm, u_hbm, v_hbm, cur_ref, pay_ref, rest_ref, near_ref, inv, u, v, ordered, both, sems
):
    leaf = rs_ref.shape[1]
    width = leaf // CHUNKS
    copies = chunked(leaf, [(inv_hbm, inv), (u_hbm, u), (v_hbm.at[:LANES], v)], sems)
    ordered[...] = gather_points(rs_ref[...], pos_ref[...])
    for j in range(CHUNKS):
        for copy in copies[j]:
            copy.wait()
        lo, hi = j * width, (j + 1) * width
        current = jnp.dot(ordered[...], inv[:, lo:hi], preferred_element_type=F32)
        cur_ref[:, lo:hi] = current
        rows = jnp.concatenate([current.astype(BF16), v[:, lo:hi]], axis=0)
        part = lax.dot_general(rows, u[:, lo:hi], NT, preferred_element_type=F32)
        if j == 0:
            both[...] = part
        else:
            both[...] += part
    pay_ref[:RHS] = both[:RHS, :LANES]
    pay_ref[RHS:] = pack(both[RHS : RHS + RANK, :LANES])
    for b in range(1, PAIRS):
        rest_ref[(b - 1) * RHS : b * RHS] = both[:RHS, b * LANES : (b + 1) * LANES]
        near_ref[(b - 1) * LANES : b * LANES] = both[RHS:, b * LANES : (b + 1) * LANES]


def products_kernel(u_hbm, v_hbm, diag_ref, keep_ref, send_ref, u, v, gram, sems):
    leaf = u.shape[1]
    width = leaf // CHUNKS
    copies = chunked(leaf, [(u_hbm.at[LANES:], u), (v_hbm.at[LANES:], v)], sems)
    for j in range(CHUNKS):
        for copy in copies[j]:
            copy.wait()
        lo, hi = j * width, (j + 1) * width
        part = lax.dot_general(v[:, lo:hi], u[:, lo:hi], NT, preferred_element_type=F32)
        if j == 0:
            gram[...] = part
        else:
            gram[...] += part

    def tile(a, b):
        return gram[(a - 1) * LANES : a * LANES, (b - 1) * LANES : b * LANES]

    diag_ref[...] = pack(tile(1, 1)[:RANK])
    diag = jnp.where(lanes(RANK) < RANK, swap(tile(2, 2)[:RANK]), tile(3, 3)[:RANK])
    tail = jnp.concatenate([tile(2, 3), diag], axis=0)
    cut = tail.shape[0] // 2
    halves = [jnp.concatenate([tile(1, 2), tail[:cut]], axis=0), jnp.concatenate([tile(1, 3), tail[cut:]], axis=0)]
    keep_ref[...], send_ref[...] = order(0, *halves)


def first_kernel(pay_ref, core_ref, out_ref):
    rows = pay_ref.shape[0]
    out_ref[:rows] = pay_ref[...]
    out_ref[rows:] = core_ref[0].astype(F32)


def even_step(k, own_ref, far_ref, w_ref, out_ref):
    own, far = own_ref[:RHS], far_ref[:RHS]
    both = both_weights(k, own, far, own_ref[PAY:], far_ref[PAY:])
    w_ref[...] = both.astype(F32)
    at = slice(RHS, PAY)
    diag = jnp.concatenate([unpack(own_ref[at]), unpack(far_ref[at])], axis=0)
    out_ref[...] = (own + far) - times(both, diag)


def level0_kernel(own_ref, far_ref, w_ref, out_ref):
    even_step(0, own_ref, far_ref, w_ref, out_ref)


def level2_kernel(own_ref, far_ref, w_ref, out_ref):
    even_step(2, own_ref, far_ref, w_ref, out_ref)


def odd_weights(k, own_ref, far_ref, core_ref, even_ref, w_ref):
    stacked = side_by_side(k, *order(k, own_ref[...], far_ref[...]))
    w_ref[:, :RANK] = even_ref[:, :RANK]
    w_ref[:, RANK:] = core_times(stacked, core_ref[0]).astype(F32)
    return w_ref[...].astype(BF16)


def level1_kernel(own_ref, far_ref, core_ref, even_ref, rest_ref, near_ref, diag_ref, w_ref, out_ref):
    both = odd_weights(1, own_ref, far_ref, core_ref, even_ref, w_ref)
    later = PAIRS - 1
    for i in range(later):
        rows = slice(i * RHS, (i + 1) * RHS)
        out_ref[rows] = rest_ref[rows] - times(both, near_ref[i * LANES : (i + 1) * LANES])
    out_ref[later * RHS :] = diag_ref[...]


def node_kernel(own_ref, far_ref, core_ref, pay_ref, keep_ref):
    total = own_ref[...] + far_ref[...]
    later = PAIRS - 1
    pay_ref[:RHS] = total[:RHS]
    pay_ref[RHS:PAY] = total[later * RHS :]
    pay_ref[PAY:] = core_ref[0].astype(F32)
    keep_ref[...] = total[RHS : later * RHS]


def level3_kernel(own_ref, far_ref, core_ref, even_ref, keep_ref, near_ref, far_near_ref, w_ref, out_ref):
    both = odd_weights(3, own_ref, far_ref, core_ref, even_ref, w_ref)
    for i, product in enumerate(order(0, near_ref[...], far_near_ref[...])):
        rows = slice(i * RHS, (i + 1) * RHS)
        out_ref[rows] = keep_ref[rows] - times(both, product)


def add_kernel(a_ref, b_ref, out_ref):
    out_ref[...] = a_ref[...] + b_ref[...]


def copy_kernel(a_ref, out_ref):
    out_ref[...] = a_ref[...]


def add_core_kernel(a_ref, b_ref, core_ref, out_ref):
    rows = a_ref.shape[0]
    out_ref[:rows] = a_ref[...] + b_ref[...]
    out_ref[rows:] = core_ref[0].astype(F32)


def take_kernel(a_ref, b_ref, near_ref, out_ref):
    rows = near_ref.shape[0]
    near_ref[...] = a_ref[:rows] + b_ref[:rows]
    out_ref[...] = a_ref[rows:] + b_ref[rows:]


def both_weights(k, own, far, core, far_core):
    stacked = side_by_side(k, *order(k, own, far))
    return core_times(stacked, jnp.concatenate([core, far_core], axis=0).astype(BF16))


def level4_kernel(
    own_ref, far_ref, prod_ref, prod_near_ref, far_prod_ref, far_near_ref, core_ref, w_ref, out_ref
):
    own, far = own_ref[...], far_ref[...]
    rows = prod_ref.shape[0] - RANK
    both = both_weights(4, own[:RHS], far[:RHS], prod_ref[rows:], far_prod_ref[rows:])
    w_ref[...] = both.astype(F32)
    mine = jnp.concatenate(order(0, prod_ref[:rows], prod_near_ref[:rows]), axis=0)
    theirs = jnp.concatenate(order(0, far_prod_ref[:rows], far_near_ref[:rows]), axis=0)
    cross = jnp.concatenate([mine[:RANK], theirs[:RANK]], axis=0)
    diag = jnp.concatenate([mine[LANES:], theirs[LANES:]], axis=0)
    diag = jnp.where(lanes(LANES) < RANK, 0.0, swap(diag))
    total = own + far
    out_ref[:RHS] = total[:RHS] - times(both, diag)
    out_ref[RHS : 2 * RHS] = total[RHS:] - times(both, cross)
    later = mine[RANK:] + theirs[RANK:]
    out_ref[2 * RHS : 2 * RHS + RANK] = later[:RANK]
    out_ref[2 * RHS + RANK : 2 * RHS + RANK + RANK // 2] = pack(later[RANK:])
    out_ref[2 * RHS + RANK + RANK // 2 :] = core_ref[0].astype(F32)


def level5_kernel(own_ref, far_ref, core_ref, w_ref, out_ref):
    cores = slice(2 * RHS + RANK + RANK // 2, own_ref.shape[0])
    both = both_weights(5, own_ref[:RHS], far_ref[:RHS], own_ref[cores], far_ref[cores])
    w_ref[...] = both.astype(F32)
    at = slice(2 * RHS, 2 * RHS + RANK)
    cross = jnp.concatenate([own_ref[at], far_ref[at]], axis=0)
    out_ref[:RHS] = (own_ref[RHS : 2 * RHS] + far_ref[RHS : 2 * RHS]) - times(both, cross)
    at = slice(2 * RHS + RANK, 2 * RHS + RANK + RANK // 2)
    out_ref[RHS:PAY] = own_ref[at] + far_ref[at]
    out_ref[PAY:] = core_ref[0].astype(F32)


def level6_kernel(own_ref, far_ref, w_ref, out_ref):
    even_step(6, own_ref, far_ref, w_ref, out_ref)


def scatter_points(values, positions):
    leaf = positions.shape[1]
    high = positions // WIDE
    count = leaf // WIDE
    parts = jnp.concatenate([x.astype(F32) for x in values], axis=0)
    rows = parts.shape[0]
    chosen = jnp.concatenate([jnp.where(high == h, parts, 0.0).astype(BF16) for h in range(count)], axis=0)
    moved = lax.dot_general(chosen, one_hot_low(positions, leaf), NT, preferred_element_type=F32)
    return [moved[h * rows : (h + 1) * rows] for h in range(count)]


def place_kernel(cur_ref, w01_ref, w23_ref, w4_ref, w5_ref, w6_ref, v_ref, pos_ref, out_ref, basis_ref):
    weights = [w01_ref[...].astype(BF16), w23_ref[...].astype(BF16)]
    weights += [w_ref[:, :RANK].astype(BF16) for w_ref in (w4_ref, w5_ref, w6_ref)]
    known = v_ref.shape[0] - RANK
    current = cur_ref[...] - jnp.dot(jnp.concatenate(weights, axis=1), v_ref[:known], preferred_element_type=F32)
    for h, block in enumerate(scatter_points(split(current, 2) + [v_ref[known:]], pos_ref[...])):
        at = slice(h * WIDE, (h + 1) * WIDE)
        out_ref[:, at] = block[:RHS] + block[RHS : 2 * RHS]
        basis_ref[:, at] = block[2 * RHS :].astype(BF16)


def last_kernel(own_ref, far_ref, core_ref, placed_ref, basis_ref, out_ref):
    weights = core_times(side_by_side(7, *order(7, own_ref[...], far_ref[...])), core_ref[0])
    out_ref[...] = placed_ref[...] - jnp.dot(weights, basis_ref[...], preferred_element_type=F32)


def local(right_sides, point_order, leaf_inverse, test_bases, trial_bases, coupling_cores):
    devices = lax.axis_size("leaf")
    leaf = right_sides.shape[1]
    total = PAIRS * LANES
    test = test_bases.reshape(total, leaf)
    trial = trial_bases.reshape(total, leaf)
    vmem = pl.BlockSpec(memory_space=pltpu.VMEM)
    anywhere = pl.BlockSpec(memory_space=pl.ANY)
    hbm = pl.BlockSpec(memory_space=pltpu.HBM)

    def shape(*dims):
        return jax.ShapeDtypeStruct(dims, F32)

    def core(level):
        return pl.BlockSpec((1, RANK, LANES), lambda *_: (level, 0, 0))

    def call(kernel, name, args, shapes, level=None, at=None, after=(), limit=16, hint=0):
        count = len(args)
        specs = [vmem] * count + [anywhere] * len(after)
        grid = {}
        if at is not None:
            specs[at] = core(level)
            grid = {"grid": (1,)}

        def body(*refs):
            kernel(*refs[:count], *refs[count + len(after) :])

        return pl.pallas_call(
            body,
            in_specs=specs,
            out_specs=[vmem] * len(shapes),
            out_shape=shapes,
            compiler_params=pltpu.CompilerParams(vmem_limit_bytes=limit * 2**20),
            name=name,
            cost_estimate=pl.CostEstimate(flops=hint, bytes_accessed=0, transcendentals=0) if hint else None,
            **grid,
        )(*args, *after)

    main = functools.partial(call, hint=int(6e9))

    def pair(values, k):
        mask = {3: 3 << 2, 5: 3 << 4, 7: 3 << 6}.get(k, 1 << k)
        return lax.ppermute(values, "leaf", [(d, d ^ mask) for d in range(devices)])

    cores = coupling_cores
    tail = (LANES + RANK) // 2
    late_rows = LANES + tail
    later_rows = (PAIRS - 1) * RHS
    big = pltpu.CompilerParams(vmem_limit_bytes=52 * 2**20)
    current, pay, rest, near = pl.pallas_call(
        leaf_kernel,
        in_specs=[vmem, vmem, anywhere, anywhere, anywhere],
        out_specs=[vmem] * 4,
        out_shape=[
            shape(RHS, leaf),
            shape(PAY, LANES),
            shape(later_rows, LANES),
            shape((PAIRS - 1) * LANES, LANES),
        ],
        scratch_shapes=[
            pltpu.VMEM((leaf, leaf), BF16),
            pltpu.VMEM((total, leaf), BF16),
            pltpu.VMEM((LANES, leaf), BF16),
            pltpu.VMEM((RHS, leaf), BF16),
            pltpu.VMEM((RHS + LANES, total), F32),
            pltpu.SemaphoreType.DMA((3, CHUNKS)),
        ],
        compiler_params=big,
        name="leaf",
    )(right_sides, point_order, leaf_inverse, test, trial)

    one = shape(RHS, LANES)
    two = shape(2 * RHS, LANES)

    (pay,) = call(first_kernel, "first", (pay, cores), [shape(PAY + RANK, LANES)], 0, 1)
    w0, half = main(level0_kernel, "level0", (pay, pair(pay, 0)), [one, one])
    half_far = pair(half, 1)

    def products_body(after_ref, *refs):
        products_kernel(*refs)

    diag, late, late_send = pl.pallas_call(
        products_body,
        in_specs=[anywhere] * 3,
        out_specs=[vmem] * 3,
        out_shape=[shape(RANK // 2, LANES), shape(late_rows, LANES), shape(late_rows, LANES)],
        scratch_shapes=[
            pltpu.VMEM((total - LANES, leaf), BF16),
            pltpu.VMEM((total - LANES, leaf), BF16),
            pltpu.VMEM((total - LANES, total - LANES), F32),
            pltpu.SemaphoreType.DMA((2, CHUNKS)),
        ],
        compiler_params=big,
        cost_estimate=pl.CostEstimate(flops=2 * leaf * (total - LANES) ** 2, bytes_accessed=4 * leaf * (total - LANES), transcendentals=0),
        name="products",
    )(half, test, trial)
    late_far = pair(late_send, 0)
    w01, rest = main(
        level1_kernel,
        "level1",
        (half, half_far, cores, w0, rest, near, diag),
        [one, shape(later_rows + RANK // 2, LANES)],
        1,
        2,
    )
    rest_far = pair(rest, 0)
    (late,) = call(add_kernel, "late0", (late, late_far), [shape(late_rows, LANES)], after=(w01,))
    late_far = pair(late, 1)
    (rest,) = main(add_kernel, "sum0", (rest, rest_far), [shape(later_rows + RANK // 2, LANES)])
    rest_far = pair(rest, 1)
    pay, keep = main(node_kernel, "node", (rest, rest_far, cores), [shape(PAY + RANK, LANES), two], 2, 2)
    pay_far = pair(pay, 2)
    near, prod = call(take_kernel, "late1", (late, late_far), [shape(LANES, LANES), shape(tail, LANES)], after=(rest,))
    near_far = pair(near, 0)
    prod_far = pair(prod, 2)
    w2, half = main(level2_kernel, "level2", (pay, pay_far), [one, one])
    half_far = pair(half, 3)
    (prod,) = call(add_kernel, "late2", (prod, prod_far), [shape(tail, LANES)], after=(half_far,))
    prod_far = pair(prod, 3)
    w23, keep = main(
        level3_kernel, "level3", (half, half_far, cores, w2, keep, near, near_far), [one, two], 3, 2
    )
    keep_far = pair(keep, 2)
    (keep,) = main(add_kernel, "sum2", (keep, keep_far), [two])
    keep_far = pair(keep, 3)
    (prod,) = call(add_core_kernel, "late3", (prod, prod_far, cores), [shape(tail + RANK, LANES)], 4, 2, (keep,))
    prod_near, far_prod = pair(prod, 0), pair(prod, 4)
    (keep,) = main(add_kernel, "sum3", (keep, keep_far), [two])
    keep_far = pair(keep, 4)
    (far_copy,) = call(copy_kernel, "late4", (far_prod,), [shape(*far_prod.shape)], after=(keep,))
    w4, keep = main(
        level4_kernel,
        "level4",
        (keep, keep_far, prod, prod_near, far_prod, pair(far_copy, 0), cores),
        [one, shape(2 * RHS + 2 * RANK + RANK // 2, LANES)],
        5,
        6,
    )
    w5, keep = main(level5_kernel, "level5", (keep, pair(keep, 5), cores), [one, shape(PAY + RANK, LANES)], 6, 2)
    w6, keep = main(level6_kernel, "level6", (keep, pair(keep, 6)), [one, one])
    keep_far = pair(keep, 7)
    placed, basis = call(
        place_kernel,
        "place",
        (current, w01, w23, w4, w5, w6, trial, point_order),
        [shape(RHS, leaf), jax.ShapeDtypeStruct((RANK, leaf), BF16)],
        limit=32,
    )
    return call(
        last_kernel, "last", (keep, keep_far, cores, placed, basis), [shape(RHS, leaf)], level=7, at=2
    )[0]


def solution(mesh):
    in_specs = (
        P(None, "leaf"),
        P("leaf", None),
        P("leaf", None),
        P(None, None, "leaf"),
        P(None, None, "leaf"),
        P(None, "leaf", None),
    )
    out_specs = P(None, "leaf")
    return jax.shard_map(local, mesh=mesh, in_specs=in_specs, out_specs=out_specs, check_vma=False)
```

time: 897 us -> 67.3 us (0.08)
  waiting for transfers between devices: 829 us -> 21.6 us
  starting transfers between devices: 0.3 us -> 30.9 us
  matrix products: 21.2 us -> 0 us
  other arithmetic: 14.1 us -> 0 us
  between operations: 13.8 us -> 0.12 us
  local copies, waits for them, and re-layouts: 15.2 us -> 1.55 us
  Pallas kernels: 0 us -> 12.9 us
    all_gather x8 -> x0, waiting for transfers between devices: 829 us -> none  [half_sums(): gathered = lax.all_gather(projection[None], 'leaf', axis=0, tiled=True)]
    ppermute x0 -> x20, starting transfers between devices: none -> 30.9 us  [pair(): return lax.ppermute(values, 'leaf', [(d, d ^ mask) for d in range(devices)])]
    ppermute x0 -> x20, waiting for transfers between devices: none -> 21.6 us  [pair(): return lax.ppermute(values, 'leaf', [(d, d ^ mask) for d in range(devices)])]
    dot_general x25 -> x0, matrix products: 21.2 us -> none  [the longest x8 9.15 us: local(): jnp.dot(weights.astype(jnp.bfloat16), trial_bases[level], preferred_eleme...]
    pallas_call x0 -> x21, Pallas kernels: none -> 12.9 us  [the longest x1 5.16 us: local(): pl.pallas_call(leaf_kernel, in_specs=[vmem, vmem, anywhere, anywhere, any...]
    reduce_sum x7 -> x0, other arithmetic: 12.6 us -> none  [half_sums(): gathered.reshape((devices >> level, 2 ** level) + projection.shape)]
  transfers between devices with their start and end apart: 8 -> 20, of which waited for: 8 -> 12; matrix products, arithmetic and copies ran while one was open for 0% -> 0% of each run, Pallas kernels for 0% -> 7%
where the time goes in v3:
time: 67.3 us; the launch traced here: 67.1 us
  starting transfers between devices  30.9 us (46%)
  waiting for transfers between devices  21.6 us (32%)
  Pallas kernels  12.9 us (19%)
  local copies, waits for them, and re-layouts  1.55 us (2%)
    ppermute x20, starting transfers between devices, pair(): return lax.ppermute(values, 'leaf', [(d, d ^ mask) for d in range(devices)])  30.9 us
    ppermute x20, waiting for transfers between devices, pair(): return lax.ppermute(values, 'leaf', [(d, d ^ mask) for d in range(devices)])  21.6 us
    pallas_call x1, Pallas kernels, local(): pl.pallas_call(leaf_kernel, in_specs=[vmem, vmem, anywhere, anywhere, any...  5.16 us
    pallas_call x19, Pallas kernels, call(): pl.pallas_call(body, in_specs=specs, out_specs=[vmem] * len(shapes), out_...  4.94 us
    pallas_call x1, Pallas kernels, local(): pl.pallas_call(products_body, in_specs=[anywhere] * 3, out_specs=[vmem] *...  2.78 us
    unnamed x10, local copies, waits for them, and re-layouts  1.55 us
  transfers between devices with their start and end apart: 20, of which 12 were waited for; matrix products, arithmetic and copies ran while one was open for 0% of the time, Pallas kernels for 7%

profile of v3, /device:TPU:32, one launch (start us, length us, event | category | flops | bytes accessed | tf_op | source)
XLA Modules:
  0.0 67.1 jit_solution(7870046269205201381)
XLA Ops:
  0.0 0.8 %copy-done.2 = bf16[16,2048]{1,0:T(8,128)(2,1)S(1)} copy-done((bf16[16,2048]{1,0:T(8,128)(2,1)S(1)}, bf16[16,2048]{1,0:T(8,128)(2,1)}, u32[]{:S(2)}) %copy-start.2) | copy-done | bytes 65560
  0.8 0.7 %copy-done.3 = s32[1,2048]{1,0:T(1,128)S(1)} copy-done((s32[1,2048]{1,0:T(1,128)S(1)}, s32[1,2048]{1,0:T(1,128)}, u32[]{:S(2)}) %copy-start.3) | copy-done | bytes 8216
  1.5 5.2 %leaf.1 = (f32[16,2048]{1,0:T(8,128)S(1)}, f32[48,128]{1,0:T(8,128)S(1)}, f32[48,128]{1,0:T(8,128)S(1)}, f32[384,128]{1,0:T(8,128)S(1)}) custom-call(bf16[16,2048]{1,0:T(8,128)(2,1)S(1)} %copy-done.2, s32[1,2048]{1,0:T(1,128)S(1)} %copy-done.3, bf16[2048,2048]{1,0:T(8,128)(2,1)} %inv_hbm.1, bf16[512,2048]{1,0:T(8,128)(2,1)} %bitcast.5, bf16[512,2048]{1,0:T(8,128)(2,1)} %bitcast.2), custom_call_target="tpu_custom_call" | custom-call | tf_op jit(solution)/shard_map/leaf/pallas_call | solution.py:349
  6.8 1.2 %collective-permute-done.refs_1_ = f32[112,128]{1,0:T(8,128)S(1)} collective-permute-done((f32[112,128]{1,0:T(8,128)S(1)}, f32[112,128]{1,0:T(8,128)S(1)}, u32[]{:S(2)}, u32[]{:S(2)}) %collective-permute-start) | collective-permute-done | bytes 57376 | tf_op jit(solution)/shard_map/ppermute | solution.py:342
  8.4 1.9 %collective-permute-start.1 = (f32[16,128]{1,0:T(8,128)S(1)}, f32[16,128]{1,0:T(8,128)S(1)}, u32[]{:S(2)}, u32[]{:S(2)}) collective-permute-start(f32[16,128]{1,0:T(8,128)S(1)} %get-tuple-element.33.after_ref.refs_0_), channel_id=1, source_target_pairs={{0,2},{1,3},{2,0},{3,1},{4,6},{5,7},{6,4},{7,5},{8,10},{9,11},{10,... | collective-permute-start | bytes 24584 | tf_op jit(solution)/shard_map/ppermute | solution.py:342
  10.2 2.8 %products.1 = (f32[32,128]{1,0:T(8,128)S(1)}, f32[224,128]{1,0:T(8,128)S(1)}, f32[224,128]{1,0:T(8,128)S(1)}) custom-call(f32[16,128]{1,0:T(8,128)S(1)} %get-tuple-element.33.after_ref.refs_0_, bf16[512,2048]{1,0:T(8,128)(2,1)} %bitcast.6, bf16[512,2048]{1,0:T(8,128)(2,1)} %bitcast.3), custom_call_target="tpu_custom_call" | custom-call | flops 603979776 | bytes 3145728 | tf_op jit(solution)/shard_map/products/pallas_call | solution.py:381
  14.0 0.7 %collective-permute-done.2.refs_1_ = f32[80,128]{1,0:T(8,128)S(1)} collective-permute-done((f32[80,128]{1,0:T(8,128)S(1)}, f32[80,128]{1,0:T(8,128)S(1)}, u32[]{:S(2)}, u32[]{:S(2)}) %collective-permute-start.2) | collective-permute-done | bytes 40992 | tf_op jit(solution)/shard_map/ppermute | solution.py:342
  14.7 0.8 %collective-permute-start.3 = (f32[80,128]{1,0:T(8,128)S(1)}, f32[80,128]{1,0:T(8,128)S(1)}, u32[]{:S(2)}, u32[]{:S(2)}) collective-permute-start(f32[80,128]{1,0:T(8,128)S(1)} %sum0.1.refs_0_.refs_2_), channel_id=1, source_target_pairs={{0,2},{1,3},{2,0},{3,1},{4,6},{5,7},{6,4},{7,5},{8,10},{9,11},{10,... | collective-permute-start | bytes 122888 | tf_op jit(solution)/shard_map/ppermute | solution.py:342
  15.6 1.3 %collective-permute-start.7 = (f32[224,128]{1,0:T(8,128)S(1)}, f32[224,128]{1,0:T(8,128)S(1)}, u32[]{:S(2)}, u32[]{:S(2)}) collective-permute-start(f32[224,128]{1,0:T(8,128)S(1)} %late0.1.refs_0_), channel_id=1, source_target_pairs={{0,2},{1,3},{2,0},{3,1},{4,6},{5,7},{6,4},{7,5},{8,10},{9,11},{10,... | collective-permute-start | bytes 344072 | tf_op jit(solution)/shard_map/ppermute | solution.py:342
  16.9 2.3 %collective-permute-done.3.refs_1_ = f32[80,128]{1,0:T(8,128)S(1)} collective-permute-done((f32[80,128]{1,0:T(8,128)S(1)}, f32[80,128]{1,0:T(8,128)S(1)}, u32[]{:S(2)}, u32[]{:S(2)}) %collective-permute-start.3) | collective-permute-done | bytes 40992 | tf_op jit(solution)/shard_map/ppermute | solution.py:342
  19.2 2.2 %collective-permute-start.4 = (f32[112,128]{1,0:T(8,128)S(1)}, f32[112,128]{1,0:T(8,128)S(1)}, u32[]{:S(2)}, u32[]{:S(2)}) collective-permute-start(f32[112,128]{1,0:T(8,128)S(1)} %get-tuple-element.39.refs_0_), channel_id=1, source_target_pairs={{0,4},{1,5},{2,6},{3,7},{4,0},{5,1},{6,2},{7,3},{8,12},{9,13},{10,... | collective-permute-start | bytes 172040 | tf_op jit(solution)/shard_map/ppermute | solution.py:342
  21.5 2.9 %collective-permute-done.4.refs_1_ = f32[112,128]{1,0:T(8,128)S(1)} collective-permute-done((f32[112,128]{1,0:T(8,128)S(1)}, f32[112,128]{1,0:T(8,128)S(1)}, u32[]{:S(2)}, u32[]{:S(2)}) %collective-permute-start.4) | collective-permute-done | bytes 57376 | tf_op jit(solution)/shard_map/ppermute | solution.py:342
  24.7 5.2 %collective-permute-start.5 = (f32[16,128]{1,0:T(8,128)S(1)}, f32[16,128]{1,0:T(8,128)S(1)}, u32[]{:S(2)}, u32[]{:S(2)}) collective-permute-start(f32[16,128]{1,0:T(8,128)S(1)} %get-tuple-element.40.refs_0_), channel_id=1, source_target_pairs={{0,12},{1,13},{2,14},{3,15},{4,8},{5,9},{6,10},{7,11},{8,4},{9,5},... | collective-permute-start | bytes 24584 | tf_op jit(solution)/shard_map/ppermute | solution.py:342
  29.8 1.0 %collective-permute-start.12 = (f32[96,128]{1,0:T(8,128)S(1)}, f32[96,128]{1,0:T(8,128)S(1)}, u32[]{:S(2)}, u32[]{:S(2)}) collective-permute-start(f32[96,128]{1,0:T(8,128)S(1)} %get-tuple-element.48.refs_0_), channel_id=1, source_target_pairs={{0,4},{1,5},{2,6},{3,7},{4,0},{5,1},{6,2},{7,3},{8,12},{9,13},{10,... | collective-permute-start | bytes 147464 | tf_op jit(solution)/shard_map/ppermute | solution.py:342
  30.8 0.7 %collective-permute-done.5.refs_1_.refs_2_ = f32[16,128]{1,0:T(8,128)S(1)} collective-permute-done((f32[16,128]{1,0:T(8,128)S(1)}, f32[16,128]{1,0:T(8,128)S(1)}, u32[]{:S(2)}, u32[]{:S(2)}) %collective-permute-start.5) | collective-permute-done | bytes 8224 | tf_op jit(solution)/shard_map/ppermute | solution.py:342
  31.9 1.3 %collective-permute-start.9 = (f32[32,128]{1,0:T(8,128)S(1)}, f32[32,128]{1,0:T(8,128)S(1)}, u32[]{:S(2)}, u32[]{:S(2)}) collective-permute-start(f32[32,128]{1,0:T(8,128)S(1)} %get-tuple-element.47.refs_0_), channel_id=1, source_target_pairs={{0,4},{1,5},{2,6},{3,7},{4,0},{5,1},{6,2},{7,3},{8,12},{9,13},{10,... | collective-permute-start | bytes 49160 | tf_op jit(solution)/shard_map/ppermute | solution.py:342
  33.2 1.6 %collective-permute-done.12.refs_1_ = f32[96,128]{1,0:T(8,128)S(1)} collective-permute-done((f32[96,128]{1,0:T(8,128)S(1)}, f32[96,128]{1,0:T(8,128)S(1)}, u32[]{:S(2)}, u32[]{:S(2)}) %collective-permute-start.12) | collective-permute-done | bytes 49184 | tf_op jit(solution)/shard_map/ppermute | solution.py:342
  34.8 2.2 %collective-permute-start.13 = (f32[96,128]{1,0:T(8,128)S(1)}, f32[96,128]{1,0:T(8,128)S(1)}, u32[]{:S(2)}, u32[]{:S(2)}) collective-permute-start(f32[96,128]{1,0:T(8,128)S(1)} %late2.1.refs_0_), channel_id=1, source_target_pairs={{0,12},{1,13},{2,14},{3,15},{4,8},{5,9},{6,10},{7,11},{8,4},{9,5},... | collective-permute-start | bytes 147464 | tf_op jit(solution)/shard_map/ppermute | solution.py:342
  37.1 3.7 %collective-permute-start.10 = (f32[32,128]{1,0:T(8,128)S(1)}, f32[32,128]{1,0:T(8,128)S(1)}, u32[]{:S(2)}, u32[]{:S(2)}) collective-permute-start(f32[32,128]{1,0:T(8,128)S(1)} %sum2.1.refs_0_.refs_3_), channel_id=1, source_target_pairs={{0,12},{1,13},{2,14},{3,15},{4,8},{5,9},{6,10},{7,11},{8,4},{9,5},... | collective-permute-start | bytes 49160 | tf_op jit(solution)/shard_map/ppermute | solution.py:342
  40.8 0.8 %collective-permute-done.13.refs_1_ = f32[96,128]{1,0:T(8,128)S(1)} collective-permute-done((f32[96,128]{1,0:T(8,128)S(1)}, f32[96,128]{1,0:T(8,128)S(1)}, u32[]{:S(2)}, u32[]{:S(2)}) %collective-permute-start.13) | collective-permute-done | bytes 49184 | tf_op jit(solution)/shard_map/ppermute | solution.py:342
  41.6 1.6 %collective-permute-start.15 = (f32[160,128]{1,0:T(8,128)S(1)}, f32[160,128]{1,0:T(8,128)S(1)}, u32[]{:S(2)}, u32[]{:S(2)}) collective-permute-start(f32[160,128]{1,0:T(8,128)S(1)} %late3.1.refs_2_), channel_id=1, source_target_pairs={{0,16},{1,17},{2,18},{3,19},{4,20},{5,21},{6,22},{7,23},{8,24},{9,... | collective-permute-start | bytes 245768 | tf_op jit(solution)/shard_map/ppermute | solution.py:342
  43.3 2.9 %collective-permute-done.15.refs_0_.refs_4_ = f32[160,128]{1,0:T(8,128)S(1)} collective-permute-done((f32[160,128]{1,0:T(8,128)S(1)}, f32[160,128]{1,0:T(8,128)S(1)}, u32[]{:S(2)}, u32[]{:S(2)}) %collective-permute-start.15) | collective-permute-done | bytes 81952 | tf_op jit(solution)/shard_map/ppermute | solution.py:342
  46.1 1.8 %collective-permute-start.11 = (f32[32,128]{1,0:T(8,128)S(1)}, f32[32,128]{1,0:T(8,128)S(1)}, u32[]{:S(2)}, u32[]{:S(2)}) collective-permute-start(f32[32,128]{1,0:T(8,128)S(1)} %sum3.1.refs_1_.refs_0_), channel_id=1, source_target_pairs={{0,16},{1,17},{2,18},{3,19},{4,20},{5,21},{6,22},{7,23},{8,24},{9,... | collective-permute-start | bytes 49160 | tf_op jit(solution)/shard_map/ppermute | solution.py:342
  48.0 2.2 %collective-permute-done.11.refs_1_ = f32[32,128]{1,0:T(8,128)S(1)} collective-permute-done((f32[32,128]{1,0:T(8,128)S(1)}, f32[32,128]{1,0:T(8,128)S(1)}, u32[]{:S(2)}, u32[]{:S(2)}) %collective-permute-start.11) | collective-permute-done | bytes 16416 | tf_op jit(solution)/shard_map/ppermute | solution.py:342
  50.5 3.0 %collective-permute-start.17 = (f32[192,128]{1,0:T(8,128)S(1)}, f32[192,128]{1,0:T(8,128)S(1)}, u32[]{:S(2)}, u32[]{:S(2)}) collective-permute-start(f32[192,128]{1,0:T(8,128)S(1)} %get-tuple-element.49.refs_0_), channel_id=1, source_target_pairs={{0,48},{1,49},{2,50},{3,51},{4,52},{5,53},{6,54},{7,55},{8,56},{9,... | collective-permute-start | bytes 294920 | tf_op jit(solution)/shard_map/ppermute | solution.py:342
  53.5 2.8 %collective-permute-done.17.refs_1_ = f32[192,128]{1,0:T(8,128)S(1)} collective-permute-done((f32[192,128]{1,0:T(8,128)S(1)}, f32[192,128]{1,0:T(8,128)S(1)}, u32[]{:S(2)}, u32[]{:S(2)}) %collective-permute-start.17) | collective-permute-done | bytes 98336 | tf_op jit(solution)/shard_map/ppermute | solution.py:342
  56.7 1.5 %collective-permute-start.18 = (f32[112,128]{1,0:T(8,128)S(1)}, f32[112,128]{1,0:T(8,128)S(1)}, u32[]{:S(2)}, u32[]{:S(2)}) collective-permute-start(f32[112,128]{1,0:T(8,128)S(1)} %get-tuple-element.50.refs_0_), channel_id=1, source_target_pairs={{0,64},{1,65},{2,66},{3,67},{4,68},{5,69},{6,70},{7,71},{8,72},{9,... | collective-permute-start | bytes 172040 | tf_op jit(solution)/shard_map/ppermute | solution.py:342
  58.2 2.7 %collective-permute-done.18.refs_1_ = f32[112,128]{1,0:T(8,128)S(1)} collective-permute-done((f32[112,128]{1,0:T(8,128)S(1)}, f32[112,128]{1,0:T(8,128)S(1)}, u32[]{:S(2)}, u32[]{:S(2)}) %collective-permute-start.18) | collective-permute-done | bytes 57376 | tf_op jit(solution)/shard_map/ppermute | solution.py:342
  61.2 2.8 %collective-permute-start.19 = (f32[16,128]{1,0:T(8,128)S(1)}, f32[16,128]{1,0:T(8,128)S(1)}, u32[]{:S(2)}, u32[]{:S(2)}) collective-permute-start(f32[16,128]{1,0:T(8,128)S(1)} %get-tuple-element.51.refs_0_), channel_id=1, source_target_pairs={{0,192},{1,193},{2,194},{3,195},{4,196},{5,197},{6,198},{7,199},{8... | collective-permute-start | bytes 24584 | tf_op jit(solution)/shard_map/ppermute | solution.py:342
  64.0 1.4 %place.1 = (f32[16,2048]{1,0:T(8,128)S(1)}, bf16[64,2048]{1,0:T(8,128)(2,1)S(1)}) custom-call(f32[16,2048]{1,0:T(8,128)S(1)} %get-tuple-element.52.refs_0_, f32[16,128]{1,0:T(8,128)S(1)} %get-tuple-element.45.refs_2_.refs_1_, f32[16,128]{1,0:T(8,128)S(1)} %get-tuple-element.53.refs_2_, f32[16,128]{1,0:T(8,128)S(1)} %get-tuple-element.54.refs_3_, ...), custom_call_target="tpu_custom_call" | custom-call | tf_op jit(solution)/shard_map/place/pallas_call | solution.py:327
  65.3 0.8 %collective-permute-done.19.refs_1_ = f32[16,128]{1,0:T(8,128)S(1)} collective-permute-done((f32[16,128]{1,0:T(8,128)S(1)}, f32[16,128]{1,0:T(8,128)S(1)}, u32[]{:S(2)}, u32[]{:S(2)}) %collective-permute-start.19) | collective-permute-done | bytes 8224 | tf_op jit(solution)/shard_map/ppermute | solution.py:342
  66.1 1.0 %last.1 = f32[16,2048]{1,0:T(8,128)} custom-call(f32[16,128]{1,0:T(8,128)S(1)} %get-tuple-element.51.refs_0_, f32[16,128]{1,0:T(8,128)S(1)} %collective-permute-done.19.refs_1_, bf16[8,64,128]{2,1,0:T(8,128)(2,1)S(1)} %copy-done.1, f32[16,2048]{1,0:T(8,128)S(1)} %get-tuple-element.57.refs_3_, bf16[64,2048]{1,0:T(8,128)(2,1)S(1)} %get-tuple-element.58.refs_4_), custom_call_target="tpu_custom_call" | custom-call | tf_op jit(solution)/shard_map/last/pallas_call | solution.py:327
  (39 shorter events, 3.3 us)
Async XLA Ops:
  0.0 0.8 %copy-start.2 = (bf16[16,2048]{1,0:T(8,128)(2,1)S(1)}, bf16[16,2048]{1,0:T(8,128)(2,1)}, u32[]{:S(2)}) copy-start(bf16[16,2048]{1,0:T(8,128)(2,1)} %rs_ref.1) | copy-start | bytes 196612
  0.8 0.7 %copy-start.3 = (s32[1,2048]{1,0:T(1,128)S(1)}, s32[1,2048]{1,0:T(1,128)}, u32[]{:S(2)}) copy-start(s32[1,2048]{1,0:T(1,128)} %refs_7_.1) | copy-start | bytes 24580
  1.5 5.2 %copy-start.1 = (bf16[8,64,128]{2,1,0:T(8,128)(2,1)S(1)}, bf16[8,64,128]{2,1,0:T(8,128)(2,1)}, u32[]{:S(2)}) copy-start(bf16[8,64,128]{2,1,0:T(8,128)(2,1)} %refs_2_.11) | copy-start | bytes 393220
  6.7 1.3 %collective-permute-start = (f32[112,128]{1,0:T(8,128)S(1)}, f32[112,128]{1,0:T(8,128)S(1)}, u32[]{:S(2)}, u32[]{:S(2)}) collective-permute-start(f32[112,128]{1,0:T(8,128)S(1)} %first.1.refs_0_), channel_id=1, source_target_pairs={{0,1},{1,0},{2,3},{3,2},{4,5},{5,4},{6,7},{7,6},{8,9},{9,8},{10,11... | collective-permute-start | bytes 172040 | tf_op jit(solution)/shard_map/ppermute | solution.py:342
  8.4 4.6 %collective-permute-start.1 = (f32[16,128]{1,0:T(8,128)S(1)}, f32[16,128]{1,0:T(8,128)S(1)}, u32[]{:S(2)}, u32[]{:S(2)}) collective-permute-start(f32[16,128]{1,0:T(8,128)S(1)} %get-tuple-element.33.after_ref.refs_0_), channel_id=1, source_target_pairs={{0,2},{1,3},{2,0},{3,1},{4,6},{5,7},{6,4},{7,5},{8,10},{9,11},{10,... | collective-permute-start | bytes 24584 | tf_op jit(solution)/shard_map/ppermute | solution.py:342
  13.5 1.2 %collective-permute-start.2 = (f32[80,128]{1,0:T(8,128)S(1)}, f32[80,128]{1,0:T(8,128)S(1)}, u32[]{:S(2)}, u32[]{:S(2)}) collective-permute-start(f32[80,128]{1,0:T(8,128)S(1)} %get-tuple-element.38.refs_0_), channel_id=1, source_target_pairs={{0,1},{1,0},{2,3},{3,2},{4,5},{5,4},{6,7},{7,6},{8,9},{9,8},{10,11... | collective-permute-start | bytes 122888 | tf_op jit(solution)/shard_map/ppermute | solution.py:342
  13.5 2.1 %collective-permute-start.6 = (f32[224,128]{1,0:T(8,128)S(1)}, f32[224,128]{1,0:T(8,128)S(1)}, u32[]{:S(2)}, u32[]{:S(2)}) collective-permute-start(f32[224,128]{1,0:T(8,128)S(1)} %get-tuple-element.44), channel_id=1, source_target_pairs={{0,1},{1,0},{2,3},{3,2},{4,5},{5,4},{6,7},{7,6},{8,9},{9,8},{10,11... | collective-permute-start | bytes 344072 | tf_op jit(solution)/shard_map/ppermute | solution.py:342
  14.7 4.4 %collective-permute-start.3 = (f32[80,128]{1,0:T(8,128)S(1)}, f32[80,128]{1,0:T(8,128)S(1)}, u32[]{:S(2)}, u32[]{:S(2)}) collective-permute-start(f32[80,128]{1,0:T(8,128)S(1)} %sum0.1.refs_0_.refs_2_), channel_id=1, source_target_pairs={{0,2},{1,3},{2,0},{3,1},{4,6},{5,7},{6,4},{7,5},{8,10},{9,11},{10,... | collective-permute-start | bytes 122888 | tf_op jit(solution)/shard_map/ppermute | solution.py:342
  15.6 5.7 %collective-permute-start.7 = (f32[224,128]{1,0:T(8,128)S(1)}, f32[224,128]{1,0:T(8,128)S(1)}, u32[]{:S(2)}, u32[]{:S(2)}) collective-permute-start(f32[224,128]{1,0:T(8,128)S(1)} %late0.1.refs_0_), channel_id=1, source_target_pairs={{0,2},{1,3},{2,0},{3,1},{4,6},{5,7},{6,4},{7,5},{8,10},{9,11},{10,... | collective-permute-start | bytes 344072 | tf_op jit(solution)/shard_map/ppermute | solution.py:342
  19.2 5.2 %collective-permute-start.4 = (f32[112,128]{1,0:T(8,128)S(1)}, f32[112,128]{1,0:T(8,128)S(1)}, u32[]{:S(2)}, u32[]{:S(2)}) collective-permute-start(f32[112,128]{1,0:T(8,128)S(1)} %get-tuple-element.39.refs_0_), channel_id=1, source_target_pairs={{0,4},{1,5},{2,6},{3,7},{4,0},{5,1},{6,2},{7,3},{8,12},{9,13},{10,... | collective-permute-start | bytes 172040 | tf_op jit(solution)/shard_map/ppermute | solution.py:342
  21.4 10.1 %collective-permute-start.8 = (f32[128,128]{1,0:T(8,128)S(1)}, f32[128,128]{1,0:T(8,128)S(1)}, u32[]{:S(2)}, u32[]{:S(2)}) collective-permute-start(f32[128,128]{1,0:T(8,128)S(1)} %get-tuple-element.46.refs_5_), channel_id=1, source_target_pairs={{0,1},{1,0},{2,3},{3,2},{4,5},{5,4},{6,7},{7,6},{8,9},{9,8},{10,11... | collective-permute-start | bytes 196616 | tf_op jit(solution)/shard_map/ppermute | solution.py:342
  24.7 6.8 %collective-permute-start.5 = (f32[16,128]{1,0:T(8,128)S(1)}, f32[16,128]{1,0:T(8,128)S(1)}, u32[]{:S(2)}, u32[]{:S(2)}) collective-permute-start(f32[16,128]{1,0:T(8,128)S(1)} %get-tuple-element.40.refs_0_), channel_id=1, source_target_pairs={{0,12},{1,13},{2,14},{3,15},{4,8},{5,9},{6,10},{7,11},{8,4},{9,5},... | collective-permute-start | bytes 24584 | tf_op jit(solution)/shard_map/ppermute | solution.py:342
  29.8 5.0 %collective-permute-start.12 = (f32[96,128]{1,0:T(8,128)S(1)}, f32[96,128]{1,0:T(8,128)S(1)}, u32[]{:S(2)}, u32[]{:S(2)}) collective-permute-start(f32[96,128]{1,0:T(8,128)S(1)} %get-tuple-element.48.refs_0_), channel_id=1, source_target_pairs={{0,4},{1,5},{2,6},{3,7},{4,0},{5,1},{6,2},{7,3},{8,12},{9,13},{10,... | collective-permute-start | bytes 147464 | tf_op jit(solution)/shard_map/ppermute | solution.py:342
  31.9 5.1 %collective-permute-start.9 = (f32[32,128]{1,0:T(8,128)S(1)}, f32[32,128]{1,0:T(8,128)S(1)}, u32[]{:S(2)}, u32[]{:S(2)}) collective-permute-start(f32[32,128]{1,0:T(8,128)S(1)} %get-tuple-element.47.refs_0_), channel_id=1, source_target_pairs={{0,4},{1,5},{2,6},{3,7},{4,0},{5,1},{6,2},{7,3},{8,12},{9,13},{10,... | collective-permute-start | bytes 49160 | tf_op jit(solution)/shard_map/ppermute | solution.py:342
  34.8 6.8 %collective-permute-start.13 = (f32[96,128]{1,0:T(8,128)S(1)}, f32[96,128]{1,0:T(8,128)S(1)}, u32[]{:S(2)}, u32[]{:S(2)}) collective-permute-start(f32[96,128]{1,0:T(8,128)S(1)} %late2.1.refs_0_), channel_id=1, source_target_pairs={{0,12},{1,13},{2,14},{3,15},{4,8},{5,9},{6,10},{7,11},{8,4},{9,5},... | collective-permute-start | bytes 147464 | tf_op jit(solution)/shard_map/ppermute | solution.py:342
  37.1 6.2 %collective-permute-start.10 = (f32[32,128]{1,0:T(8,128)S(1)}, f32[32,128]{1,0:T(8,128)S(1)}, u32[]{:S(2)}, u32[]{:S(2)}) collective-permute-start(f32[32,128]{1,0:T(8,128)S(1)} %sum2.1.refs_0_.refs_3_), channel_id=1, source_target_pairs={{0,12},{1,13},{2,14},{3,15},{4,8},{5,9},{6,10},{7,11},{8,4},{9,5},... | collective-permute-start | bytes 49160 | tf_op jit(solution)/shard_map/ppermute | solution.py:342
  41.6 4.5 %collective-permute-start.15 = (f32[160,128]{1,0:T(8,128)S(1)}, f32[160,128]{1,0:T(8,128)S(1)}, u32[]{:S(2)}, u32[]{:S(2)}) collective-permute-start(f32[160,128]{1,0:T(8,128)S(1)} %late3.1.refs_2_), channel_id=1, source_target_pairs={{0,16},{1,17},{2,18},{3,19},{4,20},{5,21},{6,22},{7,23},{8,24},{9,... | collective-permute-start | bytes 245768 | tf_op jit(solution)/shard_map/ppermute | solution.py:342
  43.2 6.9 %collective-permute-start.14 = (f32[160,128]{1,0:T(8,128)S(1)}, f32[160,128]{1,0:T(8,128)S(1)}, u32[]{:S(2)}, u32[]{:S(2)}) collective-permute-start(f32[160,128]{1,0:T(8,128)S(1)} %late3.1.refs_2_), channel_id=1, source_target_pairs={{0,1},{1,0},{2,3},{3,2},{4,5},{5,4},{6,7},{7,6},{8,9},{9,8},{10,11... | collective-permute-start | bytes 245768 | tf_op jit(solution)/shard_map/ppermute | solution.py:342
  46.1 4.0 %collective-permute-start.16 = (f32[160,128]{1,0:T(8,128)S(1)}, f32[160,128]{1,0:T(8,128)S(1)}, u32[]{:S(2)}, u32[]{:S(2)}) collective-permute-start(f32[160,128]{1,0:T(8,128)S(1)} %late4.1), channel_id=1, source_target_pairs={{0,1},{1,0},{2,3},{3,2},{4,5},{5,4},{6,7},{7,6},{8,9},{9,8},{10,11... | collective-permute-start | bytes 245768 | tf_op jit(solution)/shard_map/ppermute | solution.py:342
  46.1 4.0 %collective-permute-start.11 = (f32[32,128]{1,0:T(8,128)S(1)}, f32[32,128]{1,0:T(8,128)S(1)}, u32[]{:S(2)}, u32[]{:S(2)}) collective-permute-start(f32[32,128]{1,0:T(8,128)S(1)} %sum3.1.refs_1_.refs_0_), channel_id=1, source_target_pairs={{0,16},{1,17},{2,18},{3,19},{4,20},{5,21},{6,22},{7,23},{8,24},{9,... | collective-permute-start | bytes 49160 | tf_op jit(solution)/shard_map/ppermute | solution.py:342
  50.5 5.9 %collective-permute-start.17 = (f32[192,128]{1,0:T(8,128)S(1)}, f32[192,128]{1,0:T(8,128)S(1)}, u32[]{:S(2)}, u32[]{:S(2)}) collective-permute-start(f32[192,128]{1,0:T(8,128)S(1)} %get-tuple-element.49.refs_0_), channel_id=1, source_target_pairs={{0,48},{1,49},{2,50},{3,51},{4,52},{5,53},{6,54},{7,55},{8,56},{9,... | collective-permute-start | bytes 294920 | tf_op jit(solution)/shard_map/ppermute | solution.py:342
  56.7 7.3 %copy-start = (bf16[8,64,2048]{2,1,0:T(8,128)(2,1)S(1)}, bf16[8,64,2048]{2,1,0:T(8,128)(2,1)}, u32[]{:S(2)}) copy-start(bf16[8,64,2048]{2,1,0:T(8,128)(2,1)} %param.10) | copy-start | bytes 6291460
  56.7 7.3 %copy-start.4 = (s32[1,2048]{1,0:T(1,128)S(1)}, s32[1,2048]{1,0:T(1,128)}, u32[]{:S(2)}) copy-start(s32[1,2048]{1,0:T(1,128)} %refs_7_.1) | copy-start | bytes 24580
  56.7 4.2 %collective-permute-start.18 = (f32[112,128]{1,0:T(8,128)S(1)}, f32[112,128]{1,0:T(8,128)S(1)}, u32[]{:S(2)}, u32[]{:S(2)}) collective-permute-start(f32[112,128]{1,0:T(8,128)S(1)} %get-tuple-element.50.refs_0_), channel_id=1, source_target_pairs={{0,64},{1,65},{2,66},{3,67},{4,68},{5,69},{6,70},{7,71},{8,72},{9,... | collective-permute-start | bytes 172040 | tf_op jit(solution)/shard_map/ppermute | solution.py:342
  61.2 4.9 %collective-permute-start.19 = (f32[16,128]{1,0:T(8,128)S(1)}, f32[16,128]{1,0:T(8,128)S(1)}, u32[]{:S(2)}, u32[]{:S(2)}) collective-permute-start(f32[16,128]{1,0:T(8,128)S(1)} %get-tuple-element.51.refs_0_), channel_id=1, source_target_pairs={{0,192},{1,193},{2,194},{3,195},{4,196},{5,197},{6,198},{7,199},{8... | collective-permute-start | bytes 24584 | tf_op jit(solution)/shard_map/ppermute | solution.py:342

commit v4 on v3

--- a/solution.py
+++ b/solution.py
@@ -100,6 +100,10 @@
 def unpack(rows):
     both = jnp.concatenate([swap(rows), rows], axis=0)
     return jnp.where(lanes(RANK) < RANK, 0.0, both)
+
+
+def ready_kernel(out_ref):
+    out_ref[...] = jnp.zeros_like(out_ref)
 
 
 def leaf_kernel(
@@ -337,8 +341,8 @@
 
     main = functools.partial(call, hint=int(6e9))
 
-    def pair(values, k):
-        mask = {3: 3 << 2, 5: 3 << 4, 7: 3 << 6}.get(k, 1 << k)
+    def pair(values, k, across=0):
+        mask = {3: 3 << 2, 5: 3 << 4, 7: 3 << 6}.get(k, 1 << k) ^ across
         return lax.ppermute(values, "leaf", [(d, d ^ mask) for d in range(devices)])
 
     cores = coupling_cores
@@ -346,9 +350,14 @@
     late_rows = LANES + tail
     later_rows = (PAIRS - 1) * RHS
     big = pltpu.CompilerParams(vmem_limit_bytes=52 * 2**20)
+    (ready,) = main(ready_kernel, "ready", (), [shape(8, LANES)])
+
+    def leaf_body(after_ref, *refs):
+        leaf_kernel(*refs)
+
     current, pay, rest, near = pl.pallas_call(
-        leaf_kernel,
-        in_specs=[vmem, vmem, anywhere, anywhere, anywhere],
+        leaf_body,
+        in_specs=[anywhere, vmem, vmem, anywhere, anywhere, anywhere],
         out_specs=[vmem] * 4,
         out_shape=[
             shape(RHS, leaf),
@@ -366,14 +375,14 @@
         ],
         compiler_params=big,
         name="leaf",
-    )(right_sides, point_order, leaf_inverse, test, trial)
+    )(ready, right_sides, point_order, leaf_inverse, test, trial)
 
     one = shape(RHS, LANES)
     two = shape(2 * RHS, LANES)
 
     (pay,) = call(first_kernel, "first", (pay, cores), [shape(PAY + RANK, LANES)], 0, 1)
     w0, half = main(level0_kernel, "level0", (pay, pair(pay, 0)), [one, one])
-    half_far = pair(half, 1)
+    half_far = pair(half, 1, 1)
 
     def products_body(after_ref, *refs):
         products_kernel(*refs)
@@ -406,27 +415,27 @@
     (late,) = call(add_kernel, "late0", (late, late_far), [shape(late_rows, LANES)], after=(w01,))
     late_far = pair(late, 1)
     (rest,) = main(add_kernel, "sum0", (rest, rest_far), [shape(later_rows + RANK // 2, LANES)])
-    rest_far = pair(rest, 1)
+    rest_far = pair(rest, 1, 1)
     pay, keep = main(node_kernel, "node", (rest, rest_far, cores), [shape(PAY + RANK, LANES), two], 2, 2)
-    pay_far = pair(pay, 2)
+    pay_far = pair(pay, 2, 1)
     near, prod = call(take_kernel, "late1", (late, late_far), [shape(LANES, LANES), shape(tail, LANES)], after=(rest,))
     near_far = pair(near, 0)
     prod_far = pair(prod, 2)
     w2, half = main(level2_kernel, "level2", (pay, pay_far), [one, one])
-    half_far = pair(half, 3)
-    (prod,) = call(add_kernel, "late2", (prod, prod_far), [shape(tail, LANES)], after=(half_far,))
+    half_far = pair(half, 3, 1)
+    (prod,) = call(add_kernel, "late2", (prod, prod_far), [shape(tail, LANES)], after=(pay_far,))
     prod_far = pair(prod, 3)
     w23, keep = main(
-        level3_kernel, "level3", (half, half_far, cores, w2, keep, near, near_far), [one, two], 3, 2
+        level3_kernel, "level3", (half, half_far, cores, w2, keep, near, near_far), [one, two], 3, 2, (prod,)
     )
-    keep_far = pair(keep, 2)
-    (keep,) = main(add_kernel, "sum2", (keep, keep_far), [two])
-    keep_far = pair(keep, 3)
-    (prod,) = call(add_core_kernel, "late3", (prod, prod_far, cores), [shape(tail + RANK, LANES)], 4, 2, (keep,))
+    keep_far = pair(keep, 2, 1)
+    (prod,) = call(add_core_kernel, "late3", (prod, prod_far, cores), [shape(tail + RANK, LANES)], 4, 2, (half_far,))
     prod_near, far_prod = pair(prod, 0), pair(prod, 4)
-    (keep,) = main(add_kernel, "sum3", (keep, keep_far), [two])
-    keep_far = pair(keep, 4)
-    (far_copy,) = call(copy_kernel, "late4", (far_prod,), [shape(*far_prod.shape)], after=(keep,))
+    (keep,) = main(add_kernel, "sum2", (keep, keep_far), [two], after=(prod,))
+    keep_far = pair(keep, 3, 1)
+    (far_copy,) = call(copy_kernel, "late4", (far_prod,), [shape(*far_prod.shape)], after=(w23,))
+    (keep,) = main(add_kernel, "sum3", (keep, keep_far), [two], after=(far_copy,))
+    keep_far = pair(keep, 4, 1)
     w4, keep = main(
         level4_kernel,
         "level4",
@@ -435,9 +444,9 @@
         5,
         6,
     )
-    w5, keep = main(level5_kernel, "level5", (keep, pair(keep, 5), cores), [one, shape(PAY + RANK, LANES)], 6, 2)
-    w6, keep = main(level6_kernel, "level6", (keep, pair(keep, 6)), [one, one])
-    keep_far = pair(keep, 7)
+    w5, keep = main(level5_kernel, "level5", (keep, pair(keep, 5, 1), cores), [one, shape(PAY + RANK, LANES)], 6, 2)
+    w6, keep = main(level6_kernel, "level6", (keep, pair(keep, 6, 1)), [one, one])
+    keep_far = pair(keep, 7, 1)
     placed, basis = call(
         place_kernel,
         "place",

time: 67.3 us -> 62.2 us (0.924)
  starting transfers between devices: 30.9 us -> 24.3 us
  waiting for transfers between devices: 21.6 us -> 23.7 us
  local copies, waits for them, and re-layouts: 1.55 us -> 0.86 us
    ppermute x20, starting transfers between devices: 30.9 us -> 24.3 us  [pair(): return lax.ppermute(values, 'leaf', [(d, d ^ mask) for d in range(devices)])]
    ppermute x20, waiting for transfers between devices: 21.6 us -> 23.7 us  [pair(): return lax.ppermute(values, 'leaf', [(d, d ^ mask) for d in range(devices)])]
    unnamed x10 -> x8, local copies, waits for them, and re-layouts: 1.55 us -> 0.86 us
    pallas_call x19 -> x20, Pallas kernels: 4.94 us -> 4.94 us  [call(): pl.pallas_call(body, in_specs=specs, out_specs=[vmem] * len(shapes), out_...]
  transfers between devices with their start and end apart: 20 -> 20, of which waited for: 12 -> 13; matrix products, arithmetic and copies ran while one was open for 0% -> 0% of each run, Pallas kernels for 7% -> 8%
where the time goes in v4:
time: 62.2 us; the launch traced here: 61.8 us
  starting transfers between devices  24.3 us (39%)
  waiting for transfers between devices  23.7 us (38%)
  Pallas kernels  12.9 us (21%)
  local copies, waits for them, and re-layouts  0.86 us (1%)
    ppermute x20, starting transfers between devices, pair(): return lax.ppermute(values, 'leaf', [(d, d ^ mask) for d in range(devices)])  24.3 us
    ppermute x20, waiting for transfers between devices, pair(): return lax.ppermute(values, 'leaf', [(d, d ^ mask) for d in range(devices)])  23.7 us
    pallas_call x1, Pallas kernels, local(): pl.pallas_call(leaf_body, in_specs=[anywhere, vmem, vmem, anywhere, anywh...  5.16 us
    pallas_call x20, Pallas kernels, call(): pl.pallas_call(body, in_specs=specs, out_specs=[vmem] * len(shapes), out_...  4.94 us
    pallas_call x1, Pallas kernels, local(): pl.pallas_call(products_body, in_specs=[anywhere] * 3, out_specs=[vmem] *...  2.78 us
  transfers between devices with their start and end apart: 20, of which 13 were waited for; matrix products, arithmetic and copies ran while one was open for 0% of the time, Pallas kernels for 8%

profile of v4, /device:TPU:32, one launch (start us, length us, event | category | flops | bytes accessed | tf_op | source)
XLA Modules:
  0.0 61.8 jit_solution(15341128275620117593)
XLA Ops:
  0.0 0.7 %copy-done.3 = s32[1,2048]{1,0:T(1,128)S(1)} copy-done((s32[1,2048]{1,0:T(1,128)S(1)}, s32[1,2048]{1,0:T(1,128)}, u32[]{:S(2)}) %copy-start.3) | copy-done | bytes 8216
  0.9 5.2 %leaf.1 = (f32[16,2048]{1,0:T(8,128)S(1)}, f32[48,128]{1,0:T(8,128)S(1)}, f32[48,128]{1,0:T(8,128)S(1)}, f32[384,128]{1,0:T(8,128)S(1)}) custom-call(f32[8,128]{1,0:T(8,128)S(1)} %ready.1.after_ref, bf16[16,2048]{1,0:T(8,128)(2,1)S(1)} %copy-done.2, s32[1,2048]{1,0:T(1,128)S(1)} %copy-done.3, bf16[2048,2048]{1,0:T(8,128)(2,1)} %refs_2_.7, ...), custom_call_target="tpu_custom_call" | custom-call | tf_op jit(solution)/shard_map/leaf/pallas_call | solution.py:358
  6.2 1.2 %collective-permute-done.refs_1_ = f32[112,128]{1,0:T(8,128)S(1)} collective-permute-done((f32[112,128]{1,0:T(8,128)S(1)}, f32[112,128]{1,0:T(8,128)S(1)}, u32[]{:S(2)}, u32[]{:S(2)}) %collective-permute-start) | collective-permute-done | bytes 57376 | tf_op jit(solution)/shard_map/ppermute | solution.py:346
  7.7 1.6 %collective-permute-start.1 = (f32[16,128]{1,0:T(8,128)S(1)}, f32[16,128]{1,0:T(8,128)S(1)}, u32[]{:S(2)}, u32[]{:S(2)}) collective-permute-start(f32[16,128]{1,0:T(8,128)S(1)} %get-tuple-element.33.after_ref.refs_0_), channel_id=1, source_target_pairs={{0,3},{1,2},{2,1},{3,0},{4,7},{5,6},{6,5},{7,4},{8,11},{9,10},{10,... | collective-permute-start | bytes 24584 | tf_op jit(solution)/shard_map/ppermute | solution.py:346
  9.3 2.8 %products.1 = (f32[32,128]{1,0:T(8,128)S(1)}, f32[224,128]{1,0:T(8,128)S(1)}, f32[224,128]{1,0:T(8,128)S(1)}) custom-call(f32[16,128]{1,0:T(8,128)S(1)} %get-tuple-element.33.after_ref.refs_0_, bf16[512,2048]{1,0:T(8,128)(2,1)} %bitcast.6, bf16[512,2048]{1,0:T(8,128)(2,1)} %bitcast.3), custom_call_target="tpu_custom_call" | custom-call | flops 603979776 | bytes 3145728 | tf_op jit(solution)/shard_map/products/pallas_call | solution.py:390
  12.1 0.4 level1.1
  12.6 0.4 collective-permute-start.2
  13.1 0.7 %collective-permute-done.2.refs_1_ = f32[80,128]{1,0:T(8,128)S(1)} collective-permute-done((f32[80,128]{1,0:T(8,128)S(1)}, f32[80,128]{1,0:T(8,128)S(1)}, u32[]{:S(2)}, u32[]{:S(2)}) %collective-permute-start.2) | collective-permute-done | bytes 40992 | tf_op jit(solution)/shard_map/ppermute | solution.py:346
  14.3 1.6 %collective-permute-start.7 = (f32[224,128]{1,0:T(8,128)S(1)}, f32[224,128]{1,0:T(8,128)S(1)}, u32[]{:S(2)}, u32[]{:S(2)}) collective-permute-start(f32[224,128]{1,0:T(8,128)S(1)} %late0.1.refs_0_), channel_id=1, source_target_pairs={{0,2},{1,3},{2,0},{3,1},{4,6},{5,7},{6,4},{7,5},{8,10},{9,11},{10,... | collective-permute-start | bytes 344072 | tf_op jit(solution)/shard_map/ppermute | solution.py:346
  15.9 1.3 %collective-permute-done.3.refs_1_ = f32[80,128]{1,0:T(8,128)S(1)} collective-permute-done((f32[80,128]{1,0:T(8,128)S(1)}, f32[80,128]{1,0:T(8,128)S(1)}, u32[]{:S(2)}, u32[]{:S(2)}) %collective-permute-start.3) | collective-permute-done | bytes 40992 | tf_op jit(solution)/shard_map/ppermute | solution.py:346
  17.3 1.9 %collective-permute-start.4 = (f32[112,128]{1,0:T(8,128)S(1)}, f32[112,128]{1,0:T(8,128)S(1)}, u32[]{:S(2)}, u32[]{:S(2)}) collective-permute-start(f32[112,128]{1,0:T(8,128)S(1)} %get-tuple-element.39.refs_0_), channel_id=1, source_target_pairs={{0,5},{1,4},{2,7},{3,6},{4,1},{5,0},{6,3},{7,2},{8,13},{9,12},{10,... | collective-permute-start | bytes 172040 | tf_op jit(solution)/shard_map/ppermute | solution.py:346
  19.1 1.0 %collective-permute-done.7.refs_1_ = f32[224,128]{1,0:T(8,128)S(1)} collective-permute-done((f32[224,128]{1,0:T(8,128)S(1)}, f32[224,128]{1,0:T(8,128)S(1)}, u32[]{:S(2)}, u32[]{:S(2)}) %collective-permute-start.7) | collective-permute-done | bytes 114720 | tf_op jit(solution)/shard_map/ppermute | solution.py:346
  20.2 2.5 %collective-permute-start.9 = (f32[96,128]{1,0:T(8,128)S(1)}, f32[96,128]{1,0:T(8,128)S(1)}, u32[]{:S(2)}, u32[]{:S(2)}) collective-permute-start(f32[96,128]{1,0:T(8,128)S(1)} %get-tuple-element.47.refs_0_), channel_id=1, source_target_pairs={{0,4},{1,5},{2,6},{3,7},{4,0},{5,1},{6,2},{7,3},{8,12},{9,13},{10,... | collective-permute-start | bytes 147464 | tf_op jit(solution)/shard_map/ppermute | solution.py:346
  23.0 6.0 %collective-permute-start.5 = (f32[16,128]{1,0:T(8,128)S(1)}, f32[16,128]{1,0:T(8,128)S(1)}, u32[]{:S(2)}, u32[]{:S(2)}) collective-permute-start(f32[16,128]{1,0:T(8,128)S(1)} %get-tuple-element.40.refs_0_), channel_id=1, source_target_pairs={{0,13},{1,12},{2,15},{3,14},{4,9},{5,8},{6,11},{7,10},{8,5},{9,4},... | collective-permute-start | bytes 24584 | tf_op jit(solution)/shard_map/ppermute | solution.py:346
  29.0 1.0 %collective-permute-start.11 = (f32[96,128]{1,0:T(8,128)S(1)}, f32[96,128]{1,0:T(8,128)S(1)}, u32[]{:S(2)}, u32[]{:S(2)}) collective-permute-start(f32[96,128]{1,0:T(8,128)S(1)} %late2.1.refs_7_.refs_0_), channel_id=1, source_target_pairs={{0,12},{1,13},{2,14},{3,15},{4,8},{5,9},{6,10},{7,11},{8,4},{9,5},... | collective-permute-start | bytes 147464 | tf_op jit(solution)/shard_map/ppermute | solution.py:346
  30.3 0.4 level3.1
  30.7 0.4 collective-permute-start.10
  31.1 4.2 %collective-permute-done.11.refs_1_ = f32[96,128]{1,0:T(8,128)S(1)} collective-permute-done((f32[96,128]{1,0:T(8,128)S(1)}, f32[96,128]{1,0:T(8,128)S(1)}, u32[]{:S(2)}, u32[]{:S(2)}) %collective-permute-start.11) | collective-permute-done | bytes 49184 | tf_op jit(solution)/shard_map/ppermute | solution.py:346
  35.3 1.7 %collective-permute-start.13 = (f32[160,128]{1,0:T(8,128)S(1)}, f32[160,128]{1,0:T(8,128)S(1)}, u32[]{:S(2)}, u32[]{:S(2)}) collective-permute-start(f32[160,128]{1,0:T(8,128)S(1)} %late3.1.refs_2_), channel_id=1, source_target_pairs={{0,16},{1,17},{2,18},{3,19},{4,20},{5,21},{6,22},{7,23},{8,24},{9,... | collective-permute-start | bytes 245768 | tf_op jit(solution)/shard_map/ppermute | solution.py:346
  36.9 1.7 %collective-permute-start.12 = (f32[32,128]{1,0:T(8,128)S(1)}, f32[32,128]{1,0:T(8,128)S(1)}, u32[]{:S(2)}, u32[]{:S(2)}) collective-permute-start(f32[32,128]{1,0:T(8,128)S(1)} %sum2.1.refs_0_), channel_id=1, source_target_pairs={{0,13},{1,12},{2,15},{3,14},{4,9},{5,8},{6,11},{7,10},{8,5},{9,4},... | collective-permute-start | bytes 49160 | tf_op jit(solution)/shard_map/ppermute | solution.py:346
  38.6 1.2 %collective-permute-done.13.refs_0_.refs_4_ = f32[160,128]{1,0:T(8,128)S(1)} collective-permute-done((f32[160,128]{1,0:T(8,128)S(1)}, f32[160,128]{1,0:T(8,128)S(1)}, u32[]{:S(2)}, u32[]{:S(2)}) %collective-permute-start.13) | collective-permute-done | bytes 81952 | tf_op jit(solution)/shard_map/ppermute | solution.py:346
  39.8 2.5 %collective-permute-done.12.refs_1_ = f32[32,128]{1,0:T(8,128)S(1)} collective-permute-done((f32[32,128]{1,0:T(8,128)S(1)}, f32[32,128]{1,0:T(8,128)S(1)}, u32[]{:S(2)}, u32[]{:S(2)}) %collective-permute-start.12) | collective-permute-done | bytes 16416 | tf_op jit(solution)/shard_map/ppermute | solution.py:346
  42.3 3.1 %collective-permute-done.14.refs_1_ = f32[32,128]{1,0:T(8,128)S(1)} collective-permute-done((f32[32,128]{1,0:T(8,128)S(1)}, f32[32,128]{1,0:T(8,128)S(1)}, u32[]{:S(2)}, u32[]{:S(2)}) %collective-permute-start.14) | collective-permute-done | bytes 16416 | tf_op jit(solution)/shard_map/ppermute | solution.py:346
  45.8 1.8 %collective-permute-start.17 = (f32[192,128]{1,0:T(8,128)S(1)}, f32[192,128]{1,0:T(8,128)S(1)}, u32[]{:S(2)}, u32[]{:S(2)}) collective-permute-start(f32[192,128]{1,0:T(8,128)S(1)} %get-tuple-element.50.refs_0_), channel_id=1, source_target_pairs={{0,49},{1,48},{2,51},{3,50},{4,53},{5,52},{6,55},{7,54},{8,57},{9,... | collective-permute-start | bytes 294920 | tf_op jit(solution)/shard_map/ppermute | solution.py:346
  47.6 4.1 %collective-permute-done.17.refs_1_ = f32[192,128]{1,0:T(8,128)S(1)} collective-permute-done((f32[192,128]{1,0:T(8,128)S(1)}, f32[192,128]{1,0:T(8,128)S(1)}, u32[]{:S(2)}, u32[]{:S(2)}) %collective-permute-start.17) | collective-permute-done | bytes 98336 | tf_op jit(solution)/shard_map/ppermute | solution.py:346
  51.7 0.3 level5.1
  52.0 0.8 %collective-permute-start.18 = (f32[112,128]{1,0:T(8,128)S(1)}, f32[112,128]{1,0:T(8,128)S(1)}, u32[]{:S(2)}, u32[]{:S(2)}) collective-permute-start(f32[112,128]{1,0:T(8,128)S(1)} %get-tuple-element.51.refs_0_), channel_id=1, source_target_pairs={{0,65},{1,64},{2,67},{3,66},{4,69},{5,68},{6,71},{7,70},{8,73},{9,... | collective-permute-start | bytes 172040 | tf_op jit(solution)/shard_map/ppermute | solution.py:346
  52.8 3.3 %collective-permute-done.18.refs_1_ = f32[112,128]{1,0:T(8,128)S(1)} collective-permute-done((f32[112,128]{1,0:T(8,128)S(1)}, f32[112,128]{1,0:T(8,128)S(1)}, u32[]{:S(2)}, u32[]{:S(2)}) %collective-permute-start.18) | collective-permute-done | bytes 57376 | tf_op jit(solution)/shard_map/ppermute | solution.py:346
  56.5 2.4 %collective-permute-start.19 = (f32[16,128]{1,0:T(8,128)S(1)}, f32[16,128]{1,0:T(8,128)S(1)}, u32[]{:S(2)}, u32[]{:S(2)}) collective-permute-start(f32[16,128]{1,0:T(8,128)S(1)} %get-tuple-element.52.refs_0_), channel_id=1, source_target_pairs={{0,193},{1,192},{2,195},{3,194},{4,197},{5,196},{6,199},{7,198},{8... | collective-permute-start | bytes 24584 | tf_op jit(solution)/shard_map/ppermute | solution.py:346
  58.9 1.4 %place.1 = (f32[16,2048]{1,0:T(8,128)S(1)}, bf16[64,2048]{1,0:T(8,128)(2,1)S(1)}) custom-call(f32[16,2048]{1,0:T(8,128)S(1)} %get-tuple-element.53.refs_0_, f32[16,128]{1,0:T(8,128)S(1)} %get-tuple-element.45.refs_2_.refs_1_, f32[16,128]{1,0:T(8,128)S(1)} %get-tuple-element.49.refs_1_.refs_2_, f32[16,128]{1,0:T(8,128)S(1)} %get-tuple-element.54.refs_3_, ...), custom_call_target="tpu_custom_call" | custom-call | tf_op jit(solution)/shard_map/place/pallas_call | solution.py:331
  60.2 0.6 collective-permute-done.19.refs_1_
  60.8 1.0 %last.1 = f32[16,2048]{1,0:T(8,128)} custom-call(f32[16,128]{1,0:T(8,128)S(1)} %get-tuple-element.52.refs_0_, f32[16,128]{1,0:T(8,128)S(1)} %collective-permute-done.19.refs_1_, bf16[8,64,128]{2,1,0:T(8,128)(2,1)S(1)} %copy-done.1, f32[16,2048]{1,0:T(8,128)S(1)} %get-tuple-element.57.refs_3_, bf16[64,2048]{1,0:T(8,128)(2,1)S(1)} %get-tuple-element.58.refs_4_), custom_call_target="tpu_custom_call" | custom-call | tf_op jit(solution)/shard_map/last/pallas_call | solution.py:331
  (38 shorter events, 2.6 us)
Async XLA Ops:
  0.0 0.7 %copy-start.3 = (s32[1,2048]{1,0:T(1,128)S(1)}, s32[1,2048]{1,0:T(1,128)}, u32[]{:S(2)}) copy-start(s32[1,2048]{1,0:T(1,128)} %refs_7_.1) | copy-start | bytes 24580
  0.0 0.9 %copy-start.2 = (bf16[16,2048]{1,0:T(8,128)(2,1)S(1)}, bf16[16,2048]{1,0:T(8,128)(2,1)}, u32[]{:S(2)}) copy-start(bf16[16,2048]{1,0:T(8,128)(2,1)} %refs_0_.1) | copy-start | bytes 196612
  0.9 5.2 %copy-start.1 = (bf16[8,64,128]{2,1,0:T(8,128)(2,1)S(1)}, bf16[8,64,128]{2,1,0:T(8,128)(2,1)}, u32[]{:S(2)}) copy-start(bf16[8,64,128]{2,1,0:T(8,128)(2,1)} %refs_2_.13) | copy-start | bytes 393220
  6.0 1.3 %collective-permute-start = (f32[112,128]{1,0:T(8,128)S(1)}, f32[112,128]{1,0:T(8,128)S(1)}, u32[]{:S(2)}, u32[]{:S(2)}) collective-permute-start(f32[112,128]{1,0:T(8,128)S(1)} %first.1.refs_0_), channel_id=1, source_target_pairs={{0,1},{1,0},{2,3},{3,2},{4,5},{5,4},{6,7},{7,6},{8,9},{9,8},{10,11... | collective-permute-start | bytes 172040 | tf_op jit(solution)/shard_map/ppermute | solution.py:346
  7.7 4.4 %collective-permute-start.1 = (f32[16,128]{1,0:T(8,128)S(1)}, f32[16,128]{1,0:T(8,128)S(1)}, u32[]{:S(2)}, u32[]{:S(2)}) collective-permute-start(f32[16,128]{1,0:T(8,128)S(1)} %get-tuple-element.33.after_ref.refs_0_), channel_id=1, source_target_pairs={{0,3},{1,2},{2,1},{3,0},{4,7},{5,6},{6,5},{7,4},{8,11},{9,10},{10,... | collective-permute-start | bytes 24584 | tf_op jit(solution)/shard_map/ppermute | solution.py:346
  12.6 1.2 %collective-permute-start.2 = (f32[80,128]{1,0:T(8,128)S(1)}, f32[80,128]{1,0:T(8,128)S(1)}, u32[]{:S(2)}, u32[]{:S(2)}) collective-permute-start(f32[80,128]{1,0:T(8,128)S(1)} %get-tuple-element.38.refs_0_), channel_id=1, source_target_pairs={{0,1},{1,0},{2,3},{3,2},{4,5},{5,4},{6,7},{7,6},{8,9},{9,8},{10,11... | collective-permute-start | bytes 122888 | tf_op jit(solution)/shard_map/ppermute | solution.py:346
  12.9 1.3 %collective-permute-start.6 = (f32[224,128]{1,0:T(8,128)S(1)}, f32[224,128]{1,0:T(8,128)S(1)}, u32[]{:S(2)}, u32[]{:S(2)}) collective-permute-start(f32[224,128]{1,0:T(8,128)S(1)} %get-tuple-element.44), channel_id=1, source_target_pairs={{0,1},{1,0},{2,3},{3,2},{4,5},{5,4},{6,7},{7,6},{8,9},{9,8},{10,11... | collective-permute-start | bytes 344072 | tf_op jit(solution)/shard_map/ppermute | solution.py:346
  13.8 3.4 %collective-permute-start.3 = (f32[80,128]{1,0:T(8,128)S(1)}, f32[80,128]{1,0:T(8,128)S(1)}, u32[]{:S(2)}, u32[]{:S(2)}) collective-permute-start(f32[80,128]{1,0:T(8,128)S(1)} %sum0.1.refs_0_.refs_2_), channel_id=1, source_target_pairs={{0,3},{1,2},{2,1},{3,0},{4,7},{5,6},{6,5},{7,4},{8,11},{9,10},{10,... | collective-permute-start | bytes 122888 | tf_op jit(solution)/shard_map/ppermute | solution.py:346
  14.3 5.9 %collective-permute-start.7 = (f32[224,128]{1,0:T(8,128)S(1)}, f32[224,128]{1,0:T(8,128)S(1)}, u32[]{:S(2)}, u32[]{:S(2)}) collective-permute-start(f32[224,128]{1,0:T(8,128)S(1)} %late0.1.refs_0_), channel_id=1, source_target_pairs={{0,2},{1,3},{2,0},{3,1},{4,6},{5,7},{6,4},{7,5},{8,10},{9,11},{10,... | collective-permute-start | bytes 344072 | tf_op jit(solution)/shard_map/ppermute | solution.py:346
  17.3 5.4 %collective-permute-start.4 = (f32[112,128]{1,0:T(8,128)S(1)}, f32[112,128]{1,0:T(8,128)S(1)}, u32[]{:S(2)}, u32[]{:S(2)}) collective-permute-start(f32[112,128]{1,0:T(8,128)S(1)} %get-tuple-element.39.refs_0_), channel_id=1, source_target_pairs={{0,5},{1,4},{2,7},{3,6},{4,1},{5,0},{6,3},{7,2},{8,13},{9,12},{10,... | collective-permute-start | bytes 172040 | tf_op jit(solution)/shard_map/ppermute | solution.py:346
  20.2 8.8 %collective-permute-start.9 = (f32[96,128]{1,0:T(8,128)S(1)}, f32[96,128]{1,0:T(8,128)S(1)}, u32[]{:S(2)}, u32[]{:S(2)}) collective-permute-start(f32[96,128]{1,0:T(8,128)S(1)} %get-tuple-element.47.refs_0_), channel_id=1, source_target_pairs={{0,4},{1,5},{2,6},{3,7},{4,0},{5,1},{6,2},{7,3},{8,12},{9,13},{10,... | collective-permute-start | bytes 147464 | tf_op jit(solution)/shard_map/ppermute | solution.py:346
  22.6 7.7 %collective-permute-start.8 = (f32[128,128]{1,0:T(8,128)S(1)}, f32[128,128]{1,0:T(8,128)S(1)}, u32[]{:S(2)}, u32[]{:S(2)}) collective-permute-start(f32[128,128]{1,0:T(8,128)S(1)} %get-tuple-element.46.refs_5_), channel_id=1, source_target_pairs={{0,1},{1,0},{2,3},{3,2},{4,5},{5,4},{6,7},{7,6},{8,9},{9,8},{10,11... | collective-permute-start | bytes 196616 | tf_op jit(solution)/shard_map/ppermute | solution.py:346
  23.0 7.3 %collective-permute-start.5 = (f32[16,128]{1,0:T(8,128)S(1)}, f32[16,128]{1,0:T(8,128)S(1)}, u32[]{:S(2)}, u32[]{:S(2)}) collective-permute-start(f32[16,128]{1,0:T(8,128)S(1)} %get-tuple-element.40.refs_0_), channel_id=1, source_target_pairs={{0,13},{1,12},{2,15},{3,14},{4,9},{5,8},{6,11},{7,10},{8,5},{9,4},... | collective-permute-start | bytes 24584 | tf_op jit(solution)/shard_map/ppermute | solution.py:346
  29.0 6.3 %collective-permute-start.11 = (f32[96,128]{1,0:T(8,128)S(1)}, f32[96,128]{1,0:T(8,128)S(1)}, u32[]{:S(2)}, u32[]{:S(2)}) collective-permute-start(f32[96,128]{1,0:T(8,128)S(1)} %late2.1.refs_7_.refs_0_), channel_id=1, source_target_pairs={{0,12},{1,13},{2,14},{3,15},{4,8},{5,9},{6,10},{7,11},{8,4},{9,5},... | collective-permute-start | bytes 147464 | tf_op jit(solution)/shard_map/ppermute | solution.py:346
  30.7 6.2 %collective-permute-start.10 = (f32[32,128]{1,0:T(8,128)S(1)}, f32[32,128]{1,0:T(8,128)S(1)}, u32[]{:S(2)}, u32[]{:S(2)}) collective-permute-start(f32[32,128]{1,0:T(8,128)S(1)} %get-tuple-element.48.refs_0_), channel_id=1, source_target_pairs={{0,5},{1,4},{2,7},{3,6},{4,1},{5,0},{6,3},{7,2},{8,13},{9,12},{10,... | collective-permute-start | bytes 49160 | tf_op jit(solution)/shard_map/ppermute | solution.py:346
  35.3 4.5 %collective-permute-start.13 = (f32[160,128]{1,0:T(8,128)S(1)}, f32[160,128]{1,0:T(8,128)S(1)}, u32[]{:S(2)}, u32[]{:S(2)}) collective-permute-start(f32[160,128]{1,0:T(8,128)S(1)} %late3.1.refs_2_), channel_id=1, source_target_pairs={{0,16},{1,17},{2,18},{3,19},{4,20},{5,21},{6,22},{7,23},{8,24},{9,... | collective-permute-start | bytes 245768 | tf_op jit(solution)/shard_map/ppermute | solution.py:346
  36.9 5.4 %collective-permute-start.12 = (f32[32,128]{1,0:T(8,128)S(1)}, f32[32,128]{1,0:T(8,128)S(1)}, u32[]{:S(2)}, u32[]{:S(2)}) collective-permute-start(f32[32,128]{1,0:T(8,128)S(1)} %sum2.1.refs_0_), channel_id=1, source_target_pairs={{0,13},{1,12},{2,15},{3,14},{4,9},{5,8},{6,11},{7,10},{8,5},{9,4},... | collective-permute-start | bytes 49160 | tf_op jit(solution)/shard_map/ppermute | solution.py:346
  38.6 3.7 %collective-permute-start.15 = (f32[160,128]{1,0:T(8,128)S(1)}, f32[160,128]{1,0:T(8,128)S(1)}, u32[]{:S(2)}, u32[]{:S(2)}) collective-permute-start(f32[160,128]{1,0:T(8,128)S(1)} %late3.1.refs_2_), channel_id=1, source_target_pairs={{0,1},{1,0},{2,3},{3,2},{4,5},{5,4},{6,7},{7,6},{8,9},{9,8},{10,11... | collective-permute-start | bytes 245768 | tf_op jit(solution)/shard_map/ppermute | solution.py:346
  39.8 5.7 %collective-permute-start.16 = (f32[160,128]{1,0:T(8,128)S(1)}, f32[160,128]{1,0:T(8,128)S(1)}, u32[]{:S(2)}, u32[]{:S(2)}) collective-permute-start(f32[160,128]{1,0:T(8,128)S(1)} %late4.1.refs_2_), channel_id=1, source_target_pairs={{0,1},{1,0},{2,3},{3,2},{4,5},{5,4},{6,7},{7,6},{8,9},{9,8},{10,11... | collective-permute-start | bytes 245768 | tf_op jit(solution)/shard_map/ppermute | solution.py:346
  42.3 3.2 %collective-permute-start.14 = (f32[32,128]{1,0:T(8,128)S(1)}, f32[32,128]{1,0:T(8,128)S(1)}, u32[]{:S(2)}, u32[]{:S(2)}) collective-permute-start(f32[32,128]{1,0:T(8,128)S(1)} %sum3.1.refs_0_), channel_id=1, source_target_pairs={{0,17},{1,16},{2,19},{3,18},{4,21},{5,20},{6,23},{7,22},{8,25},{9,... | collective-permute-start | bytes 49160 | tf_op jit(solution)/shard_map/ppermute | solution.py:346
  45.8 5.9 %collective-permute-start.17 = (f32[192,128]{1,0:T(8,128)S(1)}, f32[192,128]{1,0:T(8,128)S(1)}, u32[]{:S(2)}, u32[]{:S(2)}) collective-permute-start(f32[192,128]{1,0:T(8,128)S(1)} %get-tuple-element.50.refs_0_), channel_id=1, source_target_pairs={{0,49},{1,48},{2,51},{3,50},{4,53},{5,52},{6,55},{7,54},{8,57},{9,... | collective-permute-start | bytes 294920 | tf_op jit(solution)/shard_map/ppermute | solution.py:346
  52.0 6.9 %copy-start = (bf16[8,64,2048]{2,1,0:T(8,128)(2,1)S(1)}, bf16[8,64,2048]{2,1,0:T(8,128)(2,1)}, u32[]{:S(2)}) copy-start(bf16[8,64,2048]{2,1,0:T(8,128)(2,1)} %param.10) | copy-start | bytes 6291460
  52.0 4.2 %collective-permute-start.18 = (f32[112,128]{1,0:T(8,128)S(1)}, f32[112,128]{1,0:T(8,128)S(1)}, u32[]{:S(2)}, u32[]{:S(2)}) collective-permute-start(f32[112,128]{1,0:T(8,128)S(1)} %get-tuple-element.51.refs_0_), channel_id=1, source_target_pairs={{0,65},{1,64},{2,67},{3,66},{4,69},{5,68},{6,71},{7,70},{8,73},{9,... | collective-permute-start | bytes 172040 | tf_op jit(solution)/shard_map/ppermute | solution.py:346
  56.5 4.3 %collective-permute-start.19 = (f32[16,128]{1,0:T(8,128)S(1)}, f32[16,128]{1,0:T(8,128)S(1)}, u32[]{:S(2)}, u32[]{:S(2)}) collective-permute-start(f32[16,128]{1,0:T(8,128)S(1)} %get-tuple-element.52.refs_0_), channel_id=1, source_target_pairs={{0,193},{1,192},{2,195},{3,194},{4,197},{5,196},{6,199},{7,198},{8... | collective-permute-start | bytes 24584 | tf_op jit(solution)/shard_map/ppermute | solution.py:346

commit v5 on v4

--- a/solution.py
+++ b/solution.py
@@ -55,6 +55,11 @@
 def order(k, own, far):
     upper = bit(k) == 1
     return jnp.where(upper, far, own), jnp.where(upper, own, far)
+
+
+def shared_out(own, other):
+    second = (bit(0) + bit(1) + bit(2) + bit(4)) & 1 == 1
+    return jnp.where(second, other, own), jnp.where(second, own, other)
 
 
 def side_by_side(k, low, high):
@@ -154,7 +159,7 @@
     tail = jnp.concatenate([tile(2, 3), diag], axis=0)
     cut = tail.shape[0] // 2
     halves = [jnp.concatenate([tile(1, 2), tail[:cut]], axis=0), jnp.concatenate([tile(1, 3), tail[cut:]], axis=0)]
-    keep_ref[...], send_ref[...] = order(0, *halves)
+    keep_ref[...], send_ref[...] = shared_out(*halves)
 
 
 def first_kernel(pay_ref, core_ref, out_ref):
@@ -207,7 +212,7 @@
 
 def level3_kernel(own_ref, far_ref, core_ref, even_ref, keep_ref, near_ref, far_near_ref, w_ref, out_ref):
     both = odd_weights(3, own_ref, far_ref, core_ref, even_ref, w_ref)
-    for i, product in enumerate(order(0, near_ref[...], far_near_ref[...])):
+    for i, product in enumerate(shared_out(near_ref[...], far_near_ref[...])):
         rows = slice(i * RHS, (i + 1) * RHS)
         out_ref[rows] = keep_ref[rows] - times(both, product)
 
@@ -244,8 +249,8 @@
     rows = prod_ref.shape[0] - RANK
     both = both_weights(4, own[:RHS], far[:RHS], prod_ref[rows:], far_prod_ref[rows:])
     w_ref[...] = both.astype(F32)
-    mine = jnp.concatenate(order(0, prod_ref[:rows], prod_near_ref[:rows]), axis=0)
-    theirs = jnp.concatenate(order(0, far_prod_ref[:rows], far_near_ref[:rows]), axis=0)
+    mine = jnp.concatenate(shared_out(prod_ref[:rows], prod_near_ref[:rows]), axis=0)
+    theirs = jnp.concatenate(shared_out(far_prod_ref[:rows], far_near_ref[:rows]), axis=0)
     cross = jnp.concatenate([mine[:RANK], theirs[:RANK]], axis=0)
     diag = jnp.concatenate([mine[LANES:], theirs[LANES:]], axis=0)
     diag = jnp.where(lanes(LANES) < RANK, 0.0, swap(diag))
@@ -413,24 +418,24 @@
     )
     rest_far = pair(rest, 0)
     (late,) = call(add_kernel, "late0", (late, late_far), [shape(late_rows, LANES)], after=(w01,))
-    late_far = pair(late, 1)
+    late_far = pair(late, 1, 1)
     (rest,) = main(add_kernel, "sum0", (rest, rest_far), [shape(later_rows + RANK // 2, LANES)])
     rest_far = pair(rest, 1, 1)
     pay, keep = main(node_kernel, "node", (rest, rest_far, cores), [shape(PAY + RANK, LANES), two], 2, 2)
     pay_far = pair(pay, 2, 1)
     near, prod = call(take_kernel, "late1", (late, late_far), [shape(LANES, LANES), shape(tail, LANES)], after=(rest,))
     near_far = pair(near, 0)
-    prod_far = pair(prod, 2)
+    prod_far = pair(prod, 2, 1)
     w2, half = main(level2_kernel, "level2", (pay, pay_far), [one, one])
     half_far = pair(half, 3, 1)
     (prod,) = call(add_kernel, "late2", (prod, prod_far), [shape(tail, LANES)], after=(pay_far,))
-    prod_far = pair(prod, 3)
+    prod_far = pair(prod, 3, 1)
     w23, keep = main(
         level3_kernel, "level3", (half, half_far, cores, w2, keep, near, near_far), [one, two], 3, 2, (prod,)
     )
     keep_far = pair(keep, 2, 1)
     (prod,) = call(add_core_kernel, "late3", (prod, prod_far, cores), [shape(tail + RANK, LANES)], 4, 2, (half_far,))
-    prod_near, far_prod = pair(prod, 0), pair(prod, 4)
+    prod_near, far_prod = pair(prod, 0), pair(prod, 4, 1)
     (keep,) = main(add_kernel, "sum2", (keep, keep_far), [two], after=(prod,))
     keep_far = pair(keep, 3, 1)
     (far_copy,) = call(copy_kernel, "late4", (far_prod,), [shape(*far_prod.shape)], after=(w23,))

time: 62.2 us -> 61.1 us (0.982)
  waiting for transfers between devices: 23.7 us -> 19.7 us
  starting transfers between devices: 24.3 us -> 26.8 us
    ppermute x20, waiting for transfers between devices: 23.7 us -> 19.7 us  [pair(): return lax.ppermute(values, 'leaf', [(d, d ^ mask) for d in range(devices)])]
    ppermute x20, starting transfers between devices: 24.3 us -> 26.8 us  [pair(): return lax.ppermute(values, 'leaf', [(d, d ^ mask) for d in range(devices)])]
  transfers between devices with their start and end apart: 20 -> 20, of which waited for: 13 -> 12; matrix products, arithmetic and copies ran while one was open for 0% -> 0% of each run, Pallas kernels for 8% -> 8%
where the time goes in v5:
time: 61.1 us; the launch traced here: 60.3 us
  starting transfers between devices  26.8 us (44%)
  waiting for transfers between devices  19.7 us (32%)
  Pallas kernels  12.9 us (21%)
  local copies, waits for them, and re-layouts  0.86 us (1%)
    ppermute x20, starting transfers between devices, pair(): return lax.ppermute(values, 'leaf', [(d, d ^ mask) for d in range(devices)])  26.8 us
    ppermute x20, waiting for transfers between devices, pair(): return lax.ppermute(values, 'leaf', [(d, d ^ mask) for d in range(devices)])  19.7 us
    pallas_call x1, Pallas kernels, local(): pl.pallas_call(leaf_body, in_specs=[anywhere, vmem, vmem, anywhere, anywh...  5.16 us
    pallas_call x20, Pallas kernels, call(): pl.pallas_call(body, in_specs=specs, out_specs=[vmem] * len(shapes), out_...  4.94 us
    pallas_call x1, Pallas kernels, local(): pl.pallas_call(products_body, in_specs=[anywhere] * 3, out_specs=[vmem] *...  2.78 us
  transfers between devices with their start and end apart: 20, of which 12 were waited for; matrix products, arithmetic and copies ran while one was open for 0% of the time, Pallas kernels for 8%

profile of v5, /device:TPU:32, one launch (start us, length us, event | category | flops | bytes accessed | tf_op | source)
XLA Modules:
  0.0 60.3 jit_solution(1858238106338137130)
XLA Ops:
  0.0 0.7 %copy-done.3 = s32[1,2048]{1,0:T(1,128)S(1)} copy-done((s32[1,2048]{1,0:T(1,128)S(1)}, s32[1,2048]{1,0:T(1,128)}, u32[]{:S(2)}) %copy-start.3) | copy-done | bytes 8216
  0.9 5.2 %leaf.1 = (f32[16,2048]{1,0:T(8,128)S(1)}, f32[48,128]{1,0:T(8,128)S(1)}, f32[48,128]{1,0:T(8,128)S(1)}, f32[384,128]{1,0:T(8,128)S(1)}) custom-call(f32[8,128]{1,0:T(8,128)S(1)} %ready.1.after_ref, bf16[16,2048]{1,0:T(8,128)(2,1)S(1)} %copy-done.2, s32[1,2048]{1,0:T(1,128)S(1)} %copy-done.3, bf16[2048,2048]{1,0:T(8,128)(2,1)} %refs_2_.7, ...), custom_call_target="tpu_custom_call" | custom-call | tf_op jit(solution)/shard_map/leaf/pallas_call | solution.py:363
  6.2 1.2 %collective-permute-done.refs_1_ = f32[112,128]{1,0:T(8,128)S(1)} collective-permute-done((f32[112,128]{1,0:T(8,128)S(1)}, f32[112,128]{1,0:T(8,128)S(1)}, u32[]{:S(2)}, u32[]{:S(2)}) %collective-permute-start) | collective-permute-done | bytes 57376 | tf_op jit(solution)/shard_map/ppermute | solution.py:351
  7.7 1.6 %collective-permute-start.1 = (f32[16,128]{1,0:T(8,128)S(1)}, f32[16,128]{1,0:T(8,128)S(1)}, u32[]{:S(2)}, u32[]{:S(2)}) collective-permute-start(f32[16,128]{1,0:T(8,128)S(1)} %get-tuple-element.33.after_ref.refs_0_), channel_id=1, source_target_pairs={{0,3},{1,2},{2,1},{3,0},{4,7},{5,6},{6,5},{7,4},{8,11},{9,10},{10,... | collective-permute-start | bytes 24584 | tf_op jit(solution)/shard_map/ppermute | solution.py:351
  9.3 2.8 %products.1 = (f32[32,128]{1,0:T(8,128)S(1)}, f32[224,128]{1,0:T(8,128)S(1)}, f32[224,128]{1,0:T(8,128)S(1)}) custom-call(f32[16,128]{1,0:T(8,128)S(1)} %get-tuple-element.33.after_ref.refs_0_, bf16[512,2048]{1,0:T(8,128)(2,1)} %bitcast.6, bf16[512,2048]{1,0:T(8,128)(2,1)} %bitcast.3), custom_call_target="tpu_custom_call" | custom-call | flops 603979776 | bytes 3145728 | tf_op jit(solution)/shard_map/products/pallas_call | solution.py:395
  12.1 0.4 level1.1
  12.6 0.4 collective-permute-start.2
  13.1 0.7 %collective-permute-done.2.refs_1_ = f32[80,128]{1,0:T(8,128)S(1)} collective-permute-done((f32[80,128]{1,0:T(8,128)S(1)}, f32[80,128]{1,0:T(8,128)S(1)}, u32[]{:S(2)}, u32[]{:S(2)}) %collective-permute-start.2) | collective-permute-done | bytes 40992 | tf_op jit(solution)/shard_map/ppermute | solution.py:351
  14.3 1.4 %collective-permute-start.7 = (f32[224,128]{1,0:T(8,128)S(1)}, f32[224,128]{1,0:T(8,128)S(1)}, u32[]{:S(2)}, u32[]{:S(2)}) collective-permute-start(f32[224,128]{1,0:T(8,128)S(1)} %late0.1.refs_0_), channel_id=1, source_target_pairs={{0,3},{1,2},{2,1},{3,0},{4,7},{5,6},{6,5},{7,4},{8,11},{9,10},{10,... | collective-permute-start | bytes 344072 | tf_op jit(solution)/shard_map/ppermute | solution.py:351
  15.7 1.6 %collective-permute-done.3.refs_1_ = f32[80,128]{1,0:T(8,128)S(1)} collective-permute-done((f32[80,128]{1,0:T(8,128)S(1)}, f32[80,128]{1,0:T(8,128)S(1)}, u32[]{:S(2)}, u32[]{:S(2)}) %collective-permute-start.3) | collective-permute-done | bytes 40992 | tf_op jit(solution)/shard_map/ppermute | solution.py:351
  17.3 1.9 %collective-permute-start.4 = (f32[112,128]{1,0:T(8,128)S(1)}, f32[112,128]{1,0:T(8,128)S(1)}, u32[]{:S(2)}, u32[]{:S(2)}) collective-permute-start(f32[112,128]{1,0:T(8,128)S(1)} %get-tuple-element.39.refs_0_), channel_id=1, source_target_pairs={{0,5},{1,4},{2,7},{3,6},{4,1},{5,0},{6,3},{7,2},{8,13},{9,12},{10,... | collective-permute-start | bytes 172040 | tf_op jit(solution)/shard_map/ppermute | solution.py:351
  19.1 0.7 %collective-permute-done.7.refs_1_ = f32[224,128]{1,0:T(8,128)S(1)} collective-permute-done((f32[224,128]{1,0:T(8,128)S(1)}, f32[224,128]{1,0:T(8,128)S(1)}, u32[]{:S(2)}, u32[]{:S(2)}) %collective-permute-start.7) | collective-permute-done | bytes 114720 | tf_op jit(solution)/shard_map/ppermute | solution.py:351
  19.8 2.5 %collective-permute-start.9 = (f32[96,128]{1,0:T(8,128)S(1)}, f32[96,128]{1,0:T(8,128)S(1)}, u32[]{:S(2)}, u32[]{:S(2)}) collective-permute-start(f32[96,128]{1,0:T(8,128)S(1)} %get-tuple-element.47.refs_0_), channel_id=1, source_target_pairs={{0,5},{1,4},{2,7},{3,6},{4,1},{5,0},{6,3},{7,2},{8,13},{9,12},{10,... | collective-permute-start | bytes 147464 | tf_op jit(solution)/shard_map/ppermute | solution.py:351
  22.3 0.3 collective-permute-start.8
  23.0 5.0 %collective-permute-start.5 = (f32[16,128]{1,0:T(8,128)S(1)}, f32[16,128]{1,0:T(8,128)S(1)}, u32[]{:S(2)}, u32[]{:S(2)}) collective-permute-start(f32[16,128]{1,0:T(8,128)S(1)} %get-tuple-element.40.refs_0_), channel_id=1, source_target_pairs={{0,13},{1,12},{2,15},{3,14},{4,9},{5,8},{6,11},{7,10},{8,5},{9,4},... | collective-permute-start | bytes 24584 | tf_op jit(solution)/shard_map/ppermute | solution.py:351
  28.0 2.2 %collective-permute-start.11 = (f32[96,128]{1,0:T(8,128)S(1)}, f32[96,128]{1,0:T(8,128)S(1)}, u32[]{:S(2)}, u32[]{:S(2)}) collective-permute-start(f32[96,128]{1,0:T(8,128)S(1)} %late2.1.refs_7_.refs_0_), channel_id=1, source_target_pairs={{0,13},{1,12},{2,15},{3,14},{4,9},{5,8},{6,11},{7,10},{8,5},{9,4},... | collective-permute-start | bytes 147464 | tf_op jit(solution)/shard_map/ppermute | solution.py:351
  30.2 0.4 level3.1
  30.6 0.4 collective-permute-start.10
  31.1 3.6 %collective-permute-done.11.refs_1_ = f32[96,128]{1,0:T(8,128)S(1)} collective-permute-done((f32[96,128]{1,0:T(8,128)S(1)}, f32[96,128]{1,0:T(8,128)S(1)}, u32[]{:S(2)}, u32[]{:S(2)}) %collective-permute-start.11) | collective-permute-done | bytes 49184 | tf_op jit(solution)/shard_map/ppermute | solution.py:351
  34.7 1.3 %collective-permute-start.13 = (f32[160,128]{1,0:T(8,128)S(1)}, f32[160,128]{1,0:T(8,128)S(1)}, u32[]{:S(2)}, u32[]{:S(2)}) collective-permute-start(f32[160,128]{1,0:T(8,128)S(1)} %late3.1.refs_2_), channel_id=1, source_target_pairs={{0,17},{1,16},{2,19},{3,18},{4,21},{5,20},{6,23},{7,22},{8,25},{9,... | collective-permute-start | bytes 245768 | tf_op jit(solution)/shard_map/ppermute | solution.py:351
  36.0 1.8 %collective-permute-start.12 = (f32[32,128]{1,0:T(8,128)S(1)}, f32[32,128]{1,0:T(8,128)S(1)}, u32[]{:S(2)}, u32[]{:S(2)}) collective-permute-start(f32[32,128]{1,0:T(8,128)S(1)} %sum2.1.refs_0_), channel_id=1, source_target_pairs={{0,13},{1,12},{2,15},{3,14},{4,9},{5,8},{6,11},{7,10},{8,5},{9,4},... | collective-permute-start | bytes 49160 | tf_op jit(solution)/shard_map/ppermute | solution.py:351
  37.9 1.4 %collective-permute-done.13.refs_0_.refs_4_ = f32[160,128]{1,0:T(8,128)S(1)} collective-permute-done((f32[160,128]{1,0:T(8,128)S(1)}, f32[160,128]{1,0:T(8,128)S(1)}, u32[]{:S(2)}, u32[]{:S(2)}) %collective-permute-start.13) | collective-permute-done | bytes 81952 | tf_op jit(solution)/shard_map/ppermute | solution.py:351
  39.4 2.0 %collective-permute-done.12.refs_1_ = f32[32,128]{1,0:T(8,128)S(1)} collective-permute-done((f32[32,128]{1,0:T(8,128)S(1)}, f32[32,128]{1,0:T(8,128)S(1)}, u32[]{:S(2)}, u32[]{:S(2)}) %collective-permute-start.12) | collective-permute-done | bytes 16416 | tf_op jit(solution)/shard_map/ppermute | solution.py:351
  41.4 0.6 collective-permute-start.14
  42.0 2.6 %collective-permute-done.14.refs_1_ = f32[32,128]{1,0:T(8,128)S(1)} collective-permute-done((f32[32,128]{1,0:T(8,128)S(1)}, f32[32,128]{1,0:T(8,128)S(1)}, u32[]{:S(2)}, u32[]{:S(2)}) %collective-permute-start.14) | collective-permute-done | bytes 16416 | tf_op jit(solution)/shard_map/ppermute | solution.py:351
  44.9 2.3 %collective-permute-start.17 = (f32[192,128]{1,0:T(8,128)S(1)}, f32[192,128]{1,0:T(8,128)S(1)}, u32[]{:S(2)}, u32[]{:S(2)}) collective-permute-start(f32[192,128]{1,0:T(8,128)S(1)} %get-tuple-element.50.refs_0_), channel_id=1, source_target_pairs={{0,49},{1,48},{2,51},{3,50},{4,53},{5,52},{6,55},{7,54},{8,57},{9,... | collective-permute-start | bytes 294920 | tf_op jit(solution)/shard_map/ppermute | solution.py:351
  47.1 3.5 %collective-permute-done.17.refs_1_ = f32[192,128]{1,0:T(8,128)S(1)} collective-permute-done((f32[192,128]{1,0:T(8,128)S(1)}, f32[192,128]{1,0:T(8,128)S(1)}, u32[]{:S(2)}, u32[]{:S(2)}) %collective-permute-start.17) | collective-permute-done | bytes 98336 | tf_op jit(solution)/shard_map/ppermute | solution.py:351
  51.0 1.5 %collective-permute-start.18 = (f32[112,128]{1,0:T(8,128)S(1)}, f32[112,128]{1,0:T(8,128)S(1)}, u32[]{:S(2)}, u32[]{:S(2)}) collective-permute-start(f32[112,128]{1,0:T(8,128)S(1)} %get-tuple-element.51.refs_0_), channel_id=1, source_target_pairs={{0,65},{1,64},{2,67},{3,66},{4,69},{5,68},{6,71},{7,70},{8,73},{9,... | collective-permute-start | bytes 172040 | tf_op jit(solution)/shard_map/ppermute | solution.py:351
  52.5 2.1 %collective-permute-done.18.refs_1_ = f32[112,128]{1,0:T(8,128)S(1)} collective-permute-done((f32[112,128]{1,0:T(8,128)S(1)}, f32[112,128]{1,0:T(8,128)S(1)}, u32[]{:S(2)}, u32[]{:S(2)}) %collective-permute-start.18) | collective-permute-done | bytes 57376 | tf_op jit(solution)/shard_map/ppermute | solution.py:351
  55.0 2.8 %collective-permute-start.19 = (f32[16,128]{1,0:T(8,128)S(1)}, f32[16,128]{1,0:T(8,128)S(1)}, u32[]{:S(2)}, u32[]{:S(2)}) collective-permute-start(f32[16,128]{1,0:T(8,128)S(1)} %get-tuple-element.52.refs_0_), channel_id=1, source_target_pairs={{0,193},{1,192},{2,195},{3,194},{4,197},{5,196},{6,199},{7,198},{8... | collective-permute-start | bytes 24584 | tf_op jit(solution)/shard_map/ppermute | solution.py:351
  57.7 1.4 %place.1 = (f32[16,2048]{1,0:T(8,128)S(1)}, bf16[64,2048]{1,0:T(8,128)(2,1)S(1)}) custom-call(f32[16,2048]{1,0:T(8,128)S(1)} %get-tuple-element.53.refs_0_, f32[16,128]{1,0:T(8,128)S(1)} %get-tuple-element.45.refs_2_.refs_1_, f32[16,128]{1,0:T(8,128)S(1)} %get-tuple-element.49.refs_1_.refs_2_, f32[16,128]{1,0:T(8,128)S(1)} %get-tuple-element.54.refs_3_, ...), custom_call_target="tpu_custom_call" | custom-call | tf_op jit(solution)/shard_map/place/pallas_call | solution.py:336
  59.3 1.0 %last.1 = f32[16,2048]{1,0:T(8,128)} custom-call(f32[16,128]{1,0:T(8,128)S(1)} %get-tuple-element.52.refs_0_, f32[16,128]{1,0:T(8,128)S(1)} %collective-permute-done.19.refs_1_, bf16[8,64,128]{2,1,0:T(8,128)(2,1)S(1)} %copy-done.1, f32[16,2048]{1,0:T(8,128)S(1)} %get-tuple-element.57.refs_3_, bf16[64,2048]{1,0:T(8,128)(2,1)S(1)} %get-tuple-element.58.refs_4_), custom_call_target="tpu_custom_call" | custom-call | tf_op jit(solution)/shard_map/last/pallas_call | solution.py:336
  (38 shorter events, 3.1 us)
Async XLA Ops:
  0.0 0.7 %copy-start.3 = (s32[1,2048]{1,0:T(1,128)S(1)}, s32[1,2048]{1,0:T(1,128)}, u32[]{:S(2)}) copy-start(s32[1,2048]{1,0:T(1,128)} %refs_7_.1) | copy-start | bytes 24580
  0.0 0.9 %copy-start.2 = (bf16[16,2048]{1,0:T(8,128)(2,1)S(1)}, bf16[16,2048]{1,0:T(8,128)(2,1)}, u32[]{:S(2)}) copy-start(bf16[16,2048]{1,0:T(8,128)(2,1)} %refs_0_.1) | copy-start | bytes 196612
  0.9 5.2 %copy-start.1 = (bf16[8,64,128]{2,1,0:T(8,128)(2,1)S(1)}, bf16[8,64,128]{2,1,0:T(8,128)(2,1)}, u32[]{:S(2)}) copy-start(bf16[8,64,128]{2,1,0:T(8,128)(2,1)} %refs_2_.13) | copy-start | bytes 393220
  6.0 1.3 %collective-permute-start = (f32[112,128]{1,0:T(8,128)S(1)}, f32[112,128]{1,0:T(8,128)S(1)}, u32[]{:S(2)}, u32[]{:S(2)}) collective-permute-start(f32[112,128]{1,0:T(8,128)S(1)} %first.1.refs_0_), channel_id=1, source_target_pairs={{0,1},{1,0},{2,3},{3,2},{4,5},{5,4},{6,7},{7,6},{8,9},{9,8},{10,11... | collective-permute-start | bytes 172040 | tf_op jit(solution)/shard_map/ppermute | solution.py:351
  7.7 4.4 %collective-permute-start.1 = (f32[16,128]{1,0:T(8,128)S(1)}, f32[16,128]{1,0:T(8,128)S(1)}, u32[]{:S(2)}, u32[]{:S(2)}) collective-permute-start(f32[16,128]{1,0:T(8,128)S(1)} %get-tuple-element.33.after_ref.refs_0_), channel_id=1, source_target_pairs={{0,3},{1,2},{2,1},{3,0},{4,7},{5,6},{6,5},{7,4},{8,11},{9,10},{10,... | collective-permute-start | bytes 24584 | tf_op jit(solution)/shard_map/ppermute | solution.py:351
  12.6 1.2 %collective-permute-start.2 = (f32[80,128]{1,0:T(8,128)S(1)}, f32[80,128]{1,0:T(8,128)S(1)}, u32[]{:S(2)}, u32[]{:S(2)}) collective-permute-start(f32[80,128]{1,0:T(8,128)S(1)} %get-tuple-element.38.refs_0_), channel_id=1, source_target_pairs={{0,1},{1,0},{2,3},{3,2},{4,5},{5,4},{6,7},{7,6},{8,9},{9,8},{10,11... | collective-permute-start | bytes 122888 | tf_op jit(solution)/shard_map/ppermute | solution.py:351
  12.9 1.3 %collective-permute-start.6 = (f32[224,128]{1,0:T(8,128)S(1)}, f32[224,128]{1,0:T(8,128)S(1)}, u32[]{:S(2)}, u32[]{:S(2)}) collective-permute-start(f32[224,128]{1,0:T(8,128)S(1)} %get-tuple-element.44), channel_id=1, source_target_pairs={{0,1},{1,0},{2,3},{3,2},{4,5},{5,4},{6,7},{7,6},{8,9},{9,8},{10,11... | collective-permute-start | bytes 344072 | tf_op jit(solution)/shard_map/ppermute | solution.py:351
  13.8 3.4 %collective-permute-start.3 = (f32[80,128]{1,0:T(8,128)S(1)}, f32[80,128]{1,0:T(8,128)S(1)}, u32[]{:S(2)}, u32[]{:S(2)}) collective-permute-start(f32[80,128]{1,0:T(8,128)S(1)} %sum0.1.refs_0_.refs_2_), channel_id=1, source_target_pairs={{0,3},{1,2},{2,1},{3,0},{4,7},{5,6},{6,5},{7,4},{8,11},{9,10},{10,... | collective-permute-start | bytes 122888 | tf_op jit(solution)/shard_map/ppermute | solution.py:351
  14.3 5.5 %collective-permute-start.7 = (f32[224,128]{1,0:T(8,128)S(1)}, f32[224,128]{1,0:T(8,128)S(1)}, u32[]{:S(2)}, u32[]{:S(2)}) collective-permute-start(f32[224,128]{1,0:T(8,128)S(1)} %late0.1.refs_0_), channel_id=1, source_target_pairs={{0,3},{1,2},{2,1},{3,0},{4,7},{5,6},{6,5},{7,4},{8,11},{9,10},{10,... | collective-permute-start | bytes 344072 | tf_op jit(solution)/shard_map/ppermute | solution.py:351
  17.3 5.4 %collective-permute-start.4 = (f32[112,128]{1,0:T(8,128)S(1)}, f32[112,128]{1,0:T(8,128)S(1)}, u32[]{:S(2)}, u32[]{:S(2)}) collective-permute-start(f32[112,128]{1,0:T(8,128)S(1)} %get-tuple-element.39.refs_0_), channel_id=1, source_target_pairs={{0,5},{1,4},{2,7},{3,6},{4,1},{5,0},{6,3},{7,2},{8,13},{9,12},{10,... | collective-permute-start | bytes 172040 | tf_op jit(solution)/shard_map/ppermute | solution.py:351
  19.8 8.2 %collective-permute-start.9 = (f32[96,128]{1,0:T(8,128)S(1)}, f32[96,128]{1,0:T(8,128)S(1)}, u32[]{:S(2)}, u32[]{:S(2)}) collective-permute-start(f32[96,128]{1,0:T(8,128)S(1)} %get-tuple-element.47.refs_0_), channel_id=1, source_target_pairs={{0,5},{1,4},{2,7},{3,6},{4,1},{5,0},{6,3},{7,2},{8,13},{9,12},{10,... | collective-permute-start | bytes 147464 | tf_op jit(solution)/shard_map/ppermute | solution.py:351
  22.3 7.9 %collective-permute-start.8 = (f32[128,128]{1,0:T(8,128)S(1)}, f32[128,128]{1,0:T(8,128)S(1)}, u32[]{:S(2)}, u32[]{:S(2)}) collective-permute-start(f32[128,128]{1,0:T(8,128)S(1)} %get-tuple-element.46.refs_5_), channel_id=1, source_target_pairs={{0,1},{1,0},{2,3},{3,2},{4,5},{5,4},{6,7},{7,6},{8,9},{9,8},{10,11... | collective-permute-start | bytes 196616 | tf_op jit(solution)/shard_map/ppermute | solution.py:351
  23.0 7.2 %collective-permute-start.5 = (f32[16,128]{1,0:T(8,128)S(1)}, f32[16,128]{1,0:T(8,128)S(1)}, u32[]{:S(2)}, u32[]{:S(2)}) collective-permute-start(f32[16,128]{1,0:T(8,128)S(1)} %get-tuple-element.40.refs_0_), channel_id=1, source_target_pairs={{0,13},{1,12},{2,15},{3,14},{4,9},{5,8},{6,11},{7,10},{8,5},{9,4},... | collective-permute-start | bytes 24584 | tf_op jit(solution)/shard_map/ppermute | solution.py:351
  28.0 6.6 %collective-permute-start.11 = (f32[96,128]{1,0:T(8,128)S(1)}, f32[96,128]{1,0:T(8,128)S(1)}, u32[]{:S(2)}, u32[]{:S(2)}) collective-permute-start(f32[96,128]{1,0:T(8,128)S(1)} %late2.1.refs_7_.refs_0_), channel_id=1, source_target_pairs={{0,13},{1,12},{2,15},{3,14},{4,9},{5,8},{6,11},{7,10},{8,5},{9,4},... | collective-permute-start | bytes 147464 | tf_op jit(solution)/shard_map/ppermute | solution.py:351
  30.6 5.4 %collective-permute-start.10 = (f32[32,128]{1,0:T(8,128)S(1)}, f32[32,128]{1,0:T(8,128)S(1)}, u32[]{:S(2)}, u32[]{:S(2)}) collective-permute-start(f32[32,128]{1,0:T(8,128)S(1)} %get-tuple-element.48.refs_0_), channel_id=1, source_target_pairs={{0,5},{1,4},{2,7},{3,6},{4,1},{5,0},{6,3},{7,2},{8,13},{9,12},{10,... | collective-permute-start | bytes 49160 | tf_op jit(solution)/shard_map/ppermute | solution.py:351
  34.7 4.6 %collective-permute-start.13 = (f32[160,128]{1,0:T(8,128)S(1)}, f32[160,128]{1,0:T(8,128)S(1)}, u32[]{:S(2)}, u32[]{:S(2)}) collective-permute-start(f32[160,128]{1,0:T(8,128)S(1)} %late3.1.refs_2_), channel_id=1, source_target_pairs={{0,17},{1,16},{2,19},{3,18},{4,21},{5,20},{6,23},{7,22},{8,25},{9,... | collective-permute-start | bytes 245768 | tf_op jit(solution)/shard_map/ppermute | solution.py:351
  36.0 5.4 %collective-permute-start.12 = (f32[32,128]{1,0:T(8,128)S(1)}, f32[32,128]{1,0:T(8,128)S(1)}, u32[]{:S(2)}, u32[]{:S(2)}) collective-permute-start(f32[32,128]{1,0:T(8,128)S(1)} %sum2.1.refs_0_), channel_id=1, source_target_pairs={{0,13},{1,12},{2,15},{3,14},{4,9},{5,8},{6,11},{7,10},{8,5},{9,4},... | collective-permute-start | bytes 49160 | tf_op jit(solution)/shard_map/ppermute | solution.py:351
  37.8 4.2 %collective-permute-start.15 = (f32[160,128]{1,0:T(8,128)S(1)}, f32[160,128]{1,0:T(8,128)S(1)}, u32[]{:S(2)}, u32[]{:S(2)}) collective-permute-start(f32[160,128]{1,0:T(8,128)S(1)} %late3.1.refs_2_), channel_id=1, source_target_pairs={{0,1},{1,0},{2,3},{3,2},{4,5},{5,4},{6,7},{7,6},{8,9},{9,8},{10,11... | collective-permute-start | bytes 245768 | tf_op jit(solution)/shard_map/ppermute | solution.py:351
  39.3 5.2 %collective-permute-start.16 = (f32[160,128]{1,0:T(8,128)S(1)}, f32[160,128]{1,0:T(8,128)S(1)}, u32[]{:S(2)}, u32[]{:S(2)}) collective-permute-start(f32[160,128]{1,0:T(8,128)S(1)} %late4.1.refs_2_), channel_id=1, source_target_pairs={{0,1},{1,0},{2,3},{3,2},{4,5},{5,4},{6,7},{7,6},{8,9},{9,8},{10,11... | collective-permute-start | bytes 245768 | tf_op jit(solution)/shard_map/ppermute | solution.py:351
  41.4 3.2 %collective-permute-start.14 = (f32[32,128]{1,0:T(8,128)S(1)}, f32[32,128]{1,0:T(8,128)S(1)}, u32[]{:S(2)}, u32[]{:S(2)}) collective-permute-start(f32[32,128]{1,0:T(8,128)S(1)} %sum3.1.refs_0_), channel_id=1, source_target_pairs={{0,17},{1,16},{2,19},{3,18},{4,21},{5,20},{6,23},{7,22},{8,25},{9,... | collective-permute-start | bytes 49160 | tf_op jit(solution)/shard_map/ppermute | solution.py:351
  44.9 5.8 %collective-permute-start.17 = (f32[192,128]{1,0:T(8,128)S(1)}, f32[192,128]{1,0:T(8,128)S(1)}, u32[]{:S(2)}, u32[]{:S(2)}) collective-permute-start(f32[192,128]{1,0:T(8,128)S(1)} %get-tuple-element.50.refs_0_), channel_id=1, source_target_pairs={{0,49},{1,48},{2,51},{3,50},{4,53},{5,52},{6,55},{7,54},{8,57},{9,... | collective-permute-start | bytes 294920 | tf_op jit(solution)/shard_map/ppermute | solution.py:351
  51.0 6.8 %copy-start = (bf16[8,64,2048]{2,1,0:T(8,128)(2,1)S(1)}, bf16[8,64,2048]{2,1,0:T(8,128)(2,1)}, u32[]{:S(2)}) copy-start(bf16[8,64,2048]{2,1,0:T(8,128)(2,1)} %param.10) | copy-start | bytes 6291460
  51.0 3.7 %collective-permute-start.18 = (f32[112,128]{1,0:T(8,128)S(1)}, f32[112,128]{1,0:T(8,128)S(1)}, u32[]{:S(2)}, u32[]{:S(2)}) collective-permute-start(f32[112,128]{1,0:T(8,128)S(1)} %get-tuple-element.51.refs_0_), channel_id=1, source_target_pairs={{0,65},{1,64},{2,67},{3,66},{4,69},{5,68},{6,71},{7,70},{8,73},{9,... | collective-permute-start | bytes 172040 | tf_op jit(solution)/shard_map/ppermute | solution.py:351
  55.0 4.3 %collective-permute-start.19 = (f32[16,128]{1,0:T(8,128)S(1)}, f32[16,128]{1,0:T(8,128)S(1)}, u32[]{:S(2)}, u32[]{:S(2)}) collective-permute-start(f32[16,128]{1,0:T(8,128)S(1)} %get-tuple-element.52.refs_0_), channel_id=1, source_target_pairs={{0,193},{1,192},{2,195},{3,194},{4,197},{5,196},{6,199},{7,198},{8... | collective-permute-start | bytes 24584 | tf_op jit(solution)/shard_map/ppermute | solution.py:351

commit v6 on v5

--- a/solution.py
+++ b/solution.py
@@ -30,14 +30,17 @@
 
 
 def times(weights, product):
-    high, low = split(product, 2)
-    return jnp.dot(weights, high, preferred_element_type=F32) + jnp.dot(weights, low, preferred_element_type=F32)
+    return jnp.dot(
+        jnp.concatenate([weights, weights], axis=1),
+        jnp.concatenate(split(product, 2), axis=0),
+        preferred_element_type=F32,
+    )
 
 
 def core_times(stacked, cores):
     rows = stacked.shape[0]
-    out = lax.dot_general(jnp.concatenate(split(stacked, 3), axis=0), cores, NT, preferred_element_type=F32)
-    return (out[:rows] + (out[rows : 2 * rows] + out[2 * rows :])).astype(BF16)
+    out = lax.dot_general(jnp.concatenate(split(stacked, 2), axis=0), cores, NT, preferred_element_type=F32)
+    return (out[:rows] + out[rows:]).astype(BF16)
 
 
 def lanes(rows=RHS):

time: 61.1 us -> 61 us (level)
  no operation moved by 1% of the time
where the time goes in v6:
time: 61 us; the launch traced here: 60.2 us
  starting transfers between devices  26.7 us (44%)
  waiting for transfers between devices  19.8 us (32%)
  Pallas kernels  12.8 us (21%)
  local copies, waits for them, and re-layouts  0.86 us (1%)
    ppermute x20, starting transfers between devices, pair(): return lax.ppermute(values, 'leaf', [(d, d ^ mask) for d in range(devices)])  26.7 us
    ppermute x20, waiting for transfers between devices, pair(): return lax.ppermute(values, 'leaf', [(d, d ^ mask) for d in range(devices)])  19.8 us
    pallas_call x1, Pallas kernels, local(): pl.pallas_call(leaf_body, in_specs=[anywhere, vmem, vmem, anywhere, anywh...  5.16 us
    pallas_call x20, Pallas kernels, call(): pl.pallas_call(body, in_specs=specs, out_specs=[vmem] * len(shapes), out_...  4.81 us
    pallas_call x1, Pallas kernels, local(): pl.pallas_call(products_body, in_specs=[anywhere] * 3, out_specs=[vmem] *...  2.79 us
  transfers between devices with their start and end apart: 20, of which 12 were waited for; matrix products, arithmetic and copies ran while one was open for 0% of the time, Pallas kernels for 8%

profile of v6, /device:TPU:32, one launch (start us, length us, event | category | flops | bytes accessed | tf_op | source)
XLA Modules:
  0.0 60.2 jit_solution(7331367155033556224)
XLA Ops:
  0.0 0.7 %copy-done.3 = s32[1,2048]{1,0:T(1,128)S(1)} copy-done((s32[1,2048]{1,0:T(1,128)S(1)}, s32[1,2048]{1,0:T(1,128)}, u32[]{:S(2)}) %copy-start.3) | copy-done | bytes 8216
  0.9 5.2 %leaf.1 = (f32[16,2048]{1,0:T(8,128)S(1)}, f32[48,128]{1,0:T(8,128)S(1)}, f32[48,128]{1,0:T(8,128)S(1)}, f32[384,128]{1,0:T(8,128)S(1)}) custom-call(f32[8,128]{1,0:T(8,128)S(1)} %ready.1.after_ref, bf16[16,2048]{1,0:T(8,128)(2,1)S(1)} %copy-done.2, s32[1,2048]{1,0:T(1,128)S(1)} %copy-done.3, bf16[2048,2048]{1,0:T(8,128)(2,1)} %refs_2_.7, ...), custom_call_target="tpu_custom_call" | custom-call | tf_op jit(solution)/shard_map/leaf/pallas_call | solution.py:366
  6.2 1.2 %collective-permute-done.refs_1_ = f32[112,128]{1,0:T(8,128)S(1)} collective-permute-done((f32[112,128]{1,0:T(8,128)S(1)}, f32[112,128]{1,0:T(8,128)S(1)}, u32[]{:S(2)}, u32[]{:S(2)}) %collective-permute-start) | collective-permute-done | bytes 57376 | tf_op jit(solution)/shard_map/ppermute | solution.py:354
  7.7 1.6 %collective-permute-start.1 = (f32[16,128]{1,0:T(8,128)S(1)}, f32[16,128]{1,0:T(8,128)S(1)}, u32[]{:S(2)}, u32[]{:S(2)}) collective-permute-start(f32[16,128]{1,0:T(8,128)S(1)} %get-tuple-element.33.after_ref.refs_0_), channel_id=1, source_target_pairs={{0,3},{1,2},{2,1},{3,0},{4,7},{5,6},{6,5},{7,4},{8,11},{9,10},{10,... | collective-permute-start | bytes 24584 | tf_op jit(solution)/shard_map/ppermute | solution.py:354
  9.3 2.8 %products.1 = (f32[32,128]{1,0:T(8,128)S(1)}, f32[224,128]{1,0:T(8,128)S(1)}, f32[224,128]{1,0:T(8,128)S(1)}) custom-call(f32[16,128]{1,0:T(8,128)S(1)} %get-tuple-element.33.after_ref.refs_0_, bf16[512,2048]{1,0:T(8,128)(2,1)} %bitcast.6, bf16[512,2048]{1,0:T(8,128)(2,1)} %bitcast.3), custom_call_target="tpu_custom_call" | custom-call | flops 603979776 | bytes 3145728 | tf_op jit(solution)/shard_map/products/pallas_call | solution.py:398
  12.1 0.4 level1.1
  12.5 0.4 collective-permute-start.2
  13.0 0.7 %collective-permute-done.2.refs_1_ = f32[80,128]{1,0:T(8,128)S(1)} collective-permute-done((f32[80,128]{1,0:T(8,128)S(1)}, f32[80,128]{1,0:T(8,128)S(1)}, u32[]{:S(2)}, u32[]{:S(2)}) %collective-permute-start.2) | collective-permute-done | bytes 40992 | tf_op jit(solution)/shard_map/ppermute | solution.py:354
  14.2 1.4 %collective-permute-start.7 = (f32[224,128]{1,0:T(8,128)S(1)}, f32[224,128]{1,0:T(8,128)S(1)}, u32[]{:S(2)}, u32[]{:S(2)}) collective-permute-start(f32[224,128]{1,0:T(8,128)S(1)} %late0.1.refs_0_), channel_id=1, source_target_pairs={{0,3},{1,2},{2,1},{3,0},{4,7},{5,6},{6,5},{7,4},{8,11},{9,10},{10,... | collective-permute-start | bytes 344072 | tf_op jit(solution)/shard_map/ppermute | solution.py:354
  15.6 1.6 %collective-permute-done.3.refs_1_ = f32[80,128]{1,0:T(8,128)S(1)} collective-permute-done((f32[80,128]{1,0:T(8,128)S(1)}, f32[80,128]{1,0:T(8,128)S(1)}, u32[]{:S(2)}, u32[]{:S(2)}) %collective-permute-start.3) | collective-permute-done | bytes 40992 | tf_op jit(solution)/shard_map/ppermute | solution.py:354
  17.2 1.9 %collective-permute-start.4 = (f32[112,128]{1,0:T(8,128)S(1)}, f32[112,128]{1,0:T(8,128)S(1)}, u32[]{:S(2)}, u32[]{:S(2)}) collective-permute-start(f32[112,128]{1,0:T(8,128)S(1)} %get-tuple-element.39.refs_0_), channel_id=1, source_target_pairs={{0,5},{1,4},{2,7},{3,6},{4,1},{5,0},{6,3},{7,2},{8,13},{9,12},{10,... | collective-permute-start | bytes 172040 | tf_op jit(solution)/shard_map/ppermute | solution.py:354
  19.1 0.7 %collective-permute-done.7.refs_1_ = f32[224,128]{1,0:T(8,128)S(1)} collective-permute-done((f32[224,128]{1,0:T(8,128)S(1)}, f32[224,128]{1,0:T(8,128)S(1)}, u32[]{:S(2)}, u32[]{:S(2)}) %collective-permute-start.7) | collective-permute-done | bytes 114720 | tf_op jit(solution)/shard_map/ppermute | solution.py:354
  19.8 2.5 %collective-permute-start.9 = (f32[96,128]{1,0:T(8,128)S(1)}, f32[96,128]{1,0:T(8,128)S(1)}, u32[]{:S(2)}, u32[]{:S(2)}) collective-permute-start(f32[96,128]{1,0:T(8,128)S(1)} %get-tuple-element.47.refs_0_), channel_id=1, source_target_pairs={{0,5},{1,4},{2,7},{3,6},{4,1},{5,0},{6,3},{7,2},{8,13},{9,12},{10,... | collective-permute-start | bytes 147464 | tf_op jit(solution)/shard_map/ppermute | solution.py:354
  22.3 0.3 collective-permute-start.8
  22.9 5.0 %collective-permute-start.5 = (f32[16,128]{1,0:T(8,128)S(1)}, f32[16,128]{1,0:T(8,128)S(1)}, u32[]{:S(2)}, u32[]{:S(2)}) collective-permute-start(f32[16,128]{1,0:T(8,128)S(1)} %get-tuple-element.40.refs_0_), channel_id=1, source_target_pairs={{0,13},{1,12},{2,15},{3,14},{4,9},{5,8},{6,11},{7,10},{8,5},{9,4},... | collective-permute-start | bytes 24584 | tf_op jit(solution)/shard_map/ppermute | solution.py:354
  27.9 2.2 %collective-permute-start.11 = (f32[96,128]{1,0:T(8,128)S(1)}, f32[96,128]{1,0:T(8,128)S(1)}, u32[]{:S(2)}, u32[]{:S(2)}) collective-permute-start(f32[96,128]{1,0:T(8,128)S(1)} %late2.1.refs_7_.refs_0_), channel_id=1, source_target_pairs={{0,13},{1,12},{2,15},{3,14},{4,9},{5,8},{6,11},{7,10},{8,5},{9,4},... | collective-permute-start | bytes 147464 | tf_op jit(solution)/shard_map/ppermute | solution.py:354
  30.2 0.4 level3.1
  30.6 0.4 collective-permute-start.10
  31.0 3.6 %collective-permute-done.11.refs_1_ = f32[96,128]{1,0:T(8,128)S(1)} collective-permute-done((f32[96,128]{1,0:T(8,128)S(1)}, f32[96,128]{1,0:T(8,128)S(1)}, u32[]{:S(2)}, u32[]{:S(2)}) %collective-permute-start.11) | collective-permute-done | bytes 49184 | tf_op jit(solution)/shard_map/ppermute | solution.py:354
  34.6 1.3 %collective-permute-start.13 = (f32[160,128]{1,0:T(8,128)S(1)}, f32[160,128]{1,0:T(8,128)S(1)}, u32[]{:S(2)}, u32[]{:S(2)}) collective-permute-start(f32[160,128]{1,0:T(8,128)S(1)} %late3.1.refs_2_), channel_id=1, source_target_pairs={{0,17},{1,16},{2,19},{3,18},{4,21},{5,20},{6,23},{7,22},{8,25},{9,... | collective-permute-start | bytes 245768 | tf_op jit(solution)/shard_map/ppermute | solution.py:354
  35.9 1.8 %collective-permute-start.12 = (f32[32,128]{1,0:T(8,128)S(1)}, f32[32,128]{1,0:T(8,128)S(1)}, u32[]{:S(2)}, u32[]{:S(2)}) collective-permute-start(f32[32,128]{1,0:T(8,128)S(1)} %sum2.1.refs_0_), channel_id=1, source_target_pairs={{0,13},{1,12},{2,15},{3,14},{4,9},{5,8},{6,11},{7,10},{8,5},{9,4},... | collective-permute-start | bytes 49160 | tf_op jit(solution)/shard_map/ppermute | solution.py:354
  37.8 1.4 %collective-permute-done.13.refs_0_.refs_4_ = f32[160,128]{1,0:T(8,128)S(1)} collective-permute-done((f32[160,128]{1,0:T(8,128)S(1)}, f32[160,128]{1,0:T(8,128)S(1)}, u32[]{:S(2)}, u32[]{:S(2)}) %collective-permute-start.13) | collective-permute-done | bytes 81952 | tf_op jit(solution)/shard_map/ppermute | solution.py:354
  39.3 2.0 %collective-permute-done.12.refs_1_ = f32[32,128]{1,0:T(8,128)S(1)} collective-permute-done((f32[32,128]{1,0:T(8,128)S(1)}, f32[32,128]{1,0:T(8,128)S(1)}, u32[]{:S(2)}, u32[]{:S(2)}) %collective-permute-start.12) | collective-permute-done | bytes 16416 | tf_op jit(solution)/shard_map/ppermute | solution.py:354
  41.3 0.6 collective-permute-start.14
  41.9 2.6 %collective-permute-done.14.refs_1_ = f32[32,128]{1,0:T(8,128)S(1)} collective-permute-done((f32[32,128]{1,0:T(8,128)S(1)}, f32[32,128]{1,0:T(8,128)S(1)}, u32[]{:S(2)}, u32[]{:S(2)}) %collective-permute-start.14) | collective-permute-done | bytes 16416 | tf_op jit(solution)/shard_map/ppermute | solution.py:354
  44.8 2.2 %collective-permute-start.17 = (f32[192,128]{1,0:T(8,128)S(1)}, f32[192,128]{1,0:T(8,128)S(1)}, u32[]{:S(2)}, u32[]{:S(2)}) collective-permute-start(f32[192,128]{1,0:T(8,128)S(1)} %get-tuple-element.50.refs_0_), channel_id=1, source_target_pairs={{0,49},{1,48},{2,51},{3,50},{4,53},{5,52},{6,55},{7,54},{8,57},{9,... | collective-permute-start | bytes 294920 | tf_op jit(solution)/shard_map/ppermute | solution.py:354
  47.0 3.5 %collective-permute-done.17.refs_1_ = f32[192,128]{1,0:T(8,128)S(1)} collective-permute-done((f32[192,128]{1,0:T(8,128)S(1)}, f32[192,128]{1,0:T(8,128)S(1)}, u32[]{:S(2)}, u32[]{:S(2)}) %collective-permute-start.17) | collective-permute-done | bytes 98336 | tf_op jit(solution)/shard_map/ppermute | solution.py:354
  50.9 1.5 %collective-permute-start.18 = (f32[112,128]{1,0:T(8,128)S(1)}, f32[112,128]{1,0:T(8,128)S(1)}, u32[]{:S(2)}, u32[]{:S(2)}) collective-permute-start(f32[112,128]{1,0:T(8,128)S(1)} %get-tuple-element.51.refs_0_), channel_id=1, source_target_pairs={{0,65},{1,64},{2,67},{3,66},{4,69},{5,68},{6,71},{7,70},{8,73},{9,... | collective-permute-start | bytes 172040 | tf_op jit(solution)/shard_map/ppermute | solution.py:354
  52.4 2.1 %collective-permute-done.18.refs_1_ = f32[112,128]{1,0:T(8,128)S(1)} collective-permute-done((f32[112,128]{1,0:T(8,128)S(1)}, f32[112,128]{1,0:T(8,128)S(1)}, u32[]{:S(2)}, u32[]{:S(2)}) %collective-permute-start.18) | collective-permute-done | bytes 57376 | tf_op jit(solution)/shard_map/ppermute | solution.py:354
  54.8 2.7 %collective-permute-start.19 = (f32[16,128]{1,0:T(8,128)S(1)}, f32[16,128]{1,0:T(8,128)S(1)}, u32[]{:S(2)}, u32[]{:S(2)}) collective-permute-start(f32[16,128]{1,0:T(8,128)S(1)} %get-tuple-element.52.refs_0_), channel_id=1, source_target_pairs={{0,193},{1,192},{2,195},{3,194},{4,197},{5,196},{6,199},{7,198},{8... | collective-permute-start | bytes 24584 | tf_op jit(solution)/shard_map/ppermute | solution.py:354
  57.6 1.4 %place.1 = (f32[16,2048]{1,0:T(8,128)S(1)}, bf16[64,2048]{1,0:T(8,128)(2,1)S(1)}) custom-call(f32[16,2048]{1,0:T(8,128)S(1)} %get-tuple-element.53.refs_0_, f32[16,128]{1,0:T(8,128)S(1)} %get-tuple-element.45.refs_2_.refs_1_, f32[16,128]{1,0:T(8,128)S(1)} %get-tuple-element.49.refs_1_.refs_2_, f32[16,128]{1,0:T(8,128)S(1)} %get-tuple-element.54.refs_3_, ...), custom_call_target="tpu_custom_call" | custom-call | tf_op jit(solution)/shard_map/place/pallas_call | solution.py:339
  59.1 1.0 %last.1 = f32[16,2048]{1,0:T(8,128)} custom-call(f32[16,128]{1,0:T(8,128)S(1)} %get-tuple-element.52.refs_0_, f32[16,128]{1,0:T(8,128)S(1)} %collective-permute-done.19.refs_1_, bf16[8,64,128]{2,1,0:T(8,128)(2,1)S(1)} %copy-done.1, f32[16,2048]{1,0:T(8,128)S(1)} %get-tuple-element.57.refs_3_, bf16[64,2048]{1,0:T(8,128)(2,1)S(1)} %get-tuple-element.58.refs_4_), custom_call_target="tpu_custom_call" | custom-call | tf_op jit(solution)/shard_map/last/pallas_call | solution.py:339
  (38 shorter events, 2.9 us)
Async XLA Ops:
  0.0 0.7 %copy-start.3 = (s32[1,2048]{1,0:T(1,128)S(1)}, s32[1,2048]{1,0:T(1,128)}, u32[]{:S(2)}) copy-start(s32[1,2048]{1,0:T(1,128)} %refs_7_.1) | copy-start | bytes 24580
  0.0 0.9 %copy-start.2 = (bf16[16,2048]{1,0:T(8,128)(2,1)S(1)}, bf16[16,2048]{1,0:T(8,128)(2,1)}, u32[]{:S(2)}) copy-start(bf16[16,2048]{1,0:T(8,128)(2,1)} %refs_0_.1) | copy-start | bytes 196612
  0.9 5.2 %copy-start.1 = (bf16[8,64,128]{2,1,0:T(8,128)(2,1)S(1)}, bf16[8,64,128]{2,1,0:T(8,128)(2,1)}, u32[]{:S(2)}) copy-start(bf16[8,64,128]{2,1,0:T(8,128)(2,1)} %refs_2_.13) | copy-start | bytes 393220
  6.0 1.3 %collective-permute-start = (f32[112,128]{1,0:T(8,128)S(1)}, f32[112,128]{1,0:T(8,128)S(1)}, u32[]{:S(2)}, u32[]{:S(2)}) collective-permute-start(f32[112,128]{1,0:T(8,128)S(1)} %first.1.refs_0_), channel_id=1, source_target_pairs={{0,1},{1,0},{2,3},{3,2},{4,5},{5,4},{6,7},{7,6},{8,9},{9,8},{10,11... | collective-permute-start | bytes 172040 | tf_op jit(solution)/shard_map/ppermute | solution.py:354
  7.7 4.4 %collective-permute-start.1 = (f32[16,128]{1,0:T(8,128)S(1)}, f32[16,128]{1,0:T(8,128)S(1)}, u32[]{:S(2)}, u32[]{:S(2)}) collective-permute-start(f32[16,128]{1,0:T(8,128)S(1)} %get-tuple-element.33.after_ref.refs_0_), channel_id=1, source_target_pairs={{0,3},{1,2},{2,1},{3,0},{4,7},{5,6},{6,5},{7,4},{8,11},{9,10},{10,... | collective-permute-start | bytes 24584 | tf_op jit(solution)/shard_map/ppermute | solution.py:354
  12.5 1.2 %collective-permute-start.2 = (f32[80,128]{1,0:T(8,128)S(1)}, f32[80,128]{1,0:T(8,128)S(1)}, u32[]{:S(2)}, u32[]{:S(2)}) collective-permute-start(f32[80,128]{1,0:T(8,128)S(1)} %get-tuple-element.38.refs_0_), channel_id=1, source_target_pairs={{0,1},{1,0},{2,3},{3,2},{4,5},{5,4},{6,7},{7,6},{8,9},{9,8},{10,11... | collective-permute-start | bytes 122888 | tf_op jit(solution)/shard_map/ppermute | solution.py:354
  12.9 1.3 %collective-permute-start.6 = (f32[224,128]{1,0:T(8,128)S(1)}, f32[224,128]{1,0:T(8,128)S(1)}, u32[]{:S(2)}, u32[]{:S(2)}) collective-permute-start(f32[224,128]{1,0:T(8,128)S(1)} %get-tuple-element.44), channel_id=1, source_target_pairs={{0,1},{1,0},{2,3},{3,2},{4,5},{5,4},{6,7},{7,6},{8,9},{9,8},{10,11... | collective-permute-start | bytes 344072 | tf_op jit(solution)/shard_map/ppermute | solution.py:354
  13.8 3.4 %collective-permute-start.3 = (f32[80,128]{1,0:T(8,128)S(1)}, f32[80,128]{1,0:T(8,128)S(1)}, u32[]{:S(2)}, u32[]{:S(2)}) collective-permute-start(f32[80,128]{1,0:T(8,128)S(1)} %sum0.1.refs_0_.refs_2_), channel_id=1, source_target_pairs={{0,3},{1,2},{2,1},{3,0},{4,7},{5,6},{6,5},{7,4},{8,11},{9,10},{10,... | collective-permute-start | bytes 122888 | tf_op jit(solution)/shard_map/ppermute | solution.py:354
  14.2 5.5 %collective-permute-start.7 = (f32[224,128]{1,0:T(8,128)S(1)}, f32[224,128]{1,0:T(8,128)S(1)}, u32[]{:S(2)}, u32[]{:S(2)}) collective-permute-start(f32[224,128]{1,0:T(8,128)S(1)} %late0.1.refs_0_), channel_id=1, source_target_pairs={{0,3},{1,2},{2,1},{3,0},{4,7},{5,6},{6,5},{7,4},{8,11},{9,10},{10,... | collective-permute-start | bytes 344072 | tf_op jit(solution)/shard_map/ppermute | solution.py:354
  17.2 5.4 %collective-permute-start.4 = (f32[112,128]{1,0:T(8,128)S(1)}, f32[112,128]{1,0:T(8,128)S(1)}, u32[]{:S(2)}, u32[]{:S(2)}) collective-permute-start(f32[112,128]{1,0:T(8,128)S(1)} %get-tuple-element.39.refs_0_), channel_id=1, source_target_pairs={{0,5},{1,4},{2,7},{3,6},{4,1},{5,0},{6,3},{7,2},{8,13},{9,12},{10,... | collective-permute-start | bytes 172040 | tf_op jit(solution)/shard_map/ppermute | solution.py:354
  19.8 8.2 %collective-permute-start.9 = (f32[96,128]{1,0:T(8,128)S(1)}, f32[96,128]{1,0:T(8,128)S(1)}, u32[]{:S(2)}, u32[]{:S(2)}) collective-permute-start(f32[96,128]{1,0:T(8,128)S(1)} %get-tuple-element.47.refs_0_), channel_id=1, source_target_pairs={{0,5},{1,4},{2,7},{3,6},{4,1},{5,0},{6,3},{7,2},{8,13},{9,12},{10,... | collective-permute-start | bytes 147464 | tf_op jit(solution)/shard_map/ppermute | solution.py:354
  22.3 7.9 %collective-permute-start.8 = (f32[128,128]{1,0:T(8,128)S(1)}, f32[128,128]{1,0:T(8,128)S(1)}, u32[]{:S(2)}, u32[]{:S(2)}) collective-permute-start(f32[128,128]{1,0:T(8,128)S(1)} %get-tuple-element.46.refs_5_), channel_id=1, source_target_pairs={{0,1},{1,0},{2,3},{3,2},{4,5},{5,4},{6,7},{7,6},{8,9},{9,8},{10,11... | collective-permute-start | bytes 196616 | tf_op jit(solution)/shard_map/ppermute | solution.py:354
  22.9 7.3 %collective-permute-start.5 = (f32[16,128]{1,0:T(8,128)S(1)}, f32[16,128]{1,0:T(8,128)S(1)}, u32[]{:S(2)}, u32[]{:S(2)}) collective-permute-start(f32[16,128]{1,0:T(8,128)S(1)} %get-tuple-element.40.refs_0_), channel_id=1, source_target_pairs={{0,13},{1,12},{2,15},{3,14},{4,9},{5,8},{6,11},{7,10},{8,5},{9,4},... | collective-permute-start | bytes 24584 | tf_op jit(solution)/shard_map/ppermute | solution.py:354
  27.9 6.6 %collective-permute-start.11 = (f32[96,128]{1,0:T(8,128)S(1)}, f32[96,128]{1,0:T(8,128)S(1)}, u32[]{:S(2)}, u32[]{:S(2)}) collective-permute-start(f32[96,128]{1,0:T(8,128)S(1)} %late2.1.refs_7_.refs_0_), channel_id=1, source_target_pairs={{0,13},{1,12},{2,15},{3,14},{4,9},{5,8},{6,11},{7,10},{8,5},{9,4},... | collective-permute-start | bytes 147464 | tf_op jit(solution)/shard_map/ppermute | solution.py:354
  30.6 5.4 %collective-permute-start.10 = (f32[32,128]{1,0:T(8,128)S(1)}, f32[32,128]{1,0:T(8,128)S(1)}, u32[]{:S(2)}, u32[]{:S(2)}) collective-permute-start(f32[32,128]{1,0:T(8,128)S(1)} %get-tuple-element.48.refs_0_), channel_id=1, source_target_pairs={{0,5},{1,4},{2,7},{3,6},{4,1},{5,0},{6,3},{7,2},{8,13},{9,12},{10,... | collective-permute-start | bytes 49160 | tf_op jit(solution)/shard_map/ppermute | solution.py:354
  34.6 4.6 %collective-permute-start.13 = (f32[160,128]{1,0:T(8,128)S(1)}, f32[160,128]{1,0:T(8,128)S(1)}, u32[]{:S(2)}, u32[]{:S(2)}) collective-permute-start(f32[160,128]{1,0:T(8,128)S(1)} %late3.1.refs_2_), channel_id=1, source_target_pairs={{0,17},{1,16},{2,19},{3,18},{4,21},{5,20},{6,23},{7,22},{8,25},{9,... | collective-permute-start | bytes 245768 | tf_op jit(solution)/shard_map/ppermute | solution.py:354
  35.9 5.4 %collective-permute-start.12 = (f32[32,128]{1,0:T(8,128)S(1)}, f32[32,128]{1,0:T(8,128)S(1)}, u32[]{:S(2)}, u32[]{:S(2)}) collective-permute-start(f32[32,128]{1,0:T(8,128)S(1)} %sum2.1.refs_0_), channel_id=1, source_target_pairs={{0,13},{1,12},{2,15},{3,14},{4,9},{5,8},{6,11},{7,10},{8,5},{9,4},... | collective-permute-start | bytes 49160 | tf_op jit(solution)/shard_map/ppermute | solution.py:354
  37.8 4.1 %collective-permute-start.15 = (f32[160,128]{1,0:T(8,128)S(1)}, f32[160,128]{1,0:T(8,128)S(1)}, u32[]{:S(2)}, u32[]{:S(2)}) collective-permute-start(f32[160,128]{1,0:T(8,128)S(1)} %late3.1.refs_2_), channel_id=1, source_target_pairs={{0,1},{1,0},{2,3},{3,2},{4,5},{5,4},{6,7},{7,6},{8,9},{9,8},{10,11... | collective-permute-start | bytes 245768 | tf_op jit(solution)/shard_map/ppermute | solution.py:354
  39.2 5.3 %collective-permute-start.16 = (f32[160,128]{1,0:T(8,128)S(1)}, f32[160,128]{1,0:T(8,128)S(1)}, u32[]{:S(2)}, u32[]{:S(2)}) collective-permute-start(f32[160,128]{1,0:T(8,128)S(1)} %late4.1.refs_2_), channel_id=1, source_target_pairs={{0,1},{1,0},{2,3},{3,2},{4,5},{5,4},{6,7},{7,6},{8,9},{9,8},{10,11... | collective-permute-start | bytes 245768 | tf_op jit(solution)/shard_map/ppermute | solution.py:354
  41.3 3.2 %collective-permute-start.14 = (f32[32,128]{1,0:T(8,128)S(1)}, f32[32,128]{1,0:T(8,128)S(1)}, u32[]{:S(2)}, u32[]{:S(2)}) collective-permute-start(f32[32,128]{1,0:T(8,128)S(1)} %sum3.1.refs_0_), channel_id=1, source_target_pairs={{0,17},{1,16},{2,19},{3,18},{4,21},{5,20},{6,23},{7,22},{8,25},{9,... | collective-permute-start | bytes 49160 | tf_op jit(solution)/shard_map/ppermute | solution.py:354
  44.8 5.7 %collective-permute-start.17 = (f32[192,128]{1,0:T(8,128)S(1)}, f32[192,128]{1,0:T(8,128)S(1)}, u32[]{:S(2)}, u32[]{:S(2)}) collective-permute-start(f32[192,128]{1,0:T(8,128)S(1)} %get-tuple-element.50.refs_0_), channel_id=1, source_target_pairs={{0,49},{1,48},{2,51},{3,50},{4,53},{5,52},{6,55},{7,54},{8,57},{9,... | collective-permute-start | bytes 294920 | tf_op jit(solution)/shard_map/ppermute | solution.py:354
  50.9 6.7 %copy-start = (bf16[8,64,2048]{2,1,0:T(8,128)(2,1)S(1)}, bf16[8,64,2048]{2,1,0:T(8,128)(2,1)}, u32[]{:S(2)}) copy-start(bf16[8,64,2048]{2,1,0:T(8,128)(2,1)} %param.10) | copy-start | bytes 6291460
  50.9 3.7 %collective-permute-start.18 = (f32[112,128]{1,0:T(8,128)S(1)}, f32[112,128]{1,0:T(8,128)S(1)}, u32[]{:S(2)}, u32[]{:S(2)}) collective-permute-start(f32[112,128]{1,0:T(8,128)S(1)} %get-tuple-element.51.refs_0_), channel_id=1, source_target_pairs={{0,65},{1,64},{2,67},{3,66},{4,69},{5,68},{6,71},{7,70},{8,73},{9,... | collective-permute-start | bytes 172040 | tf_op jit(solution)/shard_map/ppermute | solution.py:354
  54.8 4.3 %collective-permute-start.19 = (f32[16,128]{1,0:T(8,128)S(1)}, f32[16,128]{1,0:T(8,128)S(1)}, u32[]{:S(2)}, u32[]{:S(2)}) collective-permute-start(f32[16,128]{1,0:T(8,128)S(1)} %get-tuple-element.52.refs_0_), channel_id=1, source_target_pairs={{0,193},{1,192},{2,195},{3,194},{4,197},{5,196},{6,199},{7,198},{8... | collective-permute-start | bytes 24584 | tf_op jit(solution)/shard_map/ppermute | solution.py:354
